TPU v7x, 128 devices: a whole 4x4x4 slice. The times are simulated.
128 devices in a mesh: slab: 32 (over x, y, core), sub: 4 (over z).
Axes of the slice: x: 4, y: 4, z: 4, core: 2. Of those that a mesh axis runs over, the one named last changes fastest.
Arguments:
- load_values: float32 [3, 128, 32, 256], P(None, 'slab', 'sub'), may hold values from -6 to 6
- load_mask: int32 [128, 32, 256], P('slab', 'sub'), may hold values 0 or 1
- fixed_mask: int32 [128, 32, 256], P('slab', 'sub'), may hold values 0 or 1
- frequencies: float32 [3, 128], replicated, may hold values from -24 to 24
- weight_in: bfloat16 [256, 512], replicated, may hold values from -0.375 to 0.375
- weight_mid: bfloat16 [512, 512], replicated, may hold values from -0.25 to 0.25
- weight_out: bfloat16 [512], replicated, may hold values from -0.25 to 0.25
Outputs:
- displacement: float32 [3, 128, 32, 256], P(None, 'slab', 'sub')
- density: float32 [128, 32, 256], P('slab', 'sub')
- grad_weight_in: float32 [256, 512], replicated
- grad_weight_mid: float32 [512, 512], replicated
- grad_weight_out: float32 [512], replicated
All inputs are finite; a program needn't handle non-finite values. No bound on the sum of `load_mask` or of `fixed_mask` on one device may be relied on, other than what follows from the above.
Results may differ from a plain program's by a relative error of at most 0.00055.
Values sent between devices are 32-bit elements; how exact they have to be, the bound alone decides.
No kernel may reach another device: no remote copies, remote signals or barrier semaphores. Data moves between devices by JAX's collectives and lax.ppermute only.
A program may use at most 256 MiB of HBM per device.

v0:
```python
import functools
import itertools
import math

import jax
import jax.numpy as jnp
import numpy as np
from jax import lax
from jax.experimental import pallas as pl
from jax.experimental.pallas import tpu as pltpu
from jax.sharding import Mesh
from jax.sharding import PartitionSpec as P

ITERS = 3
SLAB = ("x", "y", "c")
CHIPS = ("x", "y", "z")
ALL = ("x", "y", "c", "z")
BF = jnp.bfloat16
F32 = jnp.float32

two_pi = 2.0 * math.pi
emin = 0.001
penalty = 4.0
vol_target = 0.3
ROWS = 16
corner_list = list(itertools.product((0, 1), repeat=3))
LAST = (((1,), (1,)), ((), ()))


def hex_stiffness():
    poisson = 0.3
    lame_first = poisson / ((1.0 + poisson) * (1.0 - 2.0 * poisson))
    lame_second = 0.5 / (1.0 + poisson)
    elastic = np.zeros((6, 6))
    elastic[:3, :3] = lame_first
    for axis_number in range(3):
        elastic[axis_number, axis_number] += 2.0 * lame_second
        elastic[axis_number + 3, axis_number + 3] = lame_second
    gauss_points = [0.5 - 0.5 / math.sqrt(3.0), 0.5 + 0.5 / math.sqrt(3.0)]
    matrix = np.zeros((24, 24))
    for location in itertools.product(gauss_points, repeat=3):
        strain = np.zeros((6, 24))
        for corner_number, corner in enumerate(corner_list):
            factors = [
                location[axis] if corner[axis] == 1 else 1.0 - location[axis] for axis in range(3)
            ]
            slopes = [1.0 if corner[axis] == 1 else -1.0 for axis in range(3)]
            derivative = [
                slopes[0] * factors[1] * factors[2],
                factors[0] * slopes[1] * factors[2],
                factors[0] * factors[1] * slopes[2],
            ]
            column = 3 * corner_number
            for axis in range(3):
                strain[axis, column + axis] = derivative[axis]
            strain[3, column + 1] = derivative[2]
            strain[3, column + 2] = derivative[1]
            strain[4, column + 0] = derivative[2]
            strain[4, column + 2] = derivative[0]
            strain[5, column + 0] = derivative[1]
            strain[5, column + 1] = derivative[0]
        matrix += strain.T @ elastic @ strain / 8.0
    return matrix


def modal_stiffness():
    table = hex_stiffness()
    change = np.zeros((24, 24))
    for row, wave in enumerate(corner_list):
        for column, corner in enumerate(corner_list):
            sign = np.prod([1.0 if c == 1 else -1.0 for w, c in zip(wave, corner) if w == 1])
            for d in range(3):
                change[3 * row + d, 3 * column + d] = sign
    modal = change @ table @ change.T / 64.0
    blocks = []
    for parity in corner_list:
        waves = [tuple(parity[a] ^ (a == d) for a in range(3)) for d in range(3)]
        index = [3 * corner_list.index(wave) + d for d, wave in enumerate(waves)]
        block = modal[np.ix_(index, index)]
        blocks.append((waves, np.where(np.abs(block) < 1e-9, 0.0, block)))
    return blocks


BLOCKS = modal_stiffness()


def lane_mask(shape, lane):
    return lax.broadcasted_iota(jnp.int32, shape, len(shape) - 1) == lane


def plane_modes(plane, rows):
    size = plane.shape[-1]
    ahead = jnp.where(lane_mask(plane.shape, size - 1), 0.0, pltpu.roll(plane, size - 1, 1))
    modes = {}
    for wave_z, part in ((0, plane + ahead), (1, ahead - plane)):
        following = pltpu.roll(part, ROWS - 1, 0)
        modes[0, wave_z] = (part + following)[:rows]
        modes[1, wave_z] = (following - part)[:rows]
    return modes


def element_modes(lower, upper):
    found = []
    for low, high in zip(lower, upper):
        modes = {}
        for key in low:
            modes[(0,) + key] = low[key] + high[key]
            modes[(1,) + key] = high[key] - low[key]
        found.append(modes)
    return found


def modal_forces(modes):
    for waves, block in BLOCKS:
        values = [modes[d][waves[d]] for d in range(3)]
        for d in range(3):
            total = None
            for other in range(3):
                if block[d, other] != 0.0:
                    term = np.float32(block[d, other]) * values[other]
                    total = term if total is None else total + term
            if total is not None:
                yield d, waves[d], values[d], total


def energy_of(modes):
    total = None
    for _, _, value, force in modal_forces(modes):
        total = value * force if total is None else total + value * force
    return total


def node_plane(gathered):
    parts = []
    for wave_z in (0, 1):
        even, odd = gathered[0, wave_z], gathered[1, wave_z]
        parts.append((even - odd) + pltpu.roll(even + odd, 1, 0))
    behind = pltpu.roll(parts[0] + parts[1], 1, 1)
    return (parts[0] - parts[1]) + jnp.where(lane_mask(behind.shape, 0), 0.0, behind)


def operator_planes(planes, stiff, free):
    modes = [[plane_modes(component, ROWS) for component in plane] for plane in planes]
    gathered = [[{} for _ in range(3)] for _ in planes]
    for e in range(len(planes) - 1):
        forces = [{} for _ in range(3)]
        for d, wave, _, force in modal_forces(element_modes(modes[e], modes[e + 1])):
            forces[d][wave] = force * stiff[e]
        for d in range(3):
            for key in itertools.product((0, 1), repeat=2):
                even, odd = forces[d].get((0,) + key), forces[d].get((1,) + key)
                for node, sign in ((e, -1), (e + 1, 1)):
                    if even is None:
                        term = odd if sign == 1 else -odd
                    else:
                        term = even + odd if sign == 1 else even - odd
                    held = gathered[node][d]
                    held[key] = term if key not in held else held[key] + term
    return [
        [node_plane(gathered[n][d]) * free[n - 1] for d in range(3)]
        for n in range(1, len(planes) - 1)
    ]


def kept_if(flag):
    return jnp.where(flag == 0, 1.0, 0.0)


def with_rows(place, block, ahead, behind):
    start, stop = kept_if(place[Z_FIRST]), kept_if(place[Z_LAST])
    space = ROWS - block.shape[0] - ahead.shape[0] - behind.shape[0]
    zeros = jnp.zeros((space, block.shape[1]), F32)
    return jnp.concatenate([block, ahead * stop, zeros, behind * start], axis=0)


def load_plane(place, loads, ahead, behind, d, p):
    slot = d * loads.shape[1] + p
    return with_rows(place, loads[d, p], ahead[slot], behind[slot])


def krylov_kernel(place, loads, ahead, behind, stiff, stiff_ahead, stiff_behind, density,
                  first, second, sums):
    planes = loads.shape[1]
    cells = planes - 5
    low, high = kept_if(place[SLAB_FIRST]), kept_if(place[SLAB_LAST])
    stiff_planes = [stiff_behind[p] * low for p in range(2)]
    stiff_planes += [stiff[p] for p in range(cells)]
    stiff_planes += [stiff_ahead[p] * high for p in range(2)]
    loaded = [
        [load_plane(place, loads, ahead, behind, d, p) for d in range(4)] for p in range(planes)
    ]
    force = [plane[:3] for plane in loaded]
    free = [plane[3] for plane in loaded]
    image = operator_planes(force, stiff_planes, free[1:-1])
    twice = operator_planes(image, stiff_planes[1:-1], free[2:-2])
    own = (force[2 : 2 + cells], image[1 : 1 + cells], twice[:cells])
    rows = density.shape[1]

    def dot(left, right):
        total = None
        for p in range(cells):
            for d in range(3):
                term = left[p][d][:rows] * right[p][d][:rows]
                total = term if total is None else total + term
        return total

    totals = [dot(own[k // 2], own[(k + 1) // 2]) for k in range(2 * ITERS - 1)]
    modes = [[plane_modes(component, rows) for component in plane] for plane in twice]
    last = None
    volume = None
    for e in range(cells):
        term = stiff_planes[2 + e][:rows] * energy_of(element_modes(modes[e], modes[e + 1]))
        last = term if last is None else last + term
        volume = density[e] if volume is None else volume + density[e]
    totals += [last, volume]
    row_number = lax.broadcasted_iota(jnp.int32, sums.shape, 0)
    result = jnp.zeros(sums.shape, F32)
    for k, total in enumerate(totals):
        scalar = jnp.sum(jnp.sum(total, axis=0, keepdims=True), axis=1, keepdims=True)
        result = jnp.where(row_number == k, scalar, result)
    sums[...] = result
    for p in range(cells + 1):
        for d in range(3):
            first[d, p] = image[1 + p][d]
            second[d, p] = twice[p][d]


def krylov_steps(moments):
    mean = moments[1] / moments[0]
    powers = [None, mean]
    for k in range(2, 2 * ITERS):
        powers.append(powers[-1] * mean)
    scaled = [moments[k] / moments[0] / powers[k] if k else 1.0 for k in range(2 * ITERS)]

    def product(left, right, shift):
        return sum(
            left[i] * right[j] * scaled[i + j + shift]
            for i in range(len(left))
            for j in range(len(right))
        )

    solution = [0.0] * ITERS
    residual = [1.0]
    direction = [1.0]
    norm_now = scaled[0]
    work = 0.0
    for iteration in range(ITERS):
        alpha = norm_now / product(direction, direction, 1)
        work = work + alpha * norm_now
        solution = [
            solution[i] + (alpha * direction[i] if i < len(direction) else 0.0)
            for i in range(ITERS)
        ]
        if iteration + 1 < ITERS:
            image = [0.0] + direction
            residual = [
                (residual[i] if i < len(residual) else 0.0) - alpha * image[i]
                for i in range(len(image))
            ]
            norm_next = product(residual, residual, 0)
            beta = norm_next / norm_now
            direction = [
                residual[i] + (beta * direction[i] if i < len(direction) else 0.0)
                for i in range(len(residual))
            ]
            norm_now = norm_next
    factors = [solution[i] / powers[i + 1] for i in range(ITERS)]
    return factors, work * moments[0] / mean


def energy_kernel(
    elements, place, sums, loads, ahead, behind, first, second, density, solution, slope, out
):
    rows_of = [sums[k : k + 1, :] for k in range(2 * ITERS + 1)]
    factors, compliance = krylov_steps(rows_of[: 2 * ITERS])
    volume = rows_of[2 * ITERS]
    constant = 2.0 * penalty * (volume / elements - vol_target) / elements
    scale = -3.0 * (1.0 - emin) / compliance
    wide = [jnp.concatenate([value, value], axis=1) for value in factors + [scale, constant]]
    cells, rows, _ = density.shape
    modes = []
    for p in range(cells + 1):
        plane = []
        for d in range(3):
            load = load_plane(place, loads, ahead, behind, d, 2 + p)
            value = wide[0] * load + wide[1] * first[d, p] + wide[2] * second[d, p]
            if p < cells:
                solution[d, p] = value[:rows]
            plane.append(plane_modes(value, rows))
        modes.append(plane)
    for e in range(cells):
        energy = energy_of(element_modes(modes[e], modes[e + 1]))
        held = density[e]
        out[e] = held
        slope[e] = (wide[3] * held * held * energy + wide[4]) * held * (1.0 - held)


def column_of(line):
    size = line.shape[1]
    shape = (size, size)
    same = lax.broadcasted_iota(jnp.int32, shape, 0) == lax.broadcasted_iota(jnp.int32, shape, 1)
    return jnp.sum(jnp.where(same, line, 0.0), axis=1, keepdims=True)


def prepare_kernel(
    grid_cells, place, load_values, load_mask, fixed_mask, frequencies, w_in, w_mid, w_out,
    loads, loads_first, loads_last, x_cos, x_sin, z_cos, z_sin, w_in_t, w_mid_t, w_mid_half,
    w_column, w_row,
):
    cells, rows, size = load_mask.shape
    free = (1 - fixed_mask[...]).astype(F32)
    held = free * load_mask[...].astype(F32)
    for d in range(4):
        field = free if d == 3 else held * load_values[d]
        loads[d] = field
        loads_first[d] = field[:3]
        loads_last[d] = field[cells - 2 :]
    columns = [column_of(frequencies[k : k + 1, :]) for k in range(3)]
    half = rows // 2
    lanes = 2 * cells * half
    number = lax.broadcasted_iota(jnp.int32, (1, lanes), 1)
    side = number // (cells * half)
    plane = (number // half) % cells
    inner = number % half
    row = jnp.where(side == 1, inner + 2, jnp.where(inner < 2, inner, inner + half))
    x_centre = ((place[X_FIRST] + plane).astype(F32) + 0.5) / grid_cells[0]
    y_centre = ((place[Y_FIRST] + row).astype(F32) + 0.5) / grid_cells[1]
    phase = two_pi * (x_centre * columns[0] + y_centre * columns[1])
    cos, sin = jnp.cos(phase), jnp.sin(phase)
    for k in range(2 * cells):
        x_cos[k] = cos[:, k * half : (k + 1) * half]
        x_sin[k] = sin[:, k * half : (k + 1) * half]
    z_number = lax.broadcasted_iota(jnp.int32, (1, size), 1)
    phase = two_pi * (((z_number.astype(F32) + 0.5) / grid_cells[2]) * columns[2])
    z_cos[...] = jnp.cos(phase)
    z_sin[...] = jnp.sin(phase)
    w_in_t[...] = (0.5 * w_in[...].astype(F32)).T.astype(BF)
    middle = 0.5 * w_mid[...].astype(F32)
    w_mid_half[...] = middle.astype(BF)
    w_mid_t[...] = middle.T.astype(BF)
    line = w_out[...].astype(F32)[None, :]
    w_column[...] = 0.5 * column_of(line)
    w_row[...] = jnp.broadcast_to(line, w_row.shape).astype(BF)


def pack_kernel(place, loads, loads_ahead, loads_behind, stiff_first, stiff_last,
                planes, to_before, to_next):
    low, high = kept_if(place[SLAB_FIRST]), kept_if(place[SLAB_LAST])
    cells, rows = loads.shape[1:3]
    count = planes.shape[1]
    for d in range(4):
        for p in range(count):
            if p < 2:
                block = loads_behind[d, p] * low
            elif p < 2 + cells:
                block = loads[d, p - 2]
            else:
                block = loads_ahead[d, p - 2 - cells] * high
            planes[d, p] = block
            to_before[d * count + p] = block[:3]
            to_next[d * count + p] = block[rows - 2 :]
    for p in range(cells):
        to_before[4 * count + p, :2, :] = stiff_first[p]
        to_before[4 * count + p, 2:, :] = stiff_first[p, 1:]
        to_next[4 * count + p] = stiff_last[p]


def stiff_rows_kernel(place, stiff, ahead, behind, joined, to_before, to_next):
    cells = stiff.shape[0]
    first = ahead.shape[0] - cells
    for p in range(cells):
        block = with_rows(place, stiff[p], ahead[first + p, :2, :], behind[first + p])
        joined[p] = block
        if p < to_before.shape[0]:
            to_before[p] = block
        if p >= cells - to_next.shape[0]:
            to_next[p - (cells - to_next.shape[0])] = block


def gated(half):
    up = 1.0 + jnp.tanh(half)
    value = half * up
    return value, up + value * (2.0 - up)


def features_of(tables, group, column, scale=None):
    x_cos, x_sin, z_cos, z_sin = tables
    cos = x_cos[group, :, column : column + 1]
    sin = x_sin[group, :, column : column + 1]
    upper = z_cos[...] * cos - z_sin[...] * sin
    lower = z_sin[...] * cos + z_cos[...] * sin
    if scale is not None:
        upper, lower = upper * scale, lower * scale
    return jnp.concatenate([upper, lower], 0).astype(BF)


def forward_columns(tables, group, weights, kept, spans):
    w_in, w_mid, w_column, w_row = weights
    hidden_in, slope_mid, slope_in, hidden_mid = kept

    def keep(array, value):
        for start, first, count in spans:
            array[:, pl.ds(start, count)] = value[:, first : first + count]

    columns = tables[0].shape[2]
    features = jnp.concatenate([features_of(tables, group, q) for q in range(columns)], 1)
    value, slope = gated(jnp.dot(w_in[...], features, preferred_element_type=F32))
    value = value.astype(BF)
    keep(hidden_in, value)
    keep(slope_in, slope.astype(BF))
    value, slope = gated(jnp.dot(w_mid[...], value, preferred_element_type=F32))
    value = value.astype(BF)
    keep(hidden_mid, value)
    keep(slope_mid, (w_column[...] * slope).astype(BF))
    logits = jnp.dot(w_row[...], value, preferred_element_type=F32)[:1]
    return 0.5 * jnp.tanh(0.5 * logits) + 0.5


def stiffness_of(density):
    return emin + (1.0 - emin) * (density * density * density)


def outer_kernel(
    x_cos, x_sin, z_cos, z_sin, w_in, w_mid, w_column, w_row,
    density, stiff_first, stiff_last, *kept,
):
    tables, weights = (x_cos, x_sin, z_cos, z_sin), (w_in, w_mid, w_column, w_row)
    cells, _, size = density.shape

    @pl.loop(0, cells)
    def _(p):
        start = pl.multiple_of(p * (8 * size), 8 * size)
        spans = [(start, 0, 2 * size), (start + 6 * size, 2 * size, 2 * size)]
        line = forward_columns(tables, p, weights, kept, spans)
        for q in range(4):
            part = line[:, q * size : (q + 1) * size]
            density[p, q : q + 1, :] = part
            (stiff_first if q < 2 else stiff_last)[p, q % 2 : q % 2 + 1, :] = stiffness_of(part)


def inner_kernel(
    x_cos, x_sin, z_cos, z_sin, w_in, w_mid, w_column, w_row, outer, *rest,
):
    tables, weights = (x_cos, x_sin, z_cos, z_sin), (w_in, w_mid, w_column, w_row)
    density, stiff = rest[4:6]
    cells, rows, size = density.shape

    @pl.loop(0, cells)
    def _(p):
        start = pl.multiple_of(p * (8 * size), 8 * size)
        spans = [(start + 2 * size, 0, 4 * size)]
        line = forward_columns(tables, cells + p, weights, rest[6:], spans)
        for r in range(rows):
            if 2 <= r < 6:
                part = line[:, (r - 2) * size : (r - 1) * size]
            else:
                q = r if r < 2 else r - 4
                part = outer[p, q : q + 1, :]
            density[p, r : r + 1, :] = part
            stiff[p, r : r + 1, :] = stiffness_of(part)


def back_kernel(w_mid, slope_mid, slope_in, back, *, first, count, span):
    for start in range(first, first + count, span):
        place = slice(start, start + span)
        product = jnp.dot(w_mid[...], slope_mid[:, place], preferred_element_type=F32)
        back[:, place] = (product * slope_in[:, place].astype(F32)).astype(BF)


def gradient_kernel(
    place, slope, x_cos, x_sin, z_cos, z_sin, hidden_in, slope_mid, back, hidden_mid,
    mine, other, grad_out, mid, first, running,
):
    tables = (x_cos, x_sin, z_cos, z_sin)
    cells, rows, size = slope.shape
    half = rows // 2
    group_of = [(0, r) if r < 2 else (0, r - half) if r >= rows - 2 else (1, r - 2) for r in range(rows)]
    for p in range(cells):
        lines = [slope[p, r : r + 1, :] for r in range(rows)]
        picked = [
            features_of(tables, side * cells + p, q, line) for (side, q), line in zip(group_of, lines)
        ]
        features = jnp.concatenate(picked, 1)
        line = jnp.concatenate(lines, 1)
        span = slice(p * rows * size, (p + 1) * rows * size)
        hidden = (hidden_in[:, span].astype(F32) * line).astype(BF)
        product = hidden_mid[:, span].astype(F32) * line
        total = product[:, :128]
        for k in range(1, rows * size // 128):
            total = total + product[:, k * 128 : (k + 1) * 128]
        terms = (
            lax.dot_general(hidden, slope_mid[:, span], LAST, preferred_element_type=F32),
            lax.dot_general(back[:, span], features, LAST, preferred_element_type=F32),
            total,
        )
        for held, term in zip((mid, first, running), terms):
            if p == 0:
                held[...] = term
            else:
                held[...] += term
    core = place[CORE]
    height = mid.shape[0]
    first_t = first[...].T
    for k in range(2):
        for owner in range(2):
            lanes = slice((2 * owner + k) * 128, (2 * owner + k + 1) * 128)

            @pl.when(core == owner)
            def _():
                mine[k, :height, :] = mid[:, lanes]
                mine[k, height:, :] = first_t[:, lanes]

            @pl.when(core != owner)
            def _():
                other[k, :height, :] = mid[:, lanes]
                other[k, height:, :] = first_t[:, lanes]

    line = jnp.sum(running[...].T, axis=0, keepdims=True)
    for k in range(grad_out.shape[0]):
        grad_out[k : k + 1, :] = line[:, k * 128 : (k + 1) * 128]


def finish_kernel(place, half, away, grad_in, grad_mid, grad_out):
    chips = half.shape[0]
    height = half.shape[1] - 2 * grad_out.shape[0]
    middle = grad_mid.shape[0]
    at_first = place[CORE] == 0
    for group in range(4):
        part = pl.ds((group % 2) * (chips // 2), chips // 2)
        own, far = half[part, :height, :], away[part, :height, :]
        picked = jnp.where(at_first, own, far) if group < 2 else jnp.where(at_first, far, own)
        picked = picked.reshape(-1, 128)
        lanes = slice(group * 128, (group + 1) * 128)
        grad_mid[:, lanes] = picked[:middle]
        grad_in[:, lanes] = picked[middle:]
    out = jnp.sum(half[:, height:, :], axis=0) + jnp.sum(away[:, height:, :], axis=0)
    grad_out[...] = out[: grad_out.shape[0]]


VM = pltpu.VMEM
WHOLE = pl.BlockSpec(memory_space=pltpu.VMEM)
SCALARS = pl.BlockSpec(memory_space=pltpu.SMEM)
X_FIRST, Y_FIRST, CORE, SLAB_FIRST, SLAB_LAST, Z_FIRST, Z_LAST = range(7)


def params(mebibytes=8):
    return pltpu.CompilerParams(vmem_limit_bytes=mebibytes << 20)


def shaped(*shape, dtype=F32):
    return jax.ShapeDtypeStruct(shape, dtype)


def held(*shape, dtype=F32):
    return VM(shape, dtype)


def run(kernel, name, out_shape, *operands, scalars=1, space=pltpu.VMEM, scratch=(), limit=8, **more):
    arrays = [pltpu.with_memory_space_constraint(array, space) for array in operands[scalars:]]
    return pl.pallas_call(
        kernel,
        name=name,
        in_specs=[SCALARS] * scalars + [WHOLE] * len(arrays),
        out_specs=[WHOLE] * len(out_shape),
        out_shape=out_shape,
        scratch_shapes=list(scratch),
        compiler_params=params(limit),
        **more,
    )(*operands[:scalars], *arrays)


def shifted(block, axis, distance):
    size = lax.axis_size(axis)
    return lax.ppermute(block, axis, [(i, (i + distance) % size) for i in range(size)])


def summed(values):
    values = values + lax.ppermute(values, "c", [(0, 1), (1, 0)])
    for axis in ("z", "y", "x"):
        others = [shifted(values, axis, k) for k in range(1, lax.axis_size(axis))]
        values = values + sum(others)
    return values


def on_device(load_values, load_mask, fixed_mask, frequencies, weight_in, weight_mid, weight_out):
    cells_x, cells_y, cells_z = fixed_mask.shape
    slab, sub = lax.axis_index(SLAB), lax.axis_index("z")
    slabs, subs = lax.axis_size(SLAB), lax.axis_size("z")
    grid_cells = (cells_x * slabs, cells_y * subs, cells_z)
    elements_total = grid_cells[0] * grid_cells[1] * grid_cells[2]
    place = jnp.stack(
        [slab * cells_x, sub * cells_y, lax.axis_index("c")]
        + [(slab == 0) * 1, (slab == slabs - 1) * 1, (sub == 0) * 1, (sub == subs - 1) * 1, slab * 0]
    ).astype(jnp.int32)
    inputs, hidden = weight_in.shape
    rows = cells_x * cells_y * cells_z
    half_rows = cells_y // 2
    field = (cells_x, cells_y, cells_z)
    table = held(2 * cells_x, inputs // 2, half_rows)
    line = held(inputs // 2, cells_z)
    (
        loads, loads_first, loads_last, x_cos, x_sin, z_cos, z_sin,
        w_in_t, w_mid_t, w_mid_half, w_column, w_row,
    ) = run(
        functools.partial(prepare_kernel, grid_cells),
        "prepare",
        [
            held(4, *field),
            held(4, 3, cells_y, cells_z),
            held(4, 2, cells_y, cells_z),
            table,
            table,
            line,
            line,
            held(hidden, inputs, dtype=BF),
            held(hidden, hidden, dtype=BF),
            held(hidden, hidden, dtype=BF),
            held(hidden, 1),
            held(16, hidden, dtype=BF),
        ],
        place, load_values, load_mask, fixed_mask, frequencies, weight_in, weight_mid,
        weight_out, space=pltpu.HBM,
    )

    loads_ahead = shifted(loads_first, SLAB, -1)
    loads_behind = shifted(loads_last, SLAB, 1)
    network = (x_cos, x_sin, z_cos, z_sin, w_in_t, w_mid_t, w_column, w_row)
    kept = [held(hidden, rows, dtype=BF)] * 4
    cost = pl.CostEstimate(
        flops=(inputs + hidden) * hidden * rows,
        bytes_accessed=4 * hidden * rows,
        transcendentals=hidden * rows,
    )
    outer, stiff_first, stiff_last, *stored = run(
        outer_kernel,
        "outer",
        [held(cells_x, half_rows, cells_z)] + [held(cells_x, 2, cells_z)] * 2 + kept,
        *network,
        scalars=0,
        limit=12,
        cost_estimate=cost,
    )
    planes = cells_x + 5
    slots = 4 * planes + cells_x
    loads, rows_first, rows_last = run(
        pack_kernel,
        "pack",
        [held(4, planes, cells_y, cells_z), held(slots, 3, cells_z), held(slots, 2, cells_z)],
        place, loads, loads_ahead, loads_behind, stiff_first, stiff_last,
    )
    rows_ahead = shifted(rows_first, "z", -1)
    rows_behind = shifted(rows_last, "z", 1)
    density, stiff, *stored = run(
        inner_kernel,
        "inner",
        [held(*field)] * 2 + kept,
        *network,
        outer,
        *stored,
        scalars=0,
        limit=12,
        input_output_aliases={9 + k: 2 + k for k in range(4)},
        cost_estimate=cost,
    )
    hidden_in, slope_mid, slope_in, hidden_mid = stored
    stiff_16, stiff_before, stiff_next = run(
        stiff_rows_kernel,
        "stiff_rows",
        [held(cells_x, ROWS, cells_z), held(2, ROWS, cells_z), held(2, ROWS, cells_z)],
        place, stiff, rows_ahead, rows_behind,
    )
    stiff_ahead = shifted(stiff_before, SLAB, -1)
    stiff_behind = shifted(stiff_next, SLAB, 1)

    back = slope_in
    parts = 2
    for part in range(parts):
        count = rows // parts
        (back,) = run(
            functools.partial(back_kernel, first=part * count, count=count, span=1024),
            f"back_{part}",
            kept[:1],
            w_mid_half,
            slope_mid,
            back,
            scalars=0,
            limit=10,
            input_output_aliases={2: 0},
            cost_estimate=pl.CostEstimate(
                flops=2 * hidden * hidden * count,
                bytes_accessed=6 * hidden * count,
                transcendentals=0,
            ),
        )

    vector = held(3, cells_x + 1, ROWS, cells_z)
    first, second, sums = run(
        krylov_kernel,
        "krylov",
        [vector, vector, held(8, 128)],
        place, loads, rows_ahead, rows_behind, stiff_16, stiff_ahead, stiff_behind, density,
    )
    solution, slope, density = run(
        functools.partial(energy_kernel, elements_total),
        "energy",
        [shaped(3, *field), held(*field), shaped(*field)],
        place, summed(sums), loads, rows_ahead, rows_behind, first, second, density,
    )

    height = hidden + inputs
    groups = hidden // 128
    mine, other, grad_out = run(
        gradient_kernel,
        "gradients",
        [held(groups // 2, height, 128)] * 2 + [held(groups, 128)],
        place, slope, x_cos, x_sin, z_cos, z_sin, hidden_in, slope_mid, back, hidden_mid,
        limit=20,
        scratch=[VM((hidden, hidden), F32), VM((hidden, inputs), F32), VM((hidden, 128), F32)],
    )

    chips = lax.axis_size(CHIPS)
    swap = [(0, 1), (1, 0)]
    half = (mine + lax.ppermute(other, "c", swap)).reshape(chips, -1, 128)
    share = jnp.sum(lax.all_to_all(half, CHIPS, 0, 0), axis=0)
    share = jnp.concatenate([share, grad_out, jnp.zeros_like(grad_out)], axis=0)
    half = lax.all_to_all(jnp.broadcast_to(share[None], (chips,) + share.shape), CHIPS, 0, 0)
    away = lax.ppermute(half, "c", swap)
    grad_in, grad_mid, grad_out = run(
        finish_kernel,
        "finish",
        [shaped(inputs, hidden), shaped(hidden, hidden), shaped(groups, 128)],
        place, half, away,
    )
    return solution, density, grad_in, grad_mid, grad_out.reshape(hidden)


def solution(mesh):
    slab, sub = mesh.devices.shape
    fine = Mesh(mesh.devices.reshape(4, 4, slab // 16, sub), ALL)
    field = P(SLAB, "z", None)
    vector = P(None, SLAB, "z", None)
    return jax.shard_map(
        on_device,
        mesh=fine,
        in_specs=(vector, field, field, P(), P(), P(), P()),
        out_specs=(vector, field, P(), P(), P()),
        check_vma=False,
    )
```

profile of v0, /device:TPU:1, one launch (start us, length us, event | category | flops | bytes accessed | tf_op | source)
XLA Modules:
  0.0 130.6 jit_solution(7204462376727348953)
XLA Ops:
  0.7 2.6 %prepare.1 = (f32[4,4,8,256]{3,2,1,0:T(8,128)S(1)}, f32[4,3,8,256]{3,2,1,0:T(8,128)S(1)}, f32[4,2,8,256]{3,2,1,0:T(8,128)S(1)}, f32[8,128,4]{2,1,0:T(8,128)S(1)}...) custom-call(s32[8]{0:T(128)S(1)} %stack.47.place, ...), custom_call_target="tpu_custom_call" | custom-call | tf_op jit(solution)/shard_map/prepare/pallas_call | solution.py:560
  3.3 1.5 %collective-permute-start = (f32[4,3,8,256]{3,2,1,0:T(8,128)S(1)}, f32[4,3,8,256]{3,2,1,0:T(8,128)S(1)}, u32[]{:S(2)}, u32[]{:S(2)}) collective-permute-start(f32[4,3,8,256]{3,2,1,0:T(8,128)S(1)} %get-tuple-element.49), channel_id=1, source_target_pairs={{0,124},{4,0},{8,4},{12,8},{16,12},{20,16},{24,20},{28,24},{32,28}... | collective-permute-start | bytes 294920 | tf_op jit(solution)/shard_map/ppermute | solution.py:574
  6.2 7.2 %outer.1 = (f32[4,4,256]{2,1,0:T(4,128)S(1)}, f32[4,2,256]{2,1,0:T(2,128)S(1)}, f32[4,2,256]{2,1,0:T(2,128)S(1)}, bf16[512,8192]{1,0:T(8,128)(2,1)S(1)}, bf16[51...) custom-call(f32[8,128,4]{2,1,0:T(8,128)S(1)} %get-tuple-element.51.x_cos, ...), custom_call_target="tpu_custom_call" | custom-call | flops 3221225472 | bytes 16777216 | tf_op jit(solution)/shard_map/outer/pallas_call | solution.py:560
  13.9 3.8 %collective-permute-start.2 = (f32[40,3,256]{2,1,0:T(4,128)S(1)}, f32[40,3,256]{2,1,0:T(4,128)S(1)}, u32[]{:S(2)}, u32[]{:S(2)}) collective-permute-start(f32[40,3,256]{2,1,0:T(4,128)S(1)} %get-tuple-element.62), channel_id=1, source_target_pairs={{0,3},{1,0},{2,1},{3,2},{4,7},{5,4},{6,5},{7,6},{8,11},{9,8},{10,9... | collective-permute-start | bytes 368648 | tf_op jit(solution)/shard_map/ppermute | solution.py:574
  17.8 7.1 %inner.1 = (f32[4,8,256]{2,1,0:T(8,128)S(1)}, f32[4,8,256]{2,1,0:T(8,128)S(1)}, bf16[512,8192]{1,0:T(8,128)(2,1)S(1)}, bf16[512,8192]{1,0:T(8,128)(2,1)S(1)}, bf...) custom-call(f32[8,128,4]{2,1,0:T(8,128)S(1)} %get-tuple-element.51.x, ...), custom_call_target="tpu_custom_call", output_to_operand_aliasing={{2}: (9, {}), {3}: (10, {}), {4}: (11, {}), {5}: (12, {})} | custom-call | flops 3221225472 | bytes 16777216 | tf_op jit(solution)/shard_map/inner/pallas_call | solution.py:560
  25.5 3.7 %collective-permute-start.4 = (f32[2,16,256]{2,1,0:T(8,128)S(1)}, f32[2,16,256]{2,1,0:T(8,128)S(1)}, u32[]{:S(2)}, u32[]{:S(2)}) collective-permute-start(f32[2,16,256]{2,1,0:T(8,128)S(1)} %get-tuple-element.71), channel_id=1, source_target_pairs={{0,124},{4,0},{8,4},{12,8},{16,12},{20,16},{24,20},{28,24},{32,28}... | collective-permute-start | bytes 98312 | tf_op jit(solution)/shard_map/ppermute | solution.py:574
  30.1 4.6 %collective-permute-done.5.stiff_behind = f32[2,16,256]{2,1,0:T(8,128)S(1)} collective-permute-done((f32[2,16,256]{2,1,0:T(8,128)S(1)}, f32[2,16,256]{2,1,0:T(8,128)S(1)}, u32[]{:S(2)}, u32[]{:S(2)}) %collective-permute-start.5) | collective-permute-done | bytes 32800 | tf_op jit(solution)/shard_map/ppermute | solution.py:574
  34.7 2.6 %krylov.1 = (f32[3,5,16,256]{3,2,1,0:T(8,128)S(1)}, f32[3,5,16,256]{3,2,1,0:T(8,128)S(1)}, f32[8,128]{1,0:T(8,128)S(1)}) custom-call(s32[8]{0:T(128)S(1)} %stack.47.place, f32[4,9,8,256]{3,2,1,0:T(8,128)S(1)} %get-tuple-element.61.loads, f32[40,3,256]{2,1,0:T(4,128)S(1)} %collective-permute-done.2.ahead, f32[40,2,256]{2,1,0:T(2,128)S(1)} %collective-permute-done.3.behind, ...), custom_call_target="tpu_custom_call" | custom-call | tf_op jit(solution)/shard_map/krylov/pallas_call | solution.py:560
  37.4 6.0 %collective-permute-start.6 = (f32[8,128]{1,0:T(8,128)S(1)}, f32[8,128]{1,0:T(8,128)S(1)}, u32[]{:S(2)}, u32[]{:S(2)}) collective-permute-start(f32[8,128]{1,0:T(8,128)S(1)} %get-tuple-element.74), channel_id=1, source_target_pairs={{0,4},{4,0},{1,5},{5,1},{2,6},{6,2},{3,7},{7,3},{8,12},{12,8},{9,1... | collective-permute-start | bytes 12296 | tf_op jit(solution)/shard_map/ppermute | solution.py:578
  44.2 3.9 %collective-permute-start.8 = (f32[8,128]{1,0:T(8,128)S(1)}, f32[8,128]{1,0:T(8,128)S(1)}, u32[]{:S(2)}, u32[]{:S(2)}) collective-permute-start(f32[8,128]{1,0:T(8,128)S(1)} %add.41), channel_id=1, source_target_pairs={{0,2},{1,3},{2,0},{3,1},{4,6},{5,7},{6,4},{7,5},{8,10},{9,11},{10,... | collective-permute-start | bytes 12296 | tf_op jit(solution)/shard_map/ppermute | solution.py:574
  50.6 2.6 %collective-permute-start.12 = (f32[8,128]{1,0:T(8,128)S(1)}, f32[8,128]{1,0:T(8,128)S(1)}, u32[]{:S(2)}, u32[]{:S(2)}) collective-permute-start(f32[8,128]{1,0:T(8,128)S(1)} %add_add_fusion.2), channel_id=1, source_target_pairs={{0,24},{8,0},{16,8},{24,16},{1,25},{9,1},{17,9},{25,17},{2,26},{10... | collective-permute-start | bytes 12296 | tf_op jit(solution)/shard_map/ppermute | solution.py:574
  53.2 2.6 %back_0.1.slope_in = bf16[512,8192]{1,0:T(8,128)(2,1)S(1)} custom-call(bf16[512,512]{1,0:T(8,128)(2,1)S(1)} %get-tuple-element.82.w_mid, bf16[512,8192]{1,0:T(8,128)(2,1)S(1)} %get-tuple-element.81.slope_mid, bf16[512,8192]{1,0:T(8,128)(2,1)S(1)} %get-tuple-element.83.slope_in), custom_call_target="tpu_custom_call", output_to_operand_aliasing={{}: (2, {})} | custom-call | flops 2147483648 | bytes 12582912 | tf_op jit(solution)/shard_map/back_0/pallas_call | solution.py:560
  56.0 2.6 %collective-permute-start.15 = (f32[8,128]{1,0:T(8,128)S(1)}, f32[8,128]{1,0:T(8,128)S(1)}, u32[]{:S(2)}, u32[]{:S(2)}) collective-permute-start(f32[8,128]{1,0:T(8,128)S(1)} %add_add_fusion.1), channel_id=1, source_target_pairs={{0,96},{32,0},{64,32},{96,64},{1,97},{33,1},{65,33},{97,65},{2,98}... | collective-permute-start | bytes 12296 | tf_op jit(solution)/shard_map/ppermute | solution.py:574
  58.6 2.6 %back_1.1.back = bf16[512,8192]{1,0:T(8,128)(2,1)S(1)} custom-call(bf16[512,512]{1,0:T(8,128)(2,1)S(1)} %get-tuple-element.82.w_mid, bf16[512,8192]{1,0:T(8,128)(2,1)S(1)} %get-tuple-element.81.slope_mid, bf16[512,8192]{1,0:T(8,128)(2,1)S(1)} %back_0.1.slope_in), custom_call_target="tpu_custom_call", output_to_operand_aliasing={{}: (2, {})} | custom-call | flops 2147483648 | bytes 12582912 | tf_op jit(solution)/shard_map/back_1/pallas_call | solution.py:560
  61.2 1.4 %energy.1 = (f32[3,4,8,256]{3,2,1,0:T(8,128)}, f32[4,8,256]{2,1,0:T(8,128)S(1)}, f32[4,8,256]{2,1,0:T(8,128)}) custom-call(s32[8]{0:T(128)S(1)} %stack.47.place, f32[8,128]{1,0:T(8,128)S(1)} %add_add_fusion.sums, f32[4,9,8,256]{3,2,1,0:T(8,128)S(1)} %get-tuple-element.61.loads, f32[40,3,256]{2,1,0:T(4,128)S(1)} %collective-permute-done.2.ahead, ...), custom_call_target="tpu_custom_call" | custom-call | tf_op jit(solution)/shard_map/energy/pallas_call | solution.py:560
  62.7 10.1 %gradients.1 = (f32[2,768,128]{2,1,0:T(8,128)S(1)}, f32[2,768,128]{2,1,0:T(8,128)S(1)}, f32[4,128]{1,0:T(4,128)S(1)}) custom-call(s32[8]{0:T(128)} %copy-done.1, f32[4,8,256]{2,1,0:T(8,128)S(1)} %get-tuple-element.79.slope, f32[8,128,4]{2,1,0:T(8,128)S(1)} %get-tuple-element.51.x_cos, f32[8,128,4]{2,1,0:T(8,128)S(1)} %get-tuple-element.52.x_sin, ...), custom_call_target="tpu_custom_call" | custom-call | tf_op jit(solution)/shard_map/gradients/pallas_call | solution.py:560
  72.8 3.2 %collective-permute-start.16 = (f32[2,768,128]{2,1,0:T(8,128)S(1)}, f32[2,768,128]{2,1,0:T(8,128)S(1)}, u32[]{:S(2)}, u32[]{:S(2)}) collective-permute-start(f32[2,768,128]{2,1,0:T(8,128)S(1)} %get-tuple-element.86), channel_id=1, source_target_pairs={{0,4},{4,0},{1,5},{5,1},{2,6},{6,2},{3,7},{7,3},{8,12},{12,8},{9,1... | collective-permute-start | bytes 2359304 | tf_op jit(solution)/shard_map/ppermute | solution.py:723
  76.0 1.9 %collective-permute-done.16 = f32[2,768,128]{2,1,0:T(8,128)S(1)} collective-permute-done((f32[2,768,128]{2,1,0:T(8,128)S(1)}, f32[2,768,128]{2,1,0:T(8,128)S(1)}, u32[]{:S(2)}, u32[]{:S(2)}) %collective-permute-start.16) | collective-permute-done | bytes 786464 | tf_op jit(solution)/shard_map/ppermute | solution.py:723
  78.9 8.5 %all-to-all-start = ((f32[64,24,128]{2,1,0:T(8,128)}), f32[64,24,128]{2,1,0:T(8,128)S(1)}, u32[]{:S(2)}, u32[]{:S(2)}) async-start(f32[64,24,128]{2,1,0:T(8,128)} %bitcast.7), calls=%async_computation | async-start | bytes 1572864 | tf_op jit(solution)/shard_map/all_to_all | solution.py:724
  87.5 14.5 %all-to-all-done = f32[64,24,128]{2,1,0:T(8,128)S(1)} async-done(((f32[64,24,128]{2,1,0:T(8,128)}), f32[64,24,128]{2,1,0:T(8,128)S(1)}, u32[]{:S(2)}, u32[]{:S(2)}) %all-to-all-start) | async-done | bytes 786464 | tf_op jit(solution)/shard_map/all_to_all | solution.py:724
  102.3 20.8 %all_to_all.10.half = f32[64,32,128]{2,1,0:T(8,128)S(1)} all-to-all(f32[64,32,128]{2,1,0:T(8,128)S(1)} %broadcast_in_dim.10), channel_id=1, replica_groups=mesh['x'=4,'y'=4,'c'=2,'z'=4] {'x','y','z'}, dimensions={0} | all-to-all | bytes 2097152 | tf_op jit(solution)/shard_map/all_to_all | solution.py:726
  123.1 3.5 %collective-permute-start.17 = (f32[64,32,128]{2,1,0:T(8,128)S(1)}, f32[64,32,128]{2,1,0:T(8,128)S(1)}, u32[]{:S(2)}, u32[]{:S(2)}) collective-permute-start(f32[64,32,128]{2,1,0:T(8,128)S(1)} %all_to_all.10.half), channel_id=1, source_target_pairs={{0,4},{4,0},{1,5},{5,1},{2,6},{6,2},{3,7},{7,3},{8,12},{12,8},{9,1... | collective-permute-start | bytes 3145736 | tf_op jit(solution)/shard_map/ppermute | solution.py:727
  126.5 2.3 %collective-permute-done.17.away = f32[64,32,128]{2,1,0:T(8,128)S(1)} collective-permute-done((f32[64,32,128]{2,1,0:T(8,128)S(1)}, f32[64,32,128]{2,1,0:T(8,128)S(1)}, u32[]{:S(2)}, u32[]{:S(2)}) %collective-permute-start.17) | collective-permute-done | bytes 1048608 | tf_op jit(solution)/shard_map/ppermute | solution.py:727
  128.8 1.8 %finish.1 = (f32[256,512]{1,0:T(8,128)}, f32[512,512]{1,0:T(8,128)}, f32[4,128]{1,0:T(4,128)}) custom-call(s32[8]{0:T(128)S(1)} %copy-done.2, f32[64,32,128]{2,1,0:T(8,128)S(1)} %all_to_all.10.half, f32[64,32,128]{2,1,0:T(8,128)S(1)} %collective-permute-done.17.away), custom_call_target="tpu_custom_call" | custom-call | tf_op jit(solution)/shard_map/finish/pallas_call | solution.py:560
  (48 shorter events, 8.3 us)
Async XLA Ops:
  0.7 60.5 %copy-start.1 = (s32[8]{0:T(128)}, s32[8]{0:T(128)S(1)}, u32[]{:S(2)}) copy-start(s32[8]{0:T(128)S(1)} %stack.47.place) | copy-start | bytes 100
  3.3 10.0 %collective-permute-start = (f32[4,3,8,256]{3,2,1,0:T(8,128)S(1)}, f32[4,3,8,256]{3,2,1,0:T(8,128)S(1)}, u32[]{:S(2)}, u32[]{:S(2)}) collective-permute-start(f32[4,3,8,256]{3,2,1,0:T(8,128)S(1)} %get-tuple-element.49), channel_id=1, source_target_pairs={{0,124},{4,0},{8,4},{12,8},{16,12},{20,16},{24,20},{28,24},{32,28}... | collective-permute-start | bytes 294920 | tf_op jit(solution)/shard_map/ppermute | solution.py:574
  4.8 8.5 %collective-permute-start.1 = (f32[4,2,8,256]{3,2,1,0:T(8,128)S(1)}, f32[4,2,8,256]{3,2,1,0:T(8,128)S(1)}, u32[]{:S(2)}, u32[]{:S(2)}) collective-permute-start(f32[4,2,8,256]{3,2,1,0:T(8,128)S(1)} %get-tuple-element.50), channel_id=1, source_target_pairs={{0,4},{4,8},{8,12},{12,16},{16,20},{20,24},{24,28},{28,32},{32,36}... | collective-permute-start | bytes 196616 | tf_op jit(solution)/shard_map/ppermute | solution.py:574
  13.9 11.0 %collective-permute-start.2 = (f32[40,3,256]{2,1,0:T(4,128)S(1)}, f32[40,3,256]{2,1,0:T(4,128)S(1)}, u32[]{:S(2)}, u32[]{:S(2)}) collective-permute-start(f32[40,3,256]{2,1,0:T(4,128)S(1)} %get-tuple-element.62), channel_id=1, source_target_pairs={{0,3},{1,0},{2,1},{3,2},{4,7},{5,4},{6,5},{7,6},{8,11},{9,8},{10,9... | collective-permute-start | bytes 368648 | tf_op jit(solution)/shard_map/ppermute | solution.py:574
  17.8 7.1 %collective-permute-start.3 = (f32[40,2,256]{2,1,0:T(2,128)S(1)}, f32[40,2,256]{2,1,0:T(2,128)S(1)}, u32[]{:S(2)}, u32[]{:S(2)}) collective-permute-start(f32[40,2,256]{2,1,0:T(2,128)S(1)} %get-tuple-element.63), channel_id=1, source_target_pairs={{0,1},{1,2},{2,3},{3,0},{4,5},{5,6},{6,7},{7,4},{8,9},{9,10},{10,1... | collective-permute-start | bytes 245768 | tf_op jit(solution)/shard_map/ppermute | solution.py:574
  24.9 30.9 %copy-start = (bf16[512,8192]{1,0:T(8,128)(2,1)}, bf16[512,8192]{1,0:T(8,128)(2,1)S(1)}, u32[]{:S(2)}) copy-start(bf16[512,8192]{1,0:T(8,128)(2,1)S(1)} %get-tuple-element.80.hidden_in) | copy-start | bytes 25165828
  25.5 4.6 %collective-permute-start.4 = (f32[2,16,256]{2,1,0:T(8,128)S(1)}, f32[2,16,256]{2,1,0:T(8,128)S(1)}, u32[]{:S(2)}, u32[]{:S(2)}) collective-permute-start(f32[2,16,256]{2,1,0:T(8,128)S(1)} %get-tuple-element.71), channel_id=1, source_target_pairs={{0,124},{4,0},{8,4},{12,8},{16,12},{20,16},{24,20},{28,24},{32,28}... | collective-permute-start | bytes 98312 | tf_op jit(solution)/shard_map/ppermute | solution.py:574
  29.2 5.5 %collective-permute-start.5 = (f32[2,16,256]{2,1,0:T(8,128)S(1)}, f32[2,16,256]{2,1,0:T(8,128)S(1)}, u32[]{:S(2)}, u32[]{:S(2)}) collective-permute-start(f32[2,16,256]{2,1,0:T(8,128)S(1)} %get-tuple-element.72), channel_id=1, source_target_pairs={{0,4},{4,8},{8,12},{12,16},{16,20},{20,24},{24,28},{28,32},{32,36}... | collective-permute-start | bytes 98312 | tf_op jit(solution)/shard_map/ppermute | solution.py:574
  37.4 6.8 %collective-permute-start.6 = (f32[8,128]{1,0:T(8,128)S(1)}, f32[8,128]{1,0:T(8,128)S(1)}, u32[]{:S(2)}, u32[]{:S(2)}) collective-permute-start(f32[8,128]{1,0:T(8,128)S(1)} %get-tuple-element.74), channel_id=1, source_target_pairs={{0,4},{4,0},{1,5},{5,1},{2,6},{6,2},{3,7},{7,3},{8,12},{12,8},{9,1... | collective-permute-start | bytes 12296 | tf_op jit(solution)/shard_map/ppermute | solution.py:578
  44.2 3.9 %collective-permute-start.7 = (f32[8,128]{1,0:T(8,128)S(1)}, f32[8,128]{1,0:T(8,128)S(1)}, u32[]{:S(2)}, u32[]{:S(2)}) collective-permute-start(f32[8,128]{1,0:T(8,128)S(1)} %add.41), channel_id=1, source_target_pairs={{0,1},{1,2},{2,3},{3,0},{4,5},{5,6},{6,7},{7,4},{8,9},{9,10},{10,1... | collective-permute-start | bytes 12296 | tf_op jit(solution)/shard_map/ppermute | solution.py:574
  44.2 4.9 %collective-permute-start.8 = (f32[8,128]{1,0:T(8,128)S(1)}, f32[8,128]{1,0:T(8,128)S(1)}, u32[]{:S(2)}, u32[]{:S(2)}) collective-permute-start(f32[8,128]{1,0:T(8,128)S(1)} %add.41), channel_id=1, source_target_pairs={{0,2},{1,3},{2,0},{3,1},{4,6},{5,7},{6,4},{7,5},{8,10},{9,11},{10,... | collective-permute-start | bytes 12296 | tf_op jit(solution)/shard_map/ppermute | solution.py:574
  48.0 2.5 %collective-permute-start.9 = (f32[8,128]{1,0:T(8,128)S(1)}, f32[8,128]{1,0:T(8,128)S(1)}, u32[]{:S(2)}, u32[]{:S(2)}) collective-permute-start(f32[8,128]{1,0:T(8,128)S(1)} %add.41), channel_id=1, source_target_pairs={{0,3},{1,0},{2,1},{3,2},{4,7},{5,4},{6,5},{7,6},{8,11},{9,8},{10,9... | collective-permute-start | bytes 12296 | tf_op jit(solution)/shard_map/ppermute | solution.py:574
  50.5 5.3 %collective-permute-start.10 = (f32[8,128]{1,0:T(8,128)S(1)}, f32[8,128]{1,0:T(8,128)S(1)}, u32[]{:S(2)}, u32[]{:S(2)}) collective-permute-start(f32[8,128]{1,0:T(8,128)S(1)} %add_add_fusion.2), channel_id=1, source_target_pairs={{0,8},{8,16},{16,24},{24,0},{1,9},{9,17},{17,25},{25,1},{2,10},{10... | collective-permute-start | bytes 12296 | tf_op jit(solution)/shard_map/ppermute | solution.py:574
  50.5 5.3 %collective-permute-start.11 = (f32[8,128]{1,0:T(8,128)S(1)}, f32[8,128]{1,0:T(8,128)S(1)}, u32[]{:S(2)}, u32[]{:S(2)}) collective-permute-start(f32[8,128]{1,0:T(8,128)S(1)} %add_add_fusion.2), channel_id=1, source_target_pairs={{0,16},{8,24},{16,0},{24,8},{1,17},{9,25},{17,1},{25,9},{2,18},{10... | collective-permute-start | bytes 12296 | tf_op jit(solution)/shard_map/ppermute | solution.py:574
  50.6 5.2 %collective-permute-start.12 = (f32[8,128]{1,0:T(8,128)S(1)}, f32[8,128]{1,0:T(8,128)S(1)}, u32[]{:S(2)}, u32[]{:S(2)}) collective-permute-start(f32[8,128]{1,0:T(8,128)S(1)} %add_add_fusion.2), channel_id=1, source_target_pairs={{0,24},{8,0},{16,8},{24,16},{1,25},{9,1},{17,9},{25,17},{2,26},{10... | collective-permute-start | bytes 12296 | tf_op jit(solution)/shard_map/ppermute | solution.py:574
  55.8 6.9 %slice-start = ((s8[8388608]{0:T(1024)(128)(4,1)}), s8[4194304]{0:T(1024)(128)(4,1)S(1)}, s32[]{:S(2)}) async-start(s8[8388608]{0:T(1024)(128)(4,1)} %bitcast.9), calls=%async_computation.2 | async-start | bytes 8388608
  55.8 6.8 %slice-start.1 = ((s8[8388608]{0:T(1024)(128)(4,1)}), s8[4194304]{0:T(1024)(128)(4,1)S(1)}, s32[]{:S(2)}) async-start(s8[8388608]{0:T(1024)(128)(4,1)} %bitcast.9), calls=%async_computation.3 | async-start | bytes 8388608
  55.8 5.3 %collective-permute-start.13 = (f32[8,128]{1,0:T(8,128)S(1)}, f32[8,128]{1,0:T(8,128)S(1)}, u32[]{:S(2)}, u32[]{:S(2)}) collective-permute-start(f32[8,128]{1,0:T(8,128)S(1)} %add_add_fusion.1), channel_id=1, source_target_pairs={{0,32},{32,64},{64,96},{96,0},{1,33},{33,65},{65,97},{97,1},{2,34}... | collective-permute-start | bytes 12296 | tf_op jit(solution)/shard_map/ppermute | solution.py:574
  55.9 5.3 %collective-permute-start.14 = (f32[8,128]{1,0:T(8,128)S(1)}, f32[8,128]{1,0:T(8,128)S(1)}, u32[]{:S(2)}, u32[]{:S(2)}) collective-permute-start(f32[8,128]{1,0:T(8,128)S(1)} %add_add_fusion.1), channel_id=1, source_target_pairs={{0,64},{32,96},{64,0},{96,32},{1,65},{33,97},{65,1},{97,33},{2,66}... | collective-permute-start | bytes 12296 | tf_op jit(solution)/shard_map/ppermute | solution.py:574
  56.0 5.2 %collective-permute-start.15 = (f32[8,128]{1,0:T(8,128)S(1)}, f32[8,128]{1,0:T(8,128)S(1)}, u32[]{:S(2)}, u32[]{:S(2)}) collective-permute-start(f32[8,128]{1,0:T(8,128)S(1)} %add_add_fusion.1), channel_id=1, source_target_pairs={{0,96},{32,0},{64,32},{96,64},{1,97},{33,1},{65,33},{97,65},{2,98}... | collective-permute-start | bytes 12296 | tf_op jit(solution)/shard_map/ppermute | solution.py:574
  62.7 66.1 %copy-start.2 = (s32[8]{0:T(128)S(1)}, s32[8]{0:T(128)}, u32[]{:S(2)}) copy-start(s32[8]{0:T(128)} %copy-done.1) | copy-start | bytes 100
  72.8 5.1 %collective-permute-start.16 = (f32[2,768,128]{2,1,0:T(8,128)S(1)}, f32[2,768,128]{2,1,0:T(8,128)S(1)}, u32[]{:S(2)}, u32[]{:S(2)}) collective-permute-start(f32[2,768,128]{2,1,0:T(8,128)S(1)} %get-tuple-element.86), channel_id=1, source_target_pairs={{0,4},{4,0},{1,5},{5,1},{2,6},{6,2},{3,7},{7,3},{8,12},{12,8},{9,1... | collective-permute-start | bytes 2359304 | tf_op jit(solution)/shard_map/ppermute | solution.py:723
  78.9 23.1 %all-to-all-start = ((f32[64,24,128]{2,1,0:T(8,128)}), f32[64,24,128]{2,1,0:T(8,128)S(1)}, u32[]{:S(2)}, u32[]{:S(2)}) async-start(f32[64,24,128]{2,1,0:T(8,128)} %bitcast.7), calls=%async_computation | async-start | bytes 1572864 | tf_op jit(solution)/shard_map/all_to_all | solution.py:724
  123.1 5.7 %collective-permute-start.17 = (f32[64,32,128]{2,1,0:T(8,128)S(1)}, f32[64,32,128]{2,1,0:T(8,128)S(1)}, u32[]{:S(2)}, u32[]{:S(2)}) collective-permute-start(f32[64,32,128]{2,1,0:T(8,128)S(1)} %all_to_all.10.half), channel_id=1, source_target_pairs={{0,4},{4,0},{1,5},{5,1},{2,6},{6,2},{3,7},{7,3},{8,12},{12,8},{9,1... | collective-permute-start | bytes 3145736 | tf_op jit(solution)/shard_map/ppermute | solution.py:727
where the time goes:
time: 131 us
  starting transfers between devices  40.8 us (31%)
  Pallas kernels  39.2 us (30%)
  waiting for transfers between devices  27.5 us (21%)
  blocking collectives  20.8 us (16%)
    pallas_call x11, Pallas kernels, run(): pl.pallas_call(kernel, name=name, in_specs=[SCALARS] * scalars + [WHOLE]...  39.2 us
    all_to_all x1, blocking collectives, on_device(): lax.all_to_all(jnp.broadcast_to(share[None], (chips,) + share.shape), CHI...  20.8 us
    ppermute x15, starting transfers between devices, shifted(): lax.ppermute(block, axis, [(i, (i + distance) % size) for i in range(size)])  19.7 us
    all_to_all x1, waiting for transfers between devices, on_device(): share = jnp.sum(lax.all_to_all(half, CHIPS, 0, 0), axis=0)  14.5 us
    all_to_all x1, starting transfers between devices, on_device(): share = jnp.sum(lax.all_to_all(half, CHIPS, 0, 0), axis=0)  8.52 us
    ppermute x15, waiting for transfers between devices, shifted(): lax.ppermute(block, axis, [(i, (i + distance) % size) for i in range(size)])  7.97 us
    ppermute x1, starting transfers between devices, summed(): values = values + lax.ppermute(values, 'c', [(0, 1), (1, 0)])  5.98 us
    ppermute x1, starting transfers between devices, on_device(): away = lax.ppermute(half, 'c', swap)  3.45 us
  transfers between devices with their start and end apart: 19, of which 8 were waited for; matrix products, arithmetic and copies ran while one was open for 0% of the time, Pallas kernels for 15%

commit v1 on v0

--- a/solution.py
+++ b/solution.py
@@ -179,7 +179,7 @@
 
 
 def krylov_kernel(place, loads, ahead, behind, stiff, stiff_ahead, stiff_behind, density,
-                  first, second, sums):
+                  ready, first, second, sums):
     planes = loads.shape[1]
     cells = planes - 5
     low, high = kept_if(place[SLAB_FIRST]), kept_if(place[SLAB_LAST])
@@ -460,7 +460,8 @@
             stiff[p, r : r + 1, :] = stiffness_of(part)
 
 
-def back_kernel(w_mid, slope_mid, slope_in, back, *, first, count, span):
+def back_kernel(w_mid, slope_mid, slope_in, back, done, *, first, count, span):
+    done[...] = jnp.zeros_like(done)
     for start in range(first, first + count, span):
         place = slice(start, start + span)
         product = jnp.dot(w_mid[...], slope_mid[:, place], preferred_element_type=F32)
@@ -520,6 +521,16 @@
         grad_out[k : k + 1, :] = line[:, k * 128 : (k + 1) * 128]
 
 
+def share_kernel(place, parts, grad_out, shares):
+    chips, height, lanes = parts.shape
+    total = parts[0]
+    for chip in range(1, chips):
+        total = total + parts[chip]
+    block = jnp.concatenate([total, grad_out[...], jnp.zeros(grad_out.shape, F32)], axis=0)
+    for chip in range(chips):
+        shares[chip] = block
+
+
 def finish_kernel(place, half, away, grad_in, grad_mid, grad_out):
     chips = half.shape[0]
     height = half.shape[1] - 2 * grad_out.shape[0]
@@ -555,7 +566,7 @@
     return VM(shape, dtype)
 
 
-def run(kernel, name, out_shape, *operands, scalars=1, space=pltpu.VMEM, scratch=(), limit=8, **more):
+def run(kernel, name, out_shape, *operands, scalars=1, space=pltpu.VMEM, scratch=(), limit=16, **more):
     arrays = [pltpu.with_memory_space_constraint(array, space) for array in operands[scalars:]]
     return pl.pallas_call(
         kernel,
@@ -637,7 +648,7 @@
         [held(cells_x, half_rows, cells_z)] + [held(cells_x, 2, cells_z)] * 2 + kept,
         *network,
         scalars=0,
-        limit=12,
+        limit=16,
         cost_estimate=cost,
     )
     planes = cells_x + 5
@@ -658,7 +669,7 @@
         outer,
         *stored,
         scalars=0,
-        limit=12,
+        limit=16,
         input_output_aliases={9 + k: 2 + k for k in range(4)},
         cost_estimate=cost,
     )
@@ -673,18 +684,19 @@
     stiff_behind = shifted(stiff_next, SLAB, 1)
 
     back = slope_in
-    parts = 2
-    for part in range(parts):
-        count = rows // parts
-        (back,) = run(
-            functools.partial(back_kernel, first=part * count, count=count, span=1024),
+    ready = []
+    begin = 0
+    for part, share in enumerate((2, 4, 4)):
+        count = rows // share
+        back, done = run(
+            functools.partial(back_kernel, first=begin, count=count, span=1024),
             f"back_{part}",
-            kept[:1],
+            kept[:1] + [held(8, 128)],
             w_mid_half,
             slope_mid,
             back,
             scalars=0,
-            limit=10,
+            limit=16,
             input_output_aliases={2: 0},
             cost_estimate=pl.CostEstimate(
                 flops=2 * hidden * hidden * count,
@@ -692,6 +704,8 @@
                 transcendentals=0,
             ),
         )
+        begin += count
+        ready.append(done)
 
     vector = held(3, cells_x + 1, ROWS, cells_z)
     first, second, sums = run(
@@ -699,6 +713,7 @@
         "krylov",
         [vector, vector, held(8, 128)],
         place, loads, rows_ahead, rows_behind, stiff_16, stiff_ahead, stiff_behind, density,
+        ready[0],
     )
     solution, slope, density = run(
         functools.partial(energy_kernel, elements_total),
@@ -714,16 +729,18 @@
         "gradients",
         [held(groups // 2, height, 128)] * 2 + [held(groups, 128)],
         place, slope, x_cos, x_sin, z_cos, z_sin, hidden_in, slope_mid, back, hidden_mid,
-        limit=20,
+        limit=16,
         scratch=[VM((hidden, hidden), F32), VM((hidden, inputs), F32), VM((hidden, 128), F32)],
     )
 
     chips = lax.axis_size(CHIPS)
     swap = [(0, 1), (1, 0)]
     half = (mine + lax.ppermute(other, "c", swap)).reshape(chips, -1, 128)
-    share = jnp.sum(lax.all_to_all(half, CHIPS, 0, 0), axis=0)
-    share = jnp.concatenate([share, grad_out, jnp.zeros_like(grad_out)], axis=0)
-    half = lax.all_to_all(jnp.broadcast_to(share[None], (chips,) + share.shape), CHIPS, 0, 0)
+    parts = lax.all_to_all(half, CHIPS, 0, 0)
+    (shares,) = run(
+        share_kernel, "share", [held(chips, half.shape[1] + 2 * groups, 128)], place, parts, grad_out
+    )
+    half = lax.all_to_all(shares, CHIPS, 0, 0)
     away = lax.ppermute(half, "c", swap)
     grad_in, grad_mid, grad_out = run(
         finish_kernel,

time: 131 us -> 130 us (level)
  blocking collectives: 20.8 us -> 42.6 us
  waiting for transfers between devices: 27.5 us -> 10.4 us
  starting transfers between devices: 40.8 us -> 33.8 us
  Pallas kernels: 39.2 us -> 41.7 us
    all_to_all x1 -> x2, blocking collectives: 20.8 us -> 42.6 us  [the longest x1 21.8 us: on_device(): parts = lax.all_to_all(half, CHIPS, 0, 0)]
    all_to_all x1 -> x0, waiting for transfers between devices: 14.5 us -> none  [on_device(): share = jnp.sum(lax.all_to_all(half, CHIPS, 0, 0), axis=0)]
    all_to_all x1 -> x0, starting transfers between devices: 8.52 us -> none  [on_device(): share = jnp.sum(lax.all_to_all(half, CHIPS, 0, 0), axis=0)]
    ppermute x15, waiting for transfers between devices: 7.97 us -> 5.37 us  [shifted(): lax.ppermute(block, axis, [(i, (i + distance) % size) for i in range(size)])]
    pallas_call x11 -> x13, Pallas kernels: 39.2 us -> 41.7 us  [run(): pl.pallas_call(kernel, name=name, in_specs=[SCALARS] * scalars + [WHOLE]...]
    ppermute x1, starting transfers between devices: 3.24 us -> 4.65 us  [on_device(): half = (mine + lax.ppermute(other, 'c', swap)).reshape(chips, -1, 128)]
  transfers between devices with their start and end apart: 19 -> 18, of which waited for: 8 -> 6; matrix products, arithmetic and copies ran while one was open for 0% -> 0% of each run, Pallas kernels for 15% -> 16%
where the time goes in v1:
time: 130 us; the launch traced here: 129 us
  blocking collectives  42.6 us (33%)
  Pallas kernels  41.7 us (32%)
  starting transfers between devices  33.8 us (26%)
  waiting for transfers between devices  10.4 us (8%)
    pallas_call x13, Pallas kernels, run(): pl.pallas_call(kernel, name=name, in_specs=[SCALARS] * scalars + [WHOLE]...  41.7 us
    all_to_all x1, blocking collectives, on_device(): parts = lax.all_to_all(half, CHIPS, 0, 0)  21.8 us
    all_to_all x1, blocking collectives, on_device(): half = lax.all_to_all(shares, CHIPS, 0, 0)  20.8 us
    ppermute x15, starting transfers between devices, shifted(): lax.ppermute(block, axis, [(i, (i + distance) % size) for i in range(size)])  19.7 us
    ppermute x1, starting transfers between devices, summed(): values = values + lax.ppermute(values, 'c', [(0, 1), (1, 0)])  5.98 us
    ppermute x15, waiting for transfers between devices, shifted(): lax.ppermute(block, axis, [(i, (i + distance) % size) for i in range(size)])  5.37 us
    ppermute x1, starting transfers between devices, on_device(): half = (mine + lax.ppermute(other, 'c', swap)).reshape(chips, -1, 128)  4.65 us
    ppermute x1, starting transfers between devices, on_device(): away = lax.ppermute(half, 'c', swap)  3.45 us
  transfers between devices with their start and end apart: 18, of which 6 were waited for; matrix products, arithmetic and copies ran while one was open for 0% of the time, Pallas kernels for 16%

profile of v1, /device:TPU:1, one launch (start us, length us, event | category | flops | bytes accessed | tf_op | source)
XLA Modules:
  0.0 129.5 jit_solution(4965032432418721681)
XLA Ops:
  0.7 2.6 %prepare.1 = (f32[4,4,8,256]{3,2,1,0:T(8,128)S(1)}, f32[4,3,8,256]{3,2,1,0:T(8,128)S(1)}, f32[4,2,8,256]{3,2,1,0:T(8,128)S(1)}, f32[8,128,4]{2,1,0:T(8,128)S(1)}...) custom-call(s32[8]{0:T(128)S(1)} %stack.47.place, ...), custom_call_target="tpu_custom_call" | custom-call | tf_op jit(solution)/shard_map/prepare/pallas_call | solution.py:571
  3.3 1.5 %collective-permute-start = (f32[4,3,8,256]{3,2,1,0:T(8,128)S(1)}, f32[4,3,8,256]{3,2,1,0:T(8,128)S(1)}, u32[]{:S(2)}, u32[]{:S(2)}) collective-permute-start(f32[4,3,8,256]{3,2,1,0:T(8,128)S(1)} %get-tuple-element.53), channel_id=1, source_target_pairs={{0,124},{4,0},{8,4},{12,8},{16,12},{20,16},{24,20},{28,24},{32,28}... | collective-permute-start | bytes 294920 | tf_op jit(solution)/shard_map/ppermute | solution.py:585
  6.2 7.3 %outer.1 = (f32[4,4,256]{2,1,0:T(4,128)S(1)}, f32[4,2,256]{2,1,0:T(2,128)S(1)}, f32[4,2,256]{2,1,0:T(2,128)S(1)}, bf16[512,8192]{1,0:T(8,128)(2,1)S(1)}, bf16[51...) custom-call(f32[8,128,4]{2,1,0:T(8,128)S(1)} %get-tuple-element.55.x_cos, ...), custom_call_target="tpu_custom_call" | custom-call | flops 3221225472 | bytes 16777216 | tf_op jit(solution)/shard_map/outer/pallas_call | solution.py:571
  14.1 3.8 %collective-permute-start.2 = (f32[40,3,256]{2,1,0:T(4,128)S(1)}, f32[40,3,256]{2,1,0:T(4,128)S(1)}, u32[]{:S(2)}, u32[]{:S(2)}) collective-permute-start(f32[40,3,256]{2,1,0:T(4,128)S(1)} %get-tuple-element.66), channel_id=1, source_target_pairs={{0,3},{1,0},{2,1},{3,2},{4,7},{5,4},{6,5},{7,6},{8,11},{9,8},{10,9... | collective-permute-start | bytes 368648 | tf_op jit(solution)/shard_map/ppermute | solution.py:585
  17.9 7.3 %inner.1 = (f32[4,8,256]{2,1,0:T(8,128)S(1)}, f32[4,8,256]{2,1,0:T(8,128)S(1)}, bf16[512,8192]{1,0:T(8,128)(2,1)S(1)}, bf16[512,8192]{1,0:T(8,128)(2,1)S(1)}, bf...) custom-call(f32[8,128,4]{2,1,0:T(8,128)S(1)} %get-tuple-element.55.x, ...), custom_call_target="tpu_custom_call", output_to_operand_aliasing={{2}: (9, {}), {3}: (10, {}), {4}: (11, {}), {5}: (12, {})} | custom-call | flops 3221225472 | bytes 16777216 | tf_op jit(solution)/shard_map/inner/pallas_call | solution.py:571
  25.9 3.7 %collective-permute-start.4 = (f32[2,16,256]{2,1,0:T(8,128)S(1)}, f32[2,16,256]{2,1,0:T(8,128)S(1)}, u32[]{:S(2)}, u32[]{:S(2)}) collective-permute-start(f32[2,16,256]{2,1,0:T(8,128)S(1)} %get-tuple-element.75), channel_id=1, source_target_pairs={{0,124},{4,0},{8,4},{12,8},{16,12},{20,16},{24,20},{28,24},{32,28}... | collective-permute-start | bytes 98312 | tf_op jit(solution)/shard_map/ppermute | solution.py:585
  29.6 2.6 %back_0.1 = (bf16[512,8192]{1,0:T(8,128)(2,1)S(1)}, f32[8,128]{1,0:T(8,128)S(1)}) custom-call(bf16[512,512]{1,0:T(8,128)(2,1)S(1)} %get-tuple-element.78.w_mid, bf16[512,8192]{1,0:T(8,128)(2,1)S(1)} %get-tuple-element.79.slope_mid, bf16[512,8192]{1,0:T(8,128)(2,1)S(1)} %get-tuple-element.80.slope_in), custom_call_target="tpu_custom_call", output_to_operand_aliasing={{0}: (2, {})} | custom-call | flops 2147483648 | bytes 12582912 | tf_op jit(solution)/shard_map/back_0/pallas_call | solution.py:571
  32.2 2.9 %collective-permute-done.5.stiff_behind = f32[2,16,256]{2,1,0:T(8,128)S(1)} collective-permute-done((f32[2,16,256]{2,1,0:T(8,128)S(1)}, f32[2,16,256]{2,1,0:T(8,128)S(1)}, u32[]{:S(2)}, u32[]{:S(2)}) %collective-permute-start.5) | collective-permute-done | bytes 32800 | tf_op jit(solution)/shard_map/ppermute | solution.py:585
  35.1 2.7 %krylov.1 = (f32[3,5,16,256]{3,2,1,0:T(8,128)S(1)}, f32[3,5,16,256]{3,2,1,0:T(8,128)S(1)}, f32[8,128]{1,0:T(8,128)S(1)}) custom-call(s32[8]{0:T(128)S(1)} %stack.47.place, f32[4,9,8,256]{3,2,1,0:T(8,128)S(1)} %get-tuple-element.65.loads, f32[40,3,256]{2,1,0:T(4,128)S(1)} %collective-permute-done.2.ahead, f32[40,2,256]{2,1,0:T(2,128)S(1)} %collective-permute-done.3.behind, ...), custom_call_target="tpu_custom_call" | custom-call | tf_op jit(solution)/shard_map/krylov/pallas_call | solution.py:571
  37.7 6.0 %collective-permute-start.6 = (f32[8,128]{1,0:T(8,128)S(1)}, f32[8,128]{1,0:T(8,128)S(1)}, u32[]{:S(2)}, u32[]{:S(2)}) collective-permute-start(f32[8,128]{1,0:T(8,128)S(1)} %get-tuple-element.82), channel_id=1, source_target_pairs={{0,4},{4,0},{1,5},{5,1},{2,6},{6,2},{3,7},{7,3},{8,12},{12,8},{9,1... | collective-permute-start | bytes 12296 | tf_op jit(solution)/shard_map/ppermute | solution.py:589
  44.6 3.9 %collective-permute-start.8 = (f32[8,128]{1,0:T(8,128)S(1)}, f32[8,128]{1,0:T(8,128)S(1)}, u32[]{:S(2)}, u32[]{:S(2)}) collective-permute-start(f32[8,128]{1,0:T(8,128)S(1)} %add.41), channel_id=1, source_target_pairs={{0,2},{1,3},{2,0},{3,1},{4,6},{5,7},{6,4},{7,5},{8,10},{9,11},{10,... | collective-permute-start | bytes 12296 | tf_op jit(solution)/shard_map/ppermute | solution.py:585
  51.0 2.6 %collective-permute-start.12 = (f32[8,128]{1,0:T(8,128)S(1)}, f32[8,128]{1,0:T(8,128)S(1)}, u32[]{:S(2)}, u32[]{:S(2)}) collective-permute-start(f32[8,128]{1,0:T(8,128)S(1)} %add_add_fusion.2), channel_id=1, source_target_pairs={{0,24},{8,0},{16,8},{24,16},{1,25},{9,1},{17,9},{25,17},{2,26},{10... | collective-permute-start | bytes 12296 | tf_op jit(solution)/shard_map/ppermute | solution.py:585
  53.6 1.9 %back_1.1 = (bf16[512,8192]{1,0:T(8,128)(2,1)S(1)}, f32[8,128]{1,0:T(8,128)}) custom-call(bf16[512,512]{1,0:T(8,128)(2,1)S(1)} %get-tuple-element.78.w_mid, bf16[512,8192]{1,0:T(8,128)(2,1)S(1)} %get-tuple-element.79.slope_mid, bf16[512,8192]{1,0:T(8,128)(2,1)S(1)} %get-tuple-element.89.slope_in), custom_call_target="tpu_custom_call", output_to_operand_aliasing={{0}: (2, {})} | custom-call | flops 1073741824 | bytes 6291456 | tf_op jit(solution)/shard_map/back_1/pallas_call | solution.py:571
  55.5 1.7 %collective-permute-start.14 = (f32[8,128]{1,0:T(8,128)S(1)}, f32[8,128]{1,0:T(8,128)S(1)}, u32[]{:S(2)}, u32[]{:S(2)}) collective-permute-start(f32[8,128]{1,0:T(8,128)S(1)} %add_add_fusion.1), channel_id=1, source_target_pairs={{0,64},{32,96},{64,0},{96,32},{1,65},{33,97},{65,1},{97,33},{2,66}... | collective-permute-start | bytes 12296 | tf_op jit(solution)/shard_map/ppermute | solution.py:585
  58.2 1.9 %back_2.1 = (bf16[512,8192]{1,0:T(8,128)(2,1)S(1)}, f32[8,128]{1,0:T(8,128)}) custom-call(bf16[512,512]{1,0:T(8,128)(2,1)S(1)} %get-tuple-element.78.w_mid, bf16[512,8192]{1,0:T(8,128)(2,1)S(1)} %get-tuple-element.79.slope_mid, bf16[512,8192]{1,0:T(8,128)(2,1)S(1)} %get-tuple-element.90.slope_in), custom_call_target="tpu_custom_call", output_to_operand_aliasing={{0}: (2, {})} | custom-call | flops 1073741824 | bytes 6291456 | tf_op jit(solution)/shard_map/back_2/pallas_call | solution.py:571
  60.1 1.4 %energy.1 = (f32[3,4,8,256]{3,2,1,0:T(8,128)}, f32[4,8,256]{2,1,0:T(8,128)S(1)}, f32[4,8,256]{2,1,0:T(8,128)}) custom-call(s32[8]{0:T(128)S(1)} %stack.47.place, f32[8,128]{1,0:T(8,128)S(1)} %add_add_fusion.sums, f32[4,9,8,256]{3,2,1,0:T(8,128)S(1)} %get-tuple-element.65.loads, f32[40,3,256]{2,1,0:T(4,128)S(1)} %collective-permute-done.2.ahead, ...), custom_call_target="tpu_custom_call" | custom-call | tf_op jit(solution)/shard_map/energy/pallas_call | solution.py:571
  61.6 10.4 %gradients.1 = (f32[2,768,128]{2,1,0:T(8,128)S(1)}, f32[2,768,128]{2,1,0:T(8,128)S(1)}, f32[4,128]{1,0:T(4,128)S(1)}) custom-call(s32[8]{0:T(128)S(1)} %stack.47.place, f32[4,8,256]{2,1,0:T(8,128)S(1)} %get-tuple-element.87.slope, f32[8,128,4]{2,1,0:T(8,128)S(1)} %get-tuple-element.55.x_cos, f32[8,128,4]{2,1,0:T(8,128)S(1)} %get-tuple-element.56.x_sin, ...), custom_call_target="tpu_custom_call" | custom-call | tf_op jit(solution)/shard_map/gradients/pallas_call | solution.py:571
  72.0 4.7 %collective-permute-start.16 = (f32[2,768,128]{2,1,0:T(8,128)S(1)}, f32[2,768,128]{2,1,0:T(8,128)S(1)}, u32[]{:S(2)}, u32[]{:S(2)}) collective-permute-start(f32[2,768,128]{2,1,0:T(8,128)S(1)} %get-tuple-element.94), channel_id=1, source_target_pairs={{0,4},{4,0},{1,5},{5,1},{2,6},{6,2},{3,7},{7,3},{8,12},{12,8},{9,1... | collective-permute-start | bytes 2359304 | tf_op jit(solution)/shard_map/ppermute | solution.py:738
  76.6 1.9 %collective-permute-done.16 = f32[2,768,128]{2,1,0:T(8,128)S(1)} collective-permute-done((f32[2,768,128]{2,1,0:T(8,128)S(1)}, f32[2,768,128]{2,1,0:T(8,128)S(1)}, u32[]{:S(2)}, u32[]{:S(2)}) %collective-permute-start.16) | collective-permute-done | bytes 786464 | tf_op jit(solution)/shard_map/ppermute | solution.py:738
  78.6 21.8 %all_to_all.10.parts = f32[64,24,128]{2,1,0:T(8,128)S(1)} all-to-all(f32[64,24,128]{2,1,0:T(8,128)S(1)} %bitcast.9), channel_id=1, replica_groups=mesh['x'=4,'y'=4,'c'=2,'z'=4] {'x','y','z'}, dimensions={0} | all-to-all | bytes 1572864 | tf_op jit(solution)/shard_map/all_to_all | solution.py:739
  101.1 20.8 %all_to_all.11.half = f32[64,32,128]{2,1,0:T(8,128)S(1)} all-to-all(f32[64,32,128]{2,1,0:T(8,128)S(1)} %share.1), channel_id=1, replica_groups=mesh['x'=4,'y'=4,'c'=2,'z'=4] {'x','y','z'}, dimensions={0} | all-to-all | bytes 2097152 | tf_op jit(solution)/shard_map/all_to_all | solution.py:743
  121.9 3.5 %collective-permute-start.17 = (f32[64,32,128]{2,1,0:T(8,128)S(1)}, f32[64,32,128]{2,1,0:T(8,128)S(1)}, u32[]{:S(2)}, u32[]{:S(2)}) collective-permute-start(f32[64,32,128]{2,1,0:T(8,128)S(1)} %all_to_all.11.half), channel_id=1, source_target_pairs={{0,4},{4,0},{1,5},{5,1},{2,6},{6,2},{3,7},{7,3},{8,12},{12,8},{9,1... | collective-permute-start | bytes 3145736 | tf_op jit(solution)/shard_map/ppermute | solution.py:744
  125.3 2.3 %collective-permute-done.17.away = f32[64,32,128]{2,1,0:T(8,128)S(1)} collective-permute-done((f32[64,32,128]{2,1,0:T(8,128)S(1)}, f32[64,32,128]{2,1,0:T(8,128)S(1)}, u32[]{:S(2)}, u32[]{:S(2)}) %collective-permute-start.17) | collective-permute-done | bytes 1048608 | tf_op jit(solution)/shard_map/ppermute | solution.py:744
  127.6 1.8 %finish.1 = (f32[256,512]{1,0:T(8,128)}, f32[512,512]{1,0:T(8,128)}, f32[4,128]{1,0:T(4,128)}) custom-call(s32[8]{0:T(128)S(1)} %stack.47.place, f32[64,32,128]{2,1,0:T(8,128)S(1)} %all_to_all.11.half, f32[64,32,128]{2,1,0:T(8,128)S(1)} %collective-permute-done.17.away), custom_call_target="tpu_custom_call" | custom-call | tf_op jit(solution)/shard_map/finish/pallas_call | solution.py:571
  (33 shorter events, 7.8 us)
Async XLA Ops:
  3.3 10.2 %collective-permute-start = (f32[4,3,8,256]{3,2,1,0:T(8,128)S(1)}, f32[4,3,8,256]{3,2,1,0:T(8,128)S(1)}, u32[]{:S(2)}, u32[]{:S(2)}) collective-permute-start(f32[4,3,8,256]{3,2,1,0:T(8,128)S(1)} %get-tuple-element.53), channel_id=1, source_target_pairs={{0,124},{4,0},{8,4},{12,8},{16,12},{20,16},{24,20},{28,24},{32,28}... | collective-permute-start | bytes 294920 | tf_op jit(solution)/shard_map/ppermute | solution.py:585
  4.8 8.7 %collective-permute-start.1 = (f32[4,2,8,256]{3,2,1,0:T(8,128)S(1)}, f32[4,2,8,256]{3,2,1,0:T(8,128)S(1)}, u32[]{:S(2)}, u32[]{:S(2)}) collective-permute-start(f32[4,2,8,256]{3,2,1,0:T(8,128)S(1)} %get-tuple-element.54), channel_id=1, source_target_pairs={{0,4},{4,8},{8,12},{12,16},{16,20},{20,24},{24,28},{28,32},{32,36}... | collective-permute-start | bytes 196616 | tf_op jit(solution)/shard_map/ppermute | solution.py:585
  14.1 11.2 %collective-permute-start.2 = (f32[40,3,256]{2,1,0:T(4,128)S(1)}, f32[40,3,256]{2,1,0:T(4,128)S(1)}, u32[]{:S(2)}, u32[]{:S(2)}) collective-permute-start(f32[40,3,256]{2,1,0:T(4,128)S(1)} %get-tuple-element.66), channel_id=1, source_target_pairs={{0,3},{1,0},{2,1},{3,2},{4,7},{5,4},{6,5},{7,6},{8,11},{9,8},{10,9... | collective-permute-start | bytes 368648 | tf_op jit(solution)/shard_map/ppermute | solution.py:585
  17.9 7.3 %collective-permute-start.3 = (f32[40,2,256]{2,1,0:T(2,128)S(1)}, f32[40,2,256]{2,1,0:T(2,128)S(1)}, u32[]{:S(2)}, u32[]{:S(2)}) collective-permute-start(f32[40,2,256]{2,1,0:T(2,128)S(1)} %get-tuple-element.67), channel_id=1, source_target_pairs={{0,1},{1,2},{2,3},{3,0},{4,5},{5,6},{6,7},{7,4},{8,9},{9,10},{10,1... | collective-permute-start | bytes 245768 | tf_op jit(solution)/shard_map/ppermute | solution.py:585
  25.9 6.3 %collective-permute-start.4 = (f32[2,16,256]{2,1,0:T(8,128)S(1)}, f32[2,16,256]{2,1,0:T(8,128)S(1)}, u32[]{:S(2)}, u32[]{:S(2)}) collective-permute-start(f32[2,16,256]{2,1,0:T(8,128)S(1)} %get-tuple-element.75), channel_id=1, source_target_pairs={{0,124},{4,0},{8,4},{12,8},{16,12},{20,16},{24,20},{28,24},{32,28}... | collective-permute-start | bytes 98312 | tf_op jit(solution)/shard_map/ppermute | solution.py:585
  29.6 5.5 %collective-permute-start.5 = (f32[2,16,256]{2,1,0:T(8,128)S(1)}, f32[2,16,256]{2,1,0:T(8,128)S(1)}, u32[]{:S(2)}, u32[]{:S(2)}) collective-permute-start(f32[2,16,256]{2,1,0:T(8,128)S(1)} %get-tuple-element.76), channel_id=1, source_target_pairs={{0,4},{4,8},{8,12},{12,16},{16,20},{20,24},{24,28},{28,32},{32,36}... | collective-permute-start | bytes 98312 | tf_op jit(solution)/shard_map/ppermute | solution.py:585
  37.7 6.8 %collective-permute-start.6 = (f32[8,128]{1,0:T(8,128)S(1)}, f32[8,128]{1,0:T(8,128)S(1)}, u32[]{:S(2)}, u32[]{:S(2)}) collective-permute-start(f32[8,128]{1,0:T(8,128)S(1)} %get-tuple-element.82), channel_id=1, source_target_pairs={{0,4},{4,0},{1,5},{5,1},{2,6},{6,2},{3,7},{7,3},{8,12},{12,8},{9,1... | collective-permute-start | bytes 12296 | tf_op jit(solution)/shard_map/ppermute | solution.py:589
  44.6 3.9 %collective-permute-start.7 = (f32[8,128]{1,0:T(8,128)S(1)}, f32[8,128]{1,0:T(8,128)S(1)}, u32[]{:S(2)}, u32[]{:S(2)}) collective-permute-start(f32[8,128]{1,0:T(8,128)S(1)} %add.41), channel_id=1, source_target_pairs={{0,1},{1,2},{2,3},{3,0},{4,5},{5,6},{6,7},{7,4},{8,9},{9,10},{10,1... | collective-permute-start | bytes 12296 | tf_op jit(solution)/shard_map/ppermute | solution.py:585
  44.6 4.9 %collective-permute-start.8 = (f32[8,128]{1,0:T(8,128)S(1)}, f32[8,128]{1,0:T(8,128)S(1)}, u32[]{:S(2)}, u32[]{:S(2)}) collective-permute-start(f32[8,128]{1,0:T(8,128)S(1)} %add.41), channel_id=1, source_target_pairs={{0,2},{1,3},{2,0},{3,1},{4,6},{5,7},{6,4},{7,5},{8,10},{9,11},{10,... | collective-permute-start | bytes 12296 | tf_op jit(solution)/shard_map/ppermute | solution.py:585
  48.4 2.5 %collective-permute-start.9 = (f32[8,128]{1,0:T(8,128)S(1)}, f32[8,128]{1,0:T(8,128)S(1)}, u32[]{:S(2)}, u32[]{:S(2)}) collective-permute-start(f32[8,128]{1,0:T(8,128)S(1)} %add.41), channel_id=1, source_target_pairs={{0,3},{1,0},{2,1},{3,2},{4,7},{5,4},{6,5},{7,6},{8,11},{9,8},{10,9... | collective-permute-start | bytes 12296 | tf_op jit(solution)/shard_map/ppermute | solution.py:585
  50.9 4.6 %collective-permute-start.10 = (f32[8,128]{1,0:T(8,128)S(1)}, f32[8,128]{1,0:T(8,128)S(1)}, u32[]{:S(2)}, u32[]{:S(2)}) collective-permute-start(f32[8,128]{1,0:T(8,128)S(1)} %add_add_fusion.2), channel_id=1, source_target_pairs={{0,8},{8,16},{16,24},{24,0},{1,9},{9,17},{17,25},{25,1},{2,10},{10... | collective-permute-start | bytes 12296 | tf_op jit(solution)/shard_map/ppermute | solution.py:585
  50.9 4.6 %collective-permute-start.11 = (f32[8,128]{1,0:T(8,128)S(1)}, f32[8,128]{1,0:T(8,128)S(1)}, u32[]{:S(2)}, u32[]{:S(2)}) collective-permute-start(f32[8,128]{1,0:T(8,128)S(1)} %add_add_fusion.2), channel_id=1, source_target_pairs={{0,16},{8,24},{16,0},{24,8},{1,17},{9,25},{17,1},{25,9},{2,18},{10... | collective-permute-start | bytes 12296 | tf_op jit(solution)/shard_map/ppermute | solution.py:585
  51.0 4.5 %collective-permute-start.12 = (f32[8,128]{1,0:T(8,128)S(1)}, f32[8,128]{1,0:T(8,128)S(1)}, u32[]{:S(2)}, u32[]{:S(2)}) collective-permute-start(f32[8,128]{1,0:T(8,128)S(1)} %add_add_fusion.2), channel_id=1, source_target_pairs={{0,24},{8,0},{16,8},{24,16},{1,25},{9,1},{17,9},{25,17},{2,26},{10... | collective-permute-start | bytes 12296 | tf_op jit(solution)/shard_map/ppermute | solution.py:585
  55.5 4.6 %collective-permute-start.13 = (f32[8,128]{1,0:T(8,128)S(1)}, f32[8,128]{1,0:T(8,128)S(1)}, u32[]{:S(2)}, u32[]{:S(2)}) collective-permute-start(f32[8,128]{1,0:T(8,128)S(1)} %add_add_fusion.1), channel_id=1, source_target_pairs={{0,32},{32,64},{64,96},{96,0},{1,33},{33,65},{65,97},{97,1},{2,34}... | collective-permute-start | bytes 12296 | tf_op jit(solution)/shard_map/ppermute | solution.py:585
  55.5 4.6 %collective-permute-start.14 = (f32[8,128]{1,0:T(8,128)S(1)}, f32[8,128]{1,0:T(8,128)S(1)}, u32[]{:S(2)}, u32[]{:S(2)}) collective-permute-start(f32[8,128]{1,0:T(8,128)S(1)} %add_add_fusion.1), channel_id=1, source_target_pairs={{0,64},{32,96},{64,0},{96,32},{1,65},{33,97},{65,1},{97,33},{2,66}... | collective-permute-start | bytes 12296 | tf_op jit(solution)/shard_map/ppermute | solution.py:585
  57.2 2.9 %collective-permute-start.15 = (f32[8,128]{1,0:T(8,128)S(1)}, f32[8,128]{1,0:T(8,128)S(1)}, u32[]{:S(2)}, u32[]{:S(2)}) collective-permute-start(f32[8,128]{1,0:T(8,128)S(1)} %add_add_fusion.1), channel_id=1, source_target_pairs={{0,96},{32,0},{64,32},{96,64},{1,97},{33,1},{65,33},{97,65},{2,98}... | collective-permute-start | bytes 12296 | tf_op jit(solution)/shard_map/ppermute | solution.py:585
  72.0 6.6 %collective-permute-start.16 = (f32[2,768,128]{2,1,0:T(8,128)S(1)}, f32[2,768,128]{2,1,0:T(8,128)S(1)}, u32[]{:S(2)}, u32[]{:S(2)}) collective-permute-start(f32[2,768,128]{2,1,0:T(8,128)S(1)} %get-tuple-element.94), channel_id=1, source_target_pairs={{0,4},{4,0},{1,5},{5,1},{2,6},{6,2},{3,7},{7,3},{8,12},{12,8},{9,1... | collective-permute-start | bytes 2359304 | tf_op jit(solution)/shard_map/ppermute | solution.py:738
  121.9 5.7 %collective-permute-start.17 = (f32[64,32,128]{2,1,0:T(8,128)S(1)}, f32[64,32,128]{2,1,0:T(8,128)S(1)}, u32[]{:S(2)}, u32[]{:S(2)}) collective-permute-start(f32[64,32,128]{2,1,0:T(8,128)S(1)} %all_to_all.11.half), channel_id=1, source_target_pairs={{0,4},{4,0},{1,5},{5,1},{2,6},{6,2},{3,7},{7,3},{8,12},{12,8},{9,1... | collective-permute-start | bytes 3145736 | tf_op jit(solution)/shard_map/ppermute | solution.py:744

commit v2 on v1

--- a/solution.py
+++ b/solution.py
@@ -173,22 +173,15 @@
     return jnp.concatenate([block, ahead * stop, zeros, behind * start], axis=0)
 
 
-def load_plane(place, loads, ahead, behind, d, p):
-    slot = d * loads.shape[1] + p
-    return with_rows(place, loads[d, p], ahead[slot], behind[slot])
-
-
-def krylov_kernel(place, loads, ahead, behind, stiff, stiff_ahead, stiff_behind, density,
-                  ready, first, second, sums):
-    planes = loads.shape[1]
-    cells = planes - 5
+def krylov_kernel(place, loads, stiff, ahead, behind, density, ready, first, second, sums):
+    cells = loads.shape[1]
     low, high = kept_if(place[SLAB_FIRST]), kept_if(place[SLAB_LAST])
-    stiff_planes = [stiff_behind[p] * low for p in range(2)]
+    stiff_planes = [behind[8 + p] * low for p in range(2)]
     stiff_planes += [stiff[p] for p in range(cells)]
-    stiff_planes += [stiff_ahead[p] * high for p in range(2)]
-    loaded = [
-        [load_plane(place, loads, ahead, behind, d, p) for d in range(4)] for p in range(planes)
-    ]
+    stiff_planes += [ahead[12 + p] * high for p in range(2)]
+    loaded = [[behind[2 * d + p] * low for d in range(4)] for p in range(2)]
+    loaded += [[loads[d, p] for d in range(4)] for p in range(cells)]
+    loaded += [[ahead[3 * d + p] * high for d in range(4)] for p in range(3)]
     force = [plane[:3] for plane in loaded]
     free = [plane[3] for plane in loaded]
     image = operator_planes(force, stiff_planes, free[1:-1])
@@ -269,7 +262,7 @@
 
 
 def energy_kernel(
-    elements, place, sums, loads, ahead, behind, first, second, density, solution, slope, out
+    elements, place, sums, loads, ahead, first, second, density, solution, slope, out
 ):
     rows_of = [sums[k : k + 1, :] for k in range(2 * ITERS + 1)]
     factors, compliance = krylov_steps(rows_of[: 2 * ITERS])
@@ -278,11 +271,12 @@
     scale = -3.0 * (1.0 - emin) / compliance
     wide = [jnp.concatenate([value, value], axis=1) for value in factors + [scale, constant]]
     cells, rows, _ = density.shape
+    high = kept_if(place[SLAB_LAST])
     modes = []
     for p in range(cells + 1):
         plane = []
         for d in range(3):
-            load = load_plane(place, loads, ahead, behind, d, 2 + p)
+            load = loads[d, p] if p < cells else ahead[3 * d] * high
             value = wide[0] * load + wide[1] * first[d, p] + wide[2] * second[d, p]
             if p < cells:
                 solution[d, p] = value[:rows]
@@ -304,17 +298,13 @@
 
 def prepare_kernel(
     grid_cells, place, load_values, load_mask, fixed_mask, frequencies, w_in, w_mid, w_out,
-    loads, loads_first, loads_last, x_cos, x_sin, z_cos, z_sin, w_in_t, w_mid_t, w_mid_half,
-    w_column, w_row,
+    loads, x_cos, x_sin, z_cos, z_sin, w_in_t, w_mid_t, w_mid_half, w_column, w_row,
 ):
     cells, rows, size = load_mask.shape
     free = (1 - fixed_mask[...]).astype(F32)
     held = free * load_mask[...].astype(F32)
     for d in range(4):
-        field = free if d == 3 else held * load_values[d]
-        loads[d] = field
-        loads_first[d] = field[:3]
-        loads_last[d] = field[cells - 2 :]
+        loads[d] = free if d == 3 else held * load_values[d]
     columns = [column_of(frequencies[k : k + 1, :]) for k in range(3)]
     half = rows // 2
     lanes = 2 * cells * half
@@ -343,38 +333,25 @@
     w_row[...] = jnp.broadcast_to(line, w_row.shape).astype(BF)
 
 
-def pack_kernel(place, loads, loads_ahead, loads_behind, stiff_first, stiff_last,
-                planes, to_before, to_next):
-    low, high = kept_if(place[SLAB_FIRST]), kept_if(place[SLAB_LAST])
-    cells, rows = loads.shape[1:3]
-    count = planes.shape[1]
+def join_kernel(place, loads, stiff, ahead, behind, loads_16, stiff_16, to_before, to_next):
+    cells = stiff.shape[0]
     for d in range(4):
-        for p in range(count):
-            if p < 2:
-                block = loads_behind[d, p] * low
-            elif p < 2 + cells:
-                block = loads[d, p - 2]
-            else:
-                block = loads_ahead[d, p - 2 - cells] * high
-            planes[d, p] = block
-            to_before[d * count + p] = block[:3]
-            to_next[d * count + p] = block[rows - 2 :]
+        for p in range(cells):
+            slot = d * cells + p
+            block = with_rows(place, loads[d, p], ahead[slot], behind[slot])
+            loads_16[d, p] = block
+            if p < 3:
+                to_before[3 * d + p] = block
+            if p >= cells - 2:
+                to_next[2 * d + p - (cells - 2)] = block
     for p in range(cells):
-        to_before[4 * count + p, :2, :] = stiff_first[p]
-        to_before[4 * count + p, 2:, :] = stiff_first[p, 1:]
-        to_next[4 * count + p] = stiff_last[p]
-
-
-def stiff_rows_kernel(place, stiff, ahead, behind, joined, to_before, to_next):
-    cells = stiff.shape[0]
-    first = ahead.shape[0] - cells
-    for p in range(cells):
-        block = with_rows(place, stiff[p], ahead[first + p, :2, :], behind[first + p])
-        joined[p] = block
-        if p < to_before.shape[0]:
-            to_before[p] = block
-        if p >= cells - to_next.shape[0]:
-            to_next[p - (cells - to_next.shape[0])] = block
+        slot = 4 * cells + p
+        block = with_rows(place, stiff[p], ahead[slot, :2, :], behind[slot])
+        stiff_16[p] = block
+        if p < 2:
+            to_before[12 + p] = block
+        if p >= cells - 2:
+            to_next[8 + p - (cells - 2)] = block
 
 
 def gated(half):
@@ -421,8 +398,8 @@
 
 
 def outer_kernel(
-    x_cos, x_sin, z_cos, z_sin, w_in, w_mid, w_column, w_row,
-    density, stiff_first, stiff_last, *kept,
+    x_cos, x_sin, z_cos, z_sin, w_in, w_mid, w_column, w_row, loads,
+    density, to_before, to_next, *kept,
 ):
     tables, weights = (x_cos, x_sin, z_cos, z_sin), (w_in, w_mid, w_column, w_row)
     cells, _, size = density.shape
@@ -435,7 +412,13 @@
         for q in range(4):
             part = line[:, q * size : (q + 1) * size]
             density[p, q : q + 1, :] = part
-            (stiff_first if q < 2 else stiff_last)[p, q % 2 : q % 2 + 1, :] = stiffness_of(part)
+            target = to_before if q < 2 else to_next
+            target[4 * cells + p, q % 2 : q % 2 + 1, :] = stiffness_of(part)
+        to_before[4 * cells + p, 2:, :] = jnp.zeros((1, size), F32)
+        rows = loads.shape[2]
+        for d in range(4):
+            to_before[d * cells + p] = loads[d, p, :3, :]
+            to_next[d * cells + p] = loads[d, p, rows - 2 :, :]
 
 
 def inner_kernel(
@@ -610,15 +593,13 @@
     table = held(2 * cells_x, inputs // 2, half_rows)
     line = held(inputs // 2, cells_z)
     (
-        loads, loads_first, loads_last, x_cos, x_sin, z_cos, z_sin,
+        loads, x_cos, x_sin, z_cos, z_sin,
         w_in_t, w_mid_t, w_mid_half, w_column, w_row,
     ) = run(
         functools.partial(prepare_kernel, grid_cells),
         "prepare",
         [
             held(4, *field),
-            held(4, 3, cells_y, cells_z),
-            held(4, 2, cells_y, cells_z),
             table,
             table,
             line,
@@ -633,8 +614,6 @@
         weight_out, space=pltpu.HBM,
     )
 
-    loads_ahead = shifted(loads_first, SLAB, -1)
-    loads_behind = shifted(loads_last, SLAB, 1)
     network = (x_cos, x_sin, z_cos, z_sin, w_in_t, w_mid_t, w_column, w_row)
     kept = [held(hidden, rows, dtype=BF)] * 4
     cost = pl.CostEstimate(
@@ -642,22 +621,16 @@
         bytes_accessed=4 * hidden * rows,
         transcendentals=hidden * rows,
     )
-    outer, stiff_first, stiff_last, *stored = run(
+    slots = 5 * cells_x
+    outer, rows_first, rows_last, *stored = run(
         outer_kernel,
         "outer",
-        [held(cells_x, half_rows, cells_z)] + [held(cells_x, 2, cells_z)] * 2 + kept,
+        [held(cells_x, half_rows, cells_z), held(slots, 3, cells_z), held(slots, 2, cells_z)] + kept,
         *network,
+        loads,
         scalars=0,
         limit=16,
         cost_estimate=cost,
-    )
-    planes = cells_x + 5
-    slots = 4 * planes + cells_x
-    loads, rows_first, rows_last = run(
-        pack_kernel,
-        "pack",
-        [held(4, planes, cells_y, cells_z), held(slots, 3, cells_z), held(slots, 2, cells_z)],
-        place, loads, loads_ahead, loads_behind, stiff_first, stiff_last,
     )
     rows_ahead = shifted(rows_first, "z", -1)
     rows_behind = shifted(rows_last, "z", 1)
@@ -674,14 +647,15 @@
         cost_estimate=cost,
     )
     hidden_in, slope_mid, slope_in, hidden_mid = stored
-    stiff_16, stiff_before, stiff_next = run(
-        stiff_rows_kernel,
-        "stiff_rows",
-        [held(cells_x, ROWS, cells_z), held(2, ROWS, cells_z), held(2, ROWS, cells_z)],
-        place, stiff, rows_ahead, rows_behind,
-    )
-    stiff_ahead = shifted(stiff_before, SLAB, -1)
-    stiff_behind = shifted(stiff_next, SLAB, 1)
+    loads, stiff, planes_first, planes_last = run(
+        join_kernel,
+        "join",
+        [held(4, cells_x, ROWS, cells_z), held(cells_x, ROWS, cells_z)]
+        + [held(14, ROWS, cells_z), held(10, ROWS, cells_z)],
+        place, loads, stiff, rows_ahead, rows_behind,
+    )
+    planes_ahead = shifted(planes_first, SLAB, -1)
+    planes_behind = shifted(planes_last, SLAB, 1)
 
     back = slope_in
     ready = []
@@ -712,14 +686,13 @@
         krylov_kernel,
         "krylov",
         [vector, vector, held(8, 128)],
-        place, loads, rows_ahead, rows_behind, stiff_16, stiff_ahead, stiff_behind, density,
-        ready[0],
+        place, loads, stiff, planes_ahead, planes_behind, density, ready[0],
     )
     solution, slope, density = run(
         functools.partial(energy_kernel, elements_total),
         "energy",
         [shaped(3, *field), held(*field), shaped(*field)],
-        place, summed(sums), loads, rows_ahead, rows_behind, first, second, density,
+        place, summed(sums), loads, planes_ahead, first, second, density,
     )
 
     height = hidden + inputs

time: 130 us -> 125 us (0.962)
  starting transfers between devices: 33.8 us -> 27.6 us
  waiting for transfers between devices: 10.4 us -> 12.7 us
    ppermute x15 -> x13, starting transfers between devices: 19.7 us -> 12.3 us  [shifted(): lax.ppermute(block, axis, [(i, (i + distance) % size) for i in range(size)])]
    ppermute x15 -> x13, waiting for transfers between devices: 5.37 us -> 7.7 us  [shifted(): lax.ppermute(block, axis, [(i, (i + distance) % size) for i in range(size)])]
    pallas_call x13 -> x12, Pallas kernels: 41.7 us -> 41.3 us  [run(): pl.pallas_call(kernel, name=name, in_specs=[SCALARS] * scalars + [WHOLE]...]
  transfers between devices with their start and end apart: 18 -> 16, of which waited for: 6 -> 10; matrix products, arithmetic and copies ran while one was open for 0% -> 0% of each run, Pallas kernels for 16% -> 11%
where the time goes in v2:
time: 125 us; the launch traced here: 124 us
  blocking collectives  41.8 us (33%)
  Pallas kernels  41.3 us (33%)
  starting transfers between devices  27.6 us (22%)
  waiting for transfers between devices  12.7 us (10%)
    pallas_call x12, Pallas kernels, run(): pl.pallas_call(kernel, name=name, in_specs=[SCALARS] * scalars + [WHOLE]...  41.3 us
    all_to_all x1, blocking collectives, on_device(): parts = lax.all_to_all(half, CHIPS, 0, 0)  21 us
    all_to_all x1, blocking collectives, on_device(): half = lax.all_to_all(shares, CHIPS, 0, 0)  20.8 us
    ppermute x13, starting transfers between devices, shifted(): lax.ppermute(block, axis, [(i, (i + distance) % size) for i in range(size)])  12.3 us
    ppermute x13, waiting for transfers between devices, shifted(): lax.ppermute(block, axis, [(i, (i + distance) % size) for i in range(size)])  7.7 us
    ppermute x1, starting transfers between devices, summed(): values = values + lax.ppermute(values, 'c', [(0, 1), (1, 0)])  7.19 us
    ppermute x1, starting transfers between devices, on_device(): half = (mine + lax.ppermute(other, 'c', swap)).reshape(chips, -1, 128)  4.69 us
    ppermute x1, starting transfers between devices, on_device(): away = lax.ppermute(half, 'c', swap)  3.45 us
  transfers between devices with their start and end apart: 16, of which 10 were waited for; matrix products, arithmetic and copies ran while one was open for 0% of the time, Pallas kernels for 11%

profile of v2, /device:TPU:1, one launch (start us, length us, event | category | flops | bytes accessed | tf_op | source)
XLA Modules:
  0.0 124.4 jit_solution(11110186595265774560)
XLA Ops:
  0.7 2.6 %prepare.1 = (f32[4,4,8,256]{3,2,1,0:T(8,128)S(1)}, f32[8,128,4]{2,1,0:T(8,128)S(1)}, f32[8,128,4]{2,1,0:T(8,128)S(1)}, f32[128,256]{1,0:T(8,128)S(1)}, f32[128,...) custom-call(s32[8]{0:T(128)S(1)} %stack.47.place, ...), custom_call_target="tpu_custom_call" | custom-call | tf_op jit(solution)/shard_map/prepare/pallas_call | solution.py:554
  3.3 7.3 %outer.1 = (f32[4,4,256]{2,1,0:T(4,128)S(1)}, f32[20,3,256]{2,1,0:T(4,128)S(1)}, f32[20,2,256]{2,1,0:T(2,128)S(1)}, bf16[512,8192]{1,0:T(8,128)(2,1)S(1)}, bf16[...) custom-call(f32[8,128,4]{2,1,0:T(8,128)S(1)} %get-tuple-element.49.x_cos, ...), custom_call_target="tpu_custom_call" | custom-call | flops 3221225472 | bytes 16777216 | tf_op jit(solution)/shard_map/outer/pallas_call | solution.py:554
  10.7 2.5 %collective-permute-start.1 = (f32[20,2,256]{2,1,0:T(2,128)S(1)}, f32[20,2,256]{2,1,0:T(2,128)S(1)}, u32[]{:S(2)}, u32[]{:S(2)}) collective-permute-start(f32[20,2,256]{2,1,0:T(2,128)S(1)} %get-tuple-element.64), channel_id=1, source_target_pairs={{0,1},{1,2},{2,3},{3,0},{4,5},{5,6},{6,7},{7,4},{8,9},{9,10},{10,1... | collective-permute-start | bytes 122888 | tf_op jit(solution)/shard_map/ppermute | solution.py:568
  13.2 2.2 %collective-permute-start = (f32[20,3,256]{2,1,0:T(4,128)S(1)}, f32[20,3,256]{2,1,0:T(4,128)S(1)}, u32[]{:S(2)}, u32[]{:S(2)}) collective-permute-start(f32[20,3,256]{2,1,0:T(4,128)S(1)} %get-tuple-element.63), channel_id=1, source_target_pairs={{0,3},{1,0},{2,1},{3,2},{4,7},{5,4},{6,5},{7,6},{8,11},{9,8},{10,9... | collective-permute-start | bytes 184328 | tf_op jit(solution)/shard_map/ppermute | solution.py:568
  15.4 7.3 %inner.1 = (f32[4,8,256]{2,1,0:T(8,128)S(1)}, f32[4,8,256]{2,1,0:T(8,128)S(1)}, bf16[512,8192]{1,0:T(8,128)(2,1)S(1)}, bf16[512,8192]{1,0:T(8,128)(2,1)S(1)}, bf...) custom-call(f32[8,128,4]{2,1,0:T(8,128)S(1)} %get-tuple-element.49.x, ...), custom_call_target="tpu_custom_call", output_to_operand_aliasing={{2}: (9, {}), {3}: (10, {}), {4}: (11, {}), {5}: (12, {})} | custom-call | flops 3221225472 | bytes 16777216 | tf_op jit(solution)/shard_map/inner/pallas_call | solution.py:554
  25.7 2.6 %back_0.1 = (bf16[512,8192]{1,0:T(8,128)(2,1)S(1)}, f32[8,128]{1,0:T(8,128)S(1)}) custom-call(bf16[512,512]{1,0:T(8,128)(2,1)S(1)} %get-tuple-element.70.w_mid, bf16[512,8192]{1,0:T(8,128)(2,1)S(1)} %get-tuple-element.71.slope_mid, bf16[512,8192]{1,0:T(8,128)(2,1)S(1)} %get-tuple-element.72.slope_in), custom_call_target="tpu_custom_call", output_to_operand_aliasing={{0}: (2, {})} | custom-call | flops 2147483648 | bytes 12582912 | tf_op jit(solution)/shard_map/back_0/pallas_call | solution.py:554
  28.2 1.4 %collective-permute-done.3.behind = f32[10,16,256]{2,1,0:T(8,128)S(1)} collective-permute-done((f32[10,16,256]{2,1,0:T(8,128)S(1)}, f32[10,16,256]{2,1,0:T(8,128)S(1)}, u32[]{:S(2)}, u32[]{:S(2)}) %collective-permute-start.3) | collective-permute-done | bytes 163872 | tf_op jit(solution)/shard_map/ppermute | solution.py:568
  29.7 2.7 %krylov.1 = (f32[3,5,16,256]{3,2,1,0:T(8,128)S(1)}, f32[3,5,16,256]{3,2,1,0:T(8,128)S(1)}, f32[8,128]{1,0:T(8,128)S(1)}) custom-call(s32[8]{0:T(128)S(1)} %stack.47.place, f32[4,4,16,256]{3,2,1,0:T(8,128)S(1)} %get-tuple-element.65.loads, f32[4,16,256]{2,1,0:T(8,128)S(1)} %get-tuple-element.66.stiff, f32[14,16,256]{2,1,0:T(8,128)S(1)} %collective-permute-done.2.ahead, ...), custom_call_target="tpu_custom_call" | custom-call | tf_op jit(solution)/shard_map/krylov/pallas_call | solution.py:554
  32.3 7.2 %collective-permute-start.4 = (f32[8,128]{1,0:T(8,128)S(1)}, f32[8,128]{1,0:T(8,128)S(1)}, u32[]{:S(2)}, u32[]{:S(2)}) collective-permute-start(f32[8,128]{1,0:T(8,128)S(1)} %get-tuple-element.74), channel_id=1, source_target_pairs={{0,4},{4,0},{1,5},{5,1},{2,6},{6,2},{3,7},{7,3},{8,12},{12,8},{9,1... | collective-permute-start | bytes 12296 | tf_op jit(solution)/shard_map/ppermute | solution.py:572
  40.3 1.4 %collective-permute-start.7 = (f32[8,128]{1,0:T(8,128)S(1)}, f32[8,128]{1,0:T(8,128)S(1)}, u32[]{:S(2)}, u32[]{:S(2)}) collective-permute-start(f32[8,128]{1,0:T(8,128)S(1)} %add.41), channel_id=1, source_target_pairs={{0,3},{1,0},{2,1},{3,2},{4,7},{5,4},{6,5},{7,6},{8,11},{9,8},{10,9... | collective-permute-start | bytes 12296 | tf_op jit(solution)/shard_map/ppermute | solution.py:568
  42.8 2.9 %collective-permute-done.6 = f32[8,128]{1,0:T(8,128)S(1)} collective-permute-done((f32[8,128]{1,0:T(8,128)S(1)}, f32[8,128]{1,0:T(8,128)S(1)}, u32[]{:S(2)}, u32[]{:S(2)}) %collective-permute-start.6) | collective-permute-done | bytes 4128 | tf_op jit(solution)/shard_map/ppermute | solution.py:568
  46.1 1.4 %collective-permute-start.8 = (f32[8,128]{1,0:T(8,128)S(1)}, f32[8,128]{1,0:T(8,128)S(1)}, u32[]{:S(2)}, u32[]{:S(2)}) collective-permute-start(f32[8,128]{1,0:T(8,128)S(1)} %add_add_fusion.2), channel_id=1, source_target_pairs={{0,8},{8,16},{16,24},{24,0},{1,9},{9,17},{17,25},{25,1},{2,10},{10... | collective-permute-start | bytes 12296 | tf_op jit(solution)/shard_map/ppermute | solution.py:568
  47.4 1.9 %back_1.1 = (bf16[512,8192]{1,0:T(8,128)(2,1)S(1)}, f32[8,128]{1,0:T(8,128)}) custom-call(bf16[512,512]{1,0:T(8,128)(2,1)S(1)} %get-tuple-element.70.w_mid, bf16[512,8192]{1,0:T(8,128)(2,1)S(1)} %get-tuple-element.71.slope_mid, bf16[512,8192]{1,0:T(8,128)(2,1)S(1)} %get-tuple-element.81.slope_in), custom_call_target="tpu_custom_call", output_to_operand_aliasing={{0}: (2, {})} | custom-call | flops 1073741824 | bytes 6291456 | tf_op jit(solution)/shard_map/back_1/pallas_call | solution.py:554
  50.9 1.4 %collective-permute-start.11 = (f32[8,128]{1,0:T(8,128)S(1)}, f32[8,128]{1,0:T(8,128)S(1)}, u32[]{:S(2)}, u32[]{:S(2)}) collective-permute-start(f32[8,128]{1,0:T(8,128)S(1)} %add_add_fusion.1), channel_id=1, source_target_pairs={{0,32},{32,64},{64,96},{96,0},{1,33},{33,65},{65,97},{97,1},{2,34}... | collective-permute-start | bytes 12296 | tf_op jit(solution)/shard_map/ppermute | solution.py:568
  52.3 1.9 %back_2.1 = (bf16[512,8192]{1,0:T(8,128)(2,1)S(1)}, f32[8,128]{1,0:T(8,128)}) custom-call(bf16[512,512]{1,0:T(8,128)(2,1)S(1)} %get-tuple-element.70.w_mid, bf16[512,8192]{1,0:T(8,128)(2,1)S(1)} %get-tuple-element.71.slope_mid, bf16[512,8192]{1,0:T(8,128)(2,1)S(1)} %get-tuple-element.82.slope_in), custom_call_target="tpu_custom_call", output_to_operand_aliasing={{0}: (2, {})} | custom-call | flops 1073741824 | bytes 6291456 | tf_op jit(solution)/shard_map/back_2/pallas_call | solution.py:554
  55.7 1.4 %energy.1 = (f32[3,4,8,256]{3,2,1,0:T(8,128)}, f32[4,8,256]{2,1,0:T(8,128)S(1)}, f32[4,8,256]{2,1,0:T(8,128)}) custom-call(s32[8]{0:T(128)S(1)} %stack.47.place, f32[8,128]{1,0:T(8,128)S(1)} %add_add_fusion.sums, f32[4,4,16,256]{3,2,1,0:T(8,128)S(1)} %get-tuple-element.65.loads, f32[14,16,256]{2,1,0:T(8,128)S(1)} %collective-permute-done.2.ahead, ...), custom_call_target="tpu_custom_call" | custom-call | tf_op jit(solution)/shard_map/energy/pallas_call | solution.py:554
  57.1 10.5 %gradients.1 = (f32[2,768,128]{2,1,0:T(8,128)S(1)}, f32[2,768,128]{2,1,0:T(8,128)S(1)}, f32[4,128]{1,0:T(4,128)S(1)}) custom-call(s32[8]{0:T(128)S(1)} %stack.47.place, f32[4,8,256]{2,1,0:T(8,128)S(1)} %get-tuple-element.79.slope, f32[8,128,4]{2,1,0:T(8,128)S(1)} %get-tuple-element.49.x_cos, f32[8,128,4]{2,1,0:T(8,128)S(1)} %get-tuple-element.50.x_sin, ...), custom_call_target="tpu_custom_call" | custom-call | tf_op jit(solution)/shard_map/gradients/pallas_call | solution.py:554
  67.6 4.7 %collective-permute-start.14 = (f32[2,768,128]{2,1,0:T(8,128)S(1)}, f32[2,768,128]{2,1,0:T(8,128)S(1)}, u32[]{:S(2)}, u32[]{:S(2)}) collective-permute-start(f32[2,768,128]{2,1,0:T(8,128)S(1)} %get-tuple-element.86), channel_id=1, source_target_pairs={{0,4},{4,0},{1,5},{5,1},{2,6},{6,2},{3,7},{7,3},{8,12},{12,8},{9,1... | collective-permute-start | bytes 2359304 | tf_op jit(solution)/shard_map/ppermute | solution.py:711
  72.3 1.9 %collective-permute-done.14 = f32[2,768,128]{2,1,0:T(8,128)S(1)} collective-permute-done((f32[2,768,128]{2,1,0:T(8,128)S(1)}, f32[2,768,128]{2,1,0:T(8,128)S(1)}, u32[]{:S(2)}, u32[]{:S(2)}) %collective-permute-start.14) | collective-permute-done | bytes 786464 | tf_op jit(solution)/shard_map/ppermute | solution.py:711
  74.3 21.0 %all_to_all.10.parts = f32[64,24,128]{2,1,0:T(8,128)S(1)} all-to-all(f32[64,24,128]{2,1,0:T(8,128)S(1)} %bitcast.9), channel_id=1, replica_groups=mesh['x'=4,'y'=4,'c'=2,'z'=4] {'x','y','z'}, dimensions={0} | all-to-all | bytes 1572864 | tf_op jit(solution)/shard_map/all_to_all | solution.py:712
  96.1 20.8 %all_to_all.11.half = f32[64,32,128]{2,1,0:T(8,128)S(1)} all-to-all(f32[64,32,128]{2,1,0:T(8,128)S(1)} %share.1), channel_id=1, replica_groups=mesh['x'=4,'y'=4,'c'=2,'z'=4] {'x','y','z'}, dimensions={0} | all-to-all | bytes 2097152 | tf_op jit(solution)/shard_map/all_to_all | solution.py:716
  116.9 3.5 %collective-permute-start.15 = (f32[64,32,128]{2,1,0:T(8,128)S(1)}, f32[64,32,128]{2,1,0:T(8,128)S(1)}, u32[]{:S(2)}, u32[]{:S(2)}) collective-permute-start(f32[64,32,128]{2,1,0:T(8,128)S(1)} %all_to_all.11.half), channel_id=1, source_target_pairs={{0,4},{4,0},{1,5},{5,1},{2,6},{6,2},{3,7},{7,3},{8,12},{12,8},{9,1... | collective-permute-start | bytes 3145736 | tf_op jit(solution)/shard_map/ppermute | solution.py:717
  120.3 2.3 %collective-permute-done.15.away = f32[64,32,128]{2,1,0:T(8,128)S(1)} collective-permute-done((f32[64,32,128]{2,1,0:T(8,128)S(1)}, f32[64,32,128]{2,1,0:T(8,128)S(1)}, u32[]{:S(2)}, u32[]{:S(2)}) %collective-permute-start.15) | collective-permute-done | bytes 1048608 | tf_op jit(solution)/shard_map/ppermute | solution.py:717
  122.6 1.8 %finish.1 = (f32[256,512]{1,0:T(8,128)}, f32[512,512]{1,0:T(8,128)}, f32[4,128]{1,0:T(4,128)}) custom-call(s32[8]{0:T(128)S(1)} %stack.47.place, f32[64,32,128]{2,1,0:T(8,128)S(1)} %all_to_all.11.half, f32[64,32,128]{2,1,0:T(8,128)S(1)} %collective-permute-done.15.away), custom_call_target="tpu_custom_call" | custom-call | tf_op jit(solution)/shard_map/finish/pallas_call | solution.py:554
  (28 shorter events, 9.1 us)
Async XLA Ops:
  10.7 12.1 %collective-permute-start.1 = (f32[20,2,256]{2,1,0:T(2,128)S(1)}, f32[20,2,256]{2,1,0:T(2,128)S(1)}, u32[]{:S(2)}, u32[]{:S(2)}) collective-permute-start(f32[20,2,256]{2,1,0:T(2,128)S(1)} %get-tuple-element.64), channel_id=1, source_target_pairs={{0,1},{1,2},{2,3},{3,0},{4,5},{5,6},{6,7},{7,4},{8,9},{9,10},{10,1... | collective-permute-start | bytes 122888 | tf_op jit(solution)/shard_map/ppermute | solution.py:568
  13.2 9.6 %collective-permute-start = (f32[20,3,256]{2,1,0:T(4,128)S(1)}, f32[20,3,256]{2,1,0:T(4,128)S(1)}, u32[]{:S(2)}, u32[]{:S(2)}) collective-permute-start(f32[20,3,256]{2,1,0:T(4,128)S(1)} %get-tuple-element.63), channel_id=1, source_target_pairs={{0,3},{1,0},{2,1},{3,2},{4,7},{5,4},{6,5},{7,6},{8,11},{9,8},{10,9... | collective-permute-start | bytes 184328 | tf_op jit(solution)/shard_map/ppermute | solution.py:568
  23.4 6.3 %collective-permute-start.2 = (f32[14,16,256]{2,1,0:T(8,128)S(1)}, f32[14,16,256]{2,1,0:T(8,128)S(1)}, u32[]{:S(2)}, u32[]{:S(2)}) collective-permute-start(f32[14,16,256]{2,1,0:T(8,128)S(1)} %get-tuple-element.67), channel_id=1, source_target_pairs={{0,124},{4,0},{8,4},{12,8},{16,12},{20,16},{24,20},{28,24},{32,28}... | collective-permute-start | bytes 688136 | tf_op jit(solution)/shard_map/ppermute | solution.py:568
  24.4 5.3 %collective-permute-start.3 = (f32[10,16,256]{2,1,0:T(8,128)S(1)}, f32[10,16,256]{2,1,0:T(8,128)S(1)}, u32[]{:S(2)}, u32[]{:S(2)}) collective-permute-start(f32[10,16,256]{2,1,0:T(8,128)S(1)} %get-tuple-element.68), channel_id=1, source_target_pairs={{0,4},{4,8},{8,12},{12,16},{16,20},{20,24},{24,28},{28,32},{32,36}... | collective-permute-start | bytes 491528 | tf_op jit(solution)/shard_map/ppermute | solution.py:568
  32.3 8.0 %collective-permute-start.4 = (f32[8,128]{1,0:T(8,128)S(1)}, f32[8,128]{1,0:T(8,128)S(1)}, u32[]{:S(2)}, u32[]{:S(2)}) collective-permute-start(f32[8,128]{1,0:T(8,128)S(1)} %get-tuple-element.74), channel_id=1, source_target_pairs={{0,4},{4,0},{1,5},{5,1},{2,6},{6,2},{3,7},{7,3},{8,12},{12,8},{9,1... | collective-permute-start | bytes 12296 | tf_op jit(solution)/shard_map/ppermute | solution.py:572
  40.3 2.5 %collective-permute-start.7 = (f32[8,128]{1,0:T(8,128)S(1)}, f32[8,128]{1,0:T(8,128)S(1)}, u32[]{:S(2)}, u32[]{:S(2)}) collective-permute-start(f32[8,128]{1,0:T(8,128)S(1)} %add.41), channel_id=1, source_target_pairs={{0,3},{1,0},{2,1},{3,2},{4,7},{5,4},{6,5},{7,6},{8,11},{9,8},{10,9... | collective-permute-start | bytes 12296 | tf_op jit(solution)/shard_map/ppermute | solution.py:568
  41.7 4.0 %collective-permute-start.6 = (f32[8,128]{1,0:T(8,128)S(1)}, f32[8,128]{1,0:T(8,128)S(1)}, u32[]{:S(2)}, u32[]{:S(2)}) collective-permute-start(f32[8,128]{1,0:T(8,128)S(1)} %add.41), channel_id=1, source_target_pairs={{0,2},{1,3},{2,0},{3,1},{4,6},{5,7},{6,4},{7,5},{8,10},{9,11},{10,... | collective-permute-start | bytes 12296 | tf_op jit(solution)/shard_map/ppermute | solution.py:568
  41.7 4.0 %collective-permute-start.5 = (f32[8,128]{1,0:T(8,128)S(1)}, f32[8,128]{1,0:T(8,128)S(1)}, u32[]{:S(2)}, u32[]{:S(2)}) collective-permute-start(f32[8,128]{1,0:T(8,128)S(1)} %add.41), channel_id=1, source_target_pairs={{0,1},{1,2},{2,3},{3,0},{4,5},{5,6},{6,7},{7,4},{8,9},{9,10},{10,1... | collective-permute-start | bytes 12296 | tf_op jit(solution)/shard_map/ppermute | solution.py:568
  45.7 3.6 %collective-permute-start.10 = (f32[8,128]{1,0:T(8,128)S(1)}, f32[8,128]{1,0:T(8,128)S(1)}, u32[]{:S(2)}, u32[]{:S(2)}) collective-permute-start(f32[8,128]{1,0:T(8,128)S(1)} %add_add_fusion.2), channel_id=1, source_target_pairs={{0,24},{8,0},{16,8},{24,16},{1,25},{9,1},{17,9},{25,17},{2,26},{10... | collective-permute-start | bytes 12296 | tf_op jit(solution)/shard_map/ppermute | solution.py:568
  46.0 4.0 %collective-permute-start.9 = (f32[8,128]{1,0:T(8,128)S(1)}, f32[8,128]{1,0:T(8,128)S(1)}, u32[]{:S(2)}, u32[]{:S(2)}) collective-permute-start(f32[8,128]{1,0:T(8,128)S(1)} %add_add_fusion.2), channel_id=1, source_target_pairs={{0,16},{8,24},{16,0},{24,8},{1,17},{9,25},{17,1},{25,9},{2,18},{10... | collective-permute-start | bytes 12296 | tf_op jit(solution)/shard_map/ppermute | solution.py:568
  46.1 4.7 %collective-permute-start.8 = (f32[8,128]{1,0:T(8,128)S(1)}, f32[8,128]{1,0:T(8,128)S(1)}, u32[]{:S(2)}, u32[]{:S(2)}) collective-permute-start(f32[8,128]{1,0:T(8,128)S(1)} %add_add_fusion.2), channel_id=1, source_target_pairs={{0,8},{8,16},{16,24},{24,0},{1,9},{9,17},{17,25},{25,1},{2,10},{10... | collective-permute-start | bytes 12296 | tf_op jit(solution)/shard_map/ppermute | solution.py:568
  50.8 3.4 %collective-permute-start.13 = (f32[8,128]{1,0:T(8,128)S(1)}, f32[8,128]{1,0:T(8,128)S(1)}, u32[]{:S(2)}, u32[]{:S(2)}) collective-permute-start(f32[8,128]{1,0:T(8,128)S(1)} %add_add_fusion.1), channel_id=1, source_target_pairs={{0,96},{32,0},{64,32},{96,64},{1,97},{33,1},{65,33},{97,65},{2,98}... | collective-permute-start | bytes 12296 | tf_op jit(solution)/shard_map/ppermute | solution.py:568
  50.9 4.0 %collective-permute-start.12 = (f32[8,128]{1,0:T(8,128)S(1)}, f32[8,128]{1,0:T(8,128)S(1)}, u32[]{:S(2)}, u32[]{:S(2)}) collective-permute-start(f32[8,128]{1,0:T(8,128)S(1)} %add_add_fusion.1), channel_id=1, source_target_pairs={{0,64},{32,96},{64,0},{96,32},{1,65},{33,97},{65,1},{97,33},{2,66}... | collective-permute-start | bytes 12296 | tf_op jit(solution)/shard_map/ppermute | solution.py:568
  50.9 4.7 %collective-permute-start.11 = (f32[8,128]{1,0:T(8,128)S(1)}, f32[8,128]{1,0:T(8,128)S(1)}, u32[]{:S(2)}, u32[]{:S(2)}) collective-permute-start(f32[8,128]{1,0:T(8,128)S(1)} %add_add_fusion.1), channel_id=1, source_target_pairs={{0,32},{32,64},{64,96},{96,0},{1,33},{33,65},{65,97},{97,1},{2,34}... | collective-permute-start | bytes 12296 | tf_op jit(solution)/shard_map/ppermute | solution.py:568
  67.6 6.6 %collective-permute-start.14 = (f32[2,768,128]{2,1,0:T(8,128)S(1)}, f32[2,768,128]{2,1,0:T(8,128)S(1)}, u32[]{:S(2)}, u32[]{:S(2)}) collective-permute-start(f32[2,768,128]{2,1,0:T(8,128)S(1)} %get-tuple-element.86), channel_id=1, source_target_pairs={{0,4},{4,0},{1,5},{5,1},{2,6},{6,2},{3,7},{7,3},{8,12},{12,8},{9,1... | collective-permute-start | bytes 2359304 | tf_op jit(solution)/shard_map/ppermute | solution.py:711
  116.9 5.7 %collective-permute-start.15 = (f32[64,32,128]{2,1,0:T(8,128)S(1)}, f32[64,32,128]{2,1,0:T(8,128)S(1)}, u32[]{:S(2)}, u32[]{:S(2)}) collective-permute-start(f32[64,32,128]{2,1,0:T(8,128)S(1)} %all_to_all.11.half), channel_id=1, source_target_pairs={{0,4},{4,0},{1,5},{5,1},{2,6},{6,2},{3,7},{7,3},{8,12},{12,8},{9,1... | collective-permute-start | bytes 3145736 | tf_op jit(solution)/shard_map/ppermute | solution.py:717

commit v3 on v2

--- a/solution.py
+++ b/solution.py
@@ -443,9 +443,9 @@
             stiff[p, r : r + 1, :] = stiffness_of(part)
 
 
-def back_kernel(w_mid, slope_mid, slope_in, back, done, *, first, count, span):
+def back_kernel(w_mid, slope_mid, slope_in, back, done, *, span):
     done[...] = jnp.zeros_like(done)
-    for start in range(first, first + count, span):
+    for start in range(0, back.shape[1], span):
         place = slice(start, start + span)
         product = jnp.dot(w_mid[...], slope_mid[:, place], preferred_element_type=F32)
         back[:, place] = (product * slope_in[:, place].astype(F32)).astype(BF)
@@ -657,36 +657,29 @@
     planes_ahead = shifted(planes_first, SLAB, -1)
     planes_behind = shifted(planes_last, SLAB, 1)
 
-    back = slope_in
-    ready = []
-    begin = 0
-    for part, share in enumerate((2, 4, 4)):
-        count = rows // share
-        back, done = run(
-            functools.partial(back_kernel, first=begin, count=count, span=1024),
-            f"back_{part}",
-            kept[:1] + [held(8, 128)],
-            w_mid_half,
-            slope_mid,
-            back,
-            scalars=0,
-            limit=16,
-            input_output_aliases={2: 0},
-            cost_estimate=pl.CostEstimate(
-                flops=2 * hidden * hidden * count,
-                bytes_accessed=6 * hidden * count,
-                transcendentals=0,
-            ),
-        )
-        begin += count
-        ready.append(done)
+    back, ready = run(
+        functools.partial(back_kernel, span=1024),
+        "back",
+        kept[:1] + [held(8, 128)],
+        w_mid_half,
+        slope_mid,
+        slope_in,
+        scalars=0,
+        limit=16,
+        input_output_aliases={2: 0},
+        cost_estimate=pl.CostEstimate(
+            flops=2 * hidden * hidden * rows,
+            bytes_accessed=6 * hidden * rows,
+            transcendentals=0,
+        ),
+    )
 
     vector = held(3, cells_x + 1, ROWS, cells_z)
     first, second, sums = run(
         krylov_kernel,
         "krylov",
         [vector, vector, held(8, 128)],
-        place, loads, stiff, planes_ahead, planes_behind, density, ready[0],
+        place, loads, stiff, planes_ahead, planes_behind, density, ready,
     )
     solution, slope, density = run(
         functools.partial(energy_kernel, elements_total),

time: 125 us -> 125 us (level)
  waiting for transfers between devices: 12.7 us -> 15.6 us
  starting transfers between devices: 27.6 us -> 26.2 us
  Pallas kernels: 41.3 us -> 40 us
    ppermute x1, starting transfers between devices: 7.19 us -> 3.21 us  [summed(): values = values + lax.ppermute(values, 'c', [(0, 1), (1, 0)])]
    ppermute x13, waiting for transfers between devices: 7.7 us -> 10.6 us  [shifted(): lax.ppermute(block, axis, [(i, (i + distance) % size) for i in range(size)])]
    ppermute x13, starting transfers between devices: 12.3 us -> 14.7 us  [shifted(): lax.ppermute(block, axis, [(i, (i + distance) % size) for i in range(size)])]
    pallas_call x12 -> x10, Pallas kernels: 41.3 us -> 40 us  [run(): pl.pallas_call(kernel, name=name, in_specs=[SCALARS] * scalars + [WHOLE]...]
  transfers between devices with their start and end apart: 16 -> 16, of which waited for: 10 -> 10; matrix products, arithmetic and copies ran while one was open for 0% -> 0% of each run, Pallas kernels for 11% -> 10%
where the time goes in v3:
time: 125 us; the launch traced here: 124 us
  blocking collectives  41.6 us (33%)
  Pallas kernels  40 us (32%)
  starting transfers between devices  26.2 us (21%)
  waiting for transfers between devices  15.6 us (12%)
    pallas_call x10, Pallas kernels, run(): pl.pallas_call(kernel, name=name, in_specs=[SCALARS] * scalars + [WHOLE]...  40 us
    all_to_all x1, blocking collectives, on_device(): parts = lax.all_to_all(half, CHIPS, 0, 0)  20.8 us
    all_to_all x1, blocking collectives, on_device(): half = lax.all_to_all(shares, CHIPS, 0, 0)  20.8 us
    ppermute x13, starting transfers between devices, shifted(): lax.ppermute(block, axis, [(i, (i + distance) % size) for i in range(size)])  14.7 us
    ppermute x13, waiting for transfers between devices, shifted(): lax.ppermute(block, axis, [(i, (i + distance) % size) for i in range(size)])  10.6 us
    ppermute x1, starting transfers between devices, on_device(): half = (mine + lax.ppermute(other, 'c', swap)).reshape(chips, -1, 128)  4.78 us
    ppermute x1, starting transfers between devices, on_device(): away = lax.ppermute(half, 'c', swap)  3.45 us
    ppermute x1, starting transfers between devices, summed(): values = values + lax.ppermute(values, 'c', [(0, 1), (1, 0)])  3.21 us
  transfers between devices with their start and end apart: 16, of which 10 were waited for; matrix products, arithmetic and copies ran while one was open for 0% of the time, Pallas kernels for 10%

profile of v3, /device:TPU:1, one launch (start us, length us, event | category | flops | bytes accessed | tf_op | source)
XLA Modules:
  0.0 124.4 jit_solution(13138732403192436262)
XLA Ops:
  0.7 2.6 %prepare.1 = (f32[4,4,8,256]{3,2,1,0:T(8,128)S(1)}, f32[8,128,4]{2,1,0:T(8,128)S(1)}, f32[8,128,4]{2,1,0:T(8,128)S(1)}, f32[128,256]{1,0:T(8,128)S(1)}, f32[128,...) custom-call(s32[8]{0:T(128)S(1)} %stack.47.place, ...), custom_call_target="tpu_custom_call" | custom-call | tf_op jit(solution)/shard_map/prepare/pallas_call | solution.py:554
  3.3 7.3 %outer.1 = (f32[4,4,256]{2,1,0:T(4,128)S(1)}, f32[20,3,256]{2,1,0:T(4,128)S(1)}, f32[20,2,256]{2,1,0:T(2,128)S(1)}, bf16[512,8192]{1,0:T(8,128)(2,1)S(1)}, bf16[...) custom-call(f32[8,128,4]{2,1,0:T(8,128)S(1)} %get-tuple-element.47.x_cos, ...), custom_call_target="tpu_custom_call" | custom-call | flops 3221225472 | bytes 16777216 | tf_op jit(solution)/shard_map/outer/pallas_call | solution.py:554
  10.7 2.5 %collective-permute-start.1 = (f32[20,2,256]{2,1,0:T(2,128)S(1)}, f32[20,2,256]{2,1,0:T(2,128)S(1)}, u32[]{:S(2)}, u32[]{:S(2)}) collective-permute-start(f32[20,2,256]{2,1,0:T(2,128)S(1)} %get-tuple-element.62), channel_id=1, source_target_pairs={{0,1},{1,2},{2,3},{3,0},{4,5},{5,6},{6,7},{7,4},{8,9},{9,10},{10,1... | collective-permute-start | bytes 122888 | tf_op jit(solution)/shard_map/ppermute | solution.py:568
  13.2 2.2 %collective-permute-start = (f32[20,3,256]{2,1,0:T(4,128)S(1)}, f32[20,3,256]{2,1,0:T(4,128)S(1)}, u32[]{:S(2)}, u32[]{:S(2)}) collective-permute-start(f32[20,3,256]{2,1,0:T(4,128)S(1)} %get-tuple-element.61), channel_id=1, source_target_pairs={{0,3},{1,0},{2,1},{3,2},{4,7},{5,4},{6,5},{7,6},{8,11},{9,8},{10,9... | collective-permute-start | bytes 184328 | tf_op jit(solution)/shard_map/ppermute | solution.py:568
  15.4 7.3 %inner.1 = (f32[4,8,256]{2,1,0:T(8,128)S(1)}, f32[4,8,256]{2,1,0:T(8,128)S(1)}, bf16[512,8192]{1,0:T(8,128)(2,1)S(1)}, bf16[512,8192]{1,0:T(8,128)(2,1)S(1)}, bf...) custom-call(f32[8,128,4]{2,1,0:T(8,128)S(1)} %get-tuple-element.47.x, ...), custom_call_target="tpu_custom_call", output_to_operand_aliasing={{2}: (9, {}), {3}: (10, {}), {4}: (11, {}), {5}: (12, {})} | custom-call | flops 3221225472 | bytes 16777216 | tf_op jit(solution)/shard_map/inner/pallas_call | solution.py:554
  23.4 2.2 %collective-permute-start.3 = (f32[10,16,256]{2,1,0:T(8,128)S(1)}, f32[10,16,256]{2,1,0:T(8,128)S(1)}, u32[]{:S(2)}, u32[]{:S(2)}) collective-permute-start(f32[10,16,256]{2,1,0:T(8,128)S(1)} %get-tuple-element.66), channel_id=1, source_target_pairs={{0,4},{4,8},{8,12},{12,16},{16,20},{20,24},{24,28},{28,32},{32,36}... | collective-permute-start | bytes 491528 | tf_op jit(solution)/shard_map/ppermute | solution.py:568
  25.6 5.0 %back.1 = (bf16[512,8192]{1,0:T(8,128)(2,1)S(1)}, f32[8,128]{1,0:T(8,128)S(1)}) custom-call(bf16[512,512]{1,0:T(8,128)(2,1)S(1)} %get-tuple-element.68.w_mid, bf16[512,8192]{1,0:T(8,128)(2,1)S(1)} %get-tuple-element.69.slope_mid, bf16[512,8192]{1,0:T(8,128)(2,1)S(1)} %get-tuple-element.70.slope_in), custom_call_target="tpu_custom_call", output_to_operand_aliasing={{0}: (2, {})} | custom-call | flops 4294967296 | bytes 25165824 | tf_op jit(solution)/shard_map/back/pallas_call | solution.py:554
  31.3 2.7 %krylov.1 = (f32[3,5,16,256]{3,2,1,0:T(8,128)S(1)}, f32[3,5,16,256]{3,2,1,0:T(8,128)S(1)}, f32[8,128]{1,0:T(8,128)S(1)}) custom-call(s32[8]{0:T(128)S(1)} %stack.47.place, f32[4,4,16,256]{3,2,1,0:T(8,128)S(1)} %get-tuple-element.63.loads, f32[4,16,256]{2,1,0:T(8,128)S(1)} %get-tuple-element.64.stiff, f32[14,16,256]{2,1,0:T(8,128)S(1)} %collective-permute-done.2.ahead, ...), custom_call_target="tpu_custom_call" | custom-call | tf_op jit(solution)/shard_map/krylov/pallas_call | solution.py:554
  34.0 3.2 %collective-permute-start.4 = (f32[8,128]{1,0:T(8,128)S(1)}, f32[8,128]{1,0:T(8,128)S(1)}, u32[]{:S(2)}, u32[]{:S(2)}) collective-permute-start(f32[8,128]{1,0:T(8,128)S(1)} %get-tuple-element.72), channel_id=1, source_target_pairs={{0,4},{4,0},{1,5},{5,1},{2,6},{6,2},{3,7},{7,3},{8,12},{12,8},{9,1... | collective-permute-start | bytes 12296 | tf_op jit(solution)/shard_map/ppermute | solution.py:572
  38.0 1.7 %collective-permute-start.7 = (f32[8,128]{1,0:T(8,128)S(1)}, f32[8,128]{1,0:T(8,128)S(1)}, u32[]{:S(2)}, u32[]{:S(2)}) collective-permute-start(f32[8,128]{1,0:T(8,128)S(1)} %add.41), channel_id=1, source_target_pairs={{0,3},{1,0},{2,1},{3,2},{4,7},{5,4},{6,5},{7,6},{8,11},{9,8},{10,9... | collective-permute-start | bytes 12296 | tf_op jit(solution)/shard_map/ppermute | solution.py:568
  40.5 3.2 %collective-permute-done.6 = f32[8,128]{1,0:T(8,128)S(1)} collective-permute-done((f32[8,128]{1,0:T(8,128)S(1)}, f32[8,128]{1,0:T(8,128)S(1)}, u32[]{:S(2)}, u32[]{:S(2)}) %collective-permute-start.6) | collective-permute-done | bytes 4128 | tf_op jit(solution)/shard_map/ppermute | solution.py:568
  43.7 1.3 %collective-permute-start.10 = (f32[8,128]{1,0:T(8,128)S(1)}, f32[8,128]{1,0:T(8,128)S(1)}, u32[]{:S(2)}, u32[]{:S(2)}) collective-permute-start(f32[8,128]{1,0:T(8,128)S(1)} %add_add_fusion.2), channel_id=1, source_target_pairs={{0,24},{8,0},{16,8},{24,16},{1,25},{9,1},{17,9},{25,17},{2,26},{10... | collective-permute-start | bytes 12296 | tf_op jit(solution)/shard_map/ppermute | solution.py:568
  46.2 2.8 %collective-permute-done.9 = f32[8,128]{1,0:T(8,128)S(1)} collective-permute-done((f32[8,128]{1,0:T(8,128)S(1)}, f32[8,128]{1,0:T(8,128)S(1)}, u32[]{:S(2)}, u32[]{:S(2)}) %collective-permute-start.9) | collective-permute-done | bytes 4128 | tf_op jit(solution)/shard_map/ppermute | solution.py:568
  49.0 2.7 %collective-permute-start.13 = (f32[8,128]{1,0:T(8,128)S(1)}, f32[8,128]{1,0:T(8,128)S(1)}, u32[]{:S(2)}, u32[]{:S(2)}) collective-permute-start(f32[8,128]{1,0:T(8,128)S(1)} %add_add_fusion.1), channel_id=1, source_target_pairs={{0,96},{32,0},{64,32},{96,64},{1,97},{33,1},{65,33},{97,65},{2,98}... | collective-permute-start | bytes 12296 | tf_op jit(solution)/shard_map/ppermute | solution.py:568
  52.5 3.2 %collective-permute-done.12 = f32[8,128]{1,0:T(8,128)S(1)} collective-permute-done((f32[8,128]{1,0:T(8,128)S(1)}, f32[8,128]{1,0:T(8,128)S(1)}, u32[]{:S(2)}, u32[]{:S(2)}) %collective-permute-start.12) | collective-permute-done | bytes 4128 | tf_op jit(solution)/shard_map/ppermute | solution.py:568
  55.7 1.4 %energy.1 = (f32[3,4,8,256]{3,2,1,0:T(8,128)}, f32[4,8,256]{2,1,0:T(8,128)S(1)}, f32[4,8,256]{2,1,0:T(8,128)}) custom-call(s32[8]{0:T(128)S(1)} %stack.47.place, f32[8,128]{1,0:T(8,128)S(1)} %add_add_fusion.sums, f32[4,4,16,256]{3,2,1,0:T(8,128)S(1)} %get-tuple-element.63.loads, f32[14,16,256]{2,1,0:T(8,128)S(1)} %collective-permute-done.2.ahead, ...), custom_call_target="tpu_custom_call" | custom-call | tf_op jit(solution)/shard_map/energy/pallas_call | solution.py:554
  57.2 10.5 %gradients.1 = (f32[2,768,128]{2,1,0:T(8,128)S(1)}, f32[2,768,128]{2,1,0:T(8,128)S(1)}, f32[4,128]{1,0:T(4,128)S(1)}) custom-call(s32[8]{0:T(128)S(1)} %stack.47.place, f32[4,8,256]{2,1,0:T(8,128)S(1)} %get-tuple-element.77.slope, f32[8,128,4]{2,1,0:T(8,128)S(1)} %get-tuple-element.47.x_cos, f32[8,128,4]{2,1,0:T(8,128)S(1)} %get-tuple-element.48.x_sin, ...), custom_call_target="tpu_custom_call" | custom-call | tf_op jit(solution)/shard_map/gradients/pallas_call | solution.py:554
  67.7 4.8 %collective-permute-start.14 = (f32[2,768,128]{2,1,0:T(8,128)S(1)}, f32[2,768,128]{2,1,0:T(8,128)S(1)}, u32[]{:S(2)}, u32[]{:S(2)}) collective-permute-start(f32[2,768,128]{2,1,0:T(8,128)S(1)} %get-tuple-element.82), channel_id=1, source_target_pairs={{0,4},{4,0},{1,5},{5,1},{2,6},{6,2},{3,7},{7,3},{8,12},{12,8},{9,1... | collective-permute-start | bytes 2359304 | tf_op jit(solution)/shard_map/ppermute | solution.py:704
  72.5 1.9 %collective-permute-done.14 = f32[2,768,128]{2,1,0:T(8,128)S(1)} collective-permute-done((f32[2,768,128]{2,1,0:T(8,128)S(1)}, f32[2,768,128]{2,1,0:T(8,128)S(1)}, u32[]{:S(2)}, u32[]{:S(2)}) %collective-permute-start.14) | collective-permute-done | bytes 786464 | tf_op jit(solution)/shard_map/ppermute | solution.py:704
  74.5 20.8 %all_to_all.10.parts = f32[64,24,128]{2,1,0:T(8,128)S(1)} all-to-all(f32[64,24,128]{2,1,0:T(8,128)S(1)} %bitcast.9), channel_id=1, replica_groups=mesh['x'=4,'y'=4,'c'=2,'z'=4] {'x','y','z'}, dimensions={0} | all-to-all | bytes 1572864 | tf_op jit(solution)/shard_map/all_to_all | solution.py:705
  96.0 20.8 %all_to_all.11.half = f32[64,32,128]{2,1,0:T(8,128)S(1)} all-to-all(f32[64,32,128]{2,1,0:T(8,128)S(1)} %share.1), channel_id=1, replica_groups=mesh['x'=4,'y'=4,'c'=2,'z'=4] {'x','y','z'}, dimensions={0} | all-to-all | bytes 2097152 | tf_op jit(solution)/shard_map/all_to_all | solution.py:709
  116.8 3.5 %collective-permute-start.15 = (f32[64,32,128]{2,1,0:T(8,128)S(1)}, f32[64,32,128]{2,1,0:T(8,128)S(1)}, u32[]{:S(2)}, u32[]{:S(2)}) collective-permute-start(f32[64,32,128]{2,1,0:T(8,128)S(1)} %all_to_all.11.half), channel_id=1, source_target_pairs={{0,4},{4,0},{1,5},{5,1},{2,6},{6,2},{3,7},{7,3},{8,12},{12,8},{9,1... | collective-permute-start | bytes 3145736 | tf_op jit(solution)/shard_map/ppermute | solution.py:710
  120.3 2.3 %collective-permute-done.15.away = f32[64,32,128]{2,1,0:T(8,128)S(1)} collective-permute-done((f32[64,32,128]{2,1,0:T(8,128)S(1)}, f32[64,32,128]{2,1,0:T(8,128)S(1)}, u32[]{:S(2)}, u32[]{:S(2)}) %collective-permute-start.15) | collective-permute-done | bytes 1048608 | tf_op jit(solution)/shard_map/ppermute | solution.py:710
  122.6 1.8 %finish.1 = (f32[256,512]{1,0:T(8,128)}, f32[512,512]{1,0:T(8,128)}, f32[4,128]{1,0:T(4,128)}) custom-call(s32[8]{0:T(128)S(1)} %stack.47.place, f32[64,32,128]{2,1,0:T(8,128)S(1)} %all_to_all.11.half, f32[64,32,128]{2,1,0:T(8,128)S(1)} %collective-permute-done.15.away), custom_call_target="tpu_custom_call" | custom-call | tf_op jit(solution)/shard_map/finish/pallas_call | solution.py:554
  (26 shorter events, 5.8 us)
Async XLA Ops:
  10.7 12.1 %collective-permute-start.1 = (f32[20,2,256]{2,1,0:T(2,128)S(1)}, f32[20,2,256]{2,1,0:T(2,128)S(1)}, u32[]{:S(2)}, u32[]{:S(2)}) collective-permute-start(f32[20,2,256]{2,1,0:T(2,128)S(1)} %get-tuple-element.62), channel_id=1, source_target_pairs={{0,1},{1,2},{2,3},{3,0},{4,5},{5,6},{6,7},{7,4},{8,9},{9,10},{10,1... | collective-permute-start | bytes 122888 | tf_op jit(solution)/shard_map/ppermute | solution.py:568
  13.2 9.6 %collective-permute-start = (f32[20,3,256]{2,1,0:T(4,128)S(1)}, f32[20,3,256]{2,1,0:T(4,128)S(1)}, u32[]{:S(2)}, u32[]{:S(2)}) collective-permute-start(f32[20,3,256]{2,1,0:T(4,128)S(1)} %get-tuple-element.61), channel_id=1, source_target_pairs={{0,3},{1,0},{2,1},{3,2},{4,7},{5,4},{6,5},{7,6},{8,11},{9,8},{10,9... | collective-permute-start | bytes 184328 | tf_op jit(solution)/shard_map/ppermute | solution.py:568
  23.4 7.2 %collective-permute-start.3 = (f32[10,16,256]{2,1,0:T(8,128)S(1)}, f32[10,16,256]{2,1,0:T(8,128)S(1)}, u32[]{:S(2)}, u32[]{:S(2)}) collective-permute-start(f32[10,16,256]{2,1,0:T(8,128)S(1)} %get-tuple-element.66), channel_id=1, source_target_pairs={{0,4},{4,8},{8,12},{12,16},{16,20},{20,24},{24,28},{28,32},{32,36}... | collective-permute-start | bytes 491528 | tf_op jit(solution)/shard_map/ppermute | solution.py:568
  25.6 5.7 %collective-permute-start.2 = (f32[14,16,256]{2,1,0:T(8,128)S(1)}, f32[14,16,256]{2,1,0:T(8,128)S(1)}, u32[]{:S(2)}, u32[]{:S(2)}) collective-permute-start(f32[14,16,256]{2,1,0:T(8,128)S(1)} %get-tuple-element.65), channel_id=1, source_target_pairs={{0,124},{4,0},{8,4},{12,8},{16,12},{20,16},{24,20},{28,24},{32,28}... | collective-permute-start | bytes 688136 | tf_op jit(solution)/shard_map/ppermute | solution.py:568
  34.0 4.0 %collective-permute-start.4 = (f32[8,128]{1,0:T(8,128)S(1)}, f32[8,128]{1,0:T(8,128)S(1)}, u32[]{:S(2)}, u32[]{:S(2)}) collective-permute-start(f32[8,128]{1,0:T(8,128)S(1)} %get-tuple-element.72), channel_id=1, source_target_pairs={{0,4},{4,0},{1,5},{5,1},{2,6},{6,2},{3,7},{7,3},{8,12},{12,8},{9,1... | collective-permute-start | bytes 12296 | tf_op jit(solution)/shard_map/ppermute | solution.py:572
  38.0 2.5 %collective-permute-start.7 = (f32[8,128]{1,0:T(8,128)S(1)}, f32[8,128]{1,0:T(8,128)S(1)}, u32[]{:S(2)}, u32[]{:S(2)}) collective-permute-start(f32[8,128]{1,0:T(8,128)S(1)} %add.41), channel_id=1, source_target_pairs={{0,3},{1,0},{2,1},{3,2},{4,7},{5,4},{6,5},{7,6},{8,11},{9,8},{10,9... | collective-permute-start | bytes 12296 | tf_op jit(solution)/shard_map/ppermute | solution.py:568
  39.7 4.0 %collective-permute-start.6 = (f32[8,128]{1,0:T(8,128)S(1)}, f32[8,128]{1,0:T(8,128)S(1)}, u32[]{:S(2)}, u32[]{:S(2)}) collective-permute-start(f32[8,128]{1,0:T(8,128)S(1)} %add.41), channel_id=1, source_target_pairs={{0,2},{1,3},{2,0},{3,1},{4,6},{5,7},{6,4},{7,5},{8,10},{9,11},{10,... | collective-permute-start | bytes 12296 | tf_op jit(solution)/shard_map/ppermute | solution.py:568
  39.7 4.0 %collective-permute-start.5 = (f32[8,128]{1,0:T(8,128)S(1)}, f32[8,128]{1,0:T(8,128)S(1)}, u32[]{:S(2)}, u32[]{:S(2)}) collective-permute-start(f32[8,128]{1,0:T(8,128)S(1)} %add.41), channel_id=1, source_target_pairs={{0,1},{1,2},{2,3},{3,0},{4,5},{5,6},{6,7},{7,4},{8,9},{9,10},{10,1... | collective-permute-start | bytes 12296 | tf_op jit(solution)/shard_map/ppermute | solution.py:568
  43.7 2.5 %collective-permute-start.10 = (f32[8,128]{1,0:T(8,128)S(1)}, f32[8,128]{1,0:T(8,128)S(1)}, u32[]{:S(2)}, u32[]{:S(2)}) collective-permute-start(f32[8,128]{1,0:T(8,128)S(1)} %add_add_fusion.2), channel_id=1, source_target_pairs={{0,24},{8,0},{16,8},{24,16},{1,25},{9,1},{17,9},{25,17},{2,26},{10... | collective-permute-start | bytes 12296 | tf_op jit(solution)/shard_map/ppermute | solution.py:568
  45.0 4.0 %collective-permute-start.9 = (f32[8,128]{1,0:T(8,128)S(1)}, f32[8,128]{1,0:T(8,128)S(1)}, u32[]{:S(2)}, u32[]{:S(2)}) collective-permute-start(f32[8,128]{1,0:T(8,128)S(1)} %add_add_fusion.2), channel_id=1, source_target_pairs={{0,16},{8,24},{16,0},{24,8},{1,17},{9,25},{17,1},{25,9},{2,18},{10... | collective-permute-start | bytes 12296 | tf_op jit(solution)/shard_map/ppermute | solution.py:568
  45.0 4.0 %collective-permute-start.8 = (f32[8,128]{1,0:T(8,128)S(1)}, f32[8,128]{1,0:T(8,128)S(1)}, u32[]{:S(2)}, u32[]{:S(2)}) collective-permute-start(f32[8,128]{1,0:T(8,128)S(1)} %add_add_fusion.2), channel_id=1, source_target_pairs={{0,8},{8,16},{16,24},{24,0},{1,9},{9,17},{17,25},{25,1},{2,10},{10... | collective-permute-start | bytes 12296 | tf_op jit(solution)/shard_map/ppermute | solution.py:568
  49.0 3.5 %collective-permute-start.13 = (f32[8,128]{1,0:T(8,128)S(1)}, f32[8,128]{1,0:T(8,128)S(1)}, u32[]{:S(2)}, u32[]{:S(2)}) collective-permute-start(f32[8,128]{1,0:T(8,128)S(1)} %add_add_fusion.1), channel_id=1, source_target_pairs={{0,96},{32,0},{64,32},{96,64},{1,97},{33,1},{65,33},{97,65},{2,98}... | collective-permute-start | bytes 12296 | tf_op jit(solution)/shard_map/ppermute | solution.py:568
  51.7 4.0 %collective-permute-start.12 = (f32[8,128]{1,0:T(8,128)S(1)}, f32[8,128]{1,0:T(8,128)S(1)}, u32[]{:S(2)}, u32[]{:S(2)}) collective-permute-start(f32[8,128]{1,0:T(8,128)S(1)} %add_add_fusion.1), channel_id=1, source_target_pairs={{0,64},{32,96},{64,0},{96,32},{1,65},{33,97},{65,1},{97,33},{2,66}... | collective-permute-start | bytes 12296 | tf_op jit(solution)/shard_map/ppermute | solution.py:568
  52.1 3.7 %collective-permute-start.11 = (f32[8,128]{1,0:T(8,128)S(1)}, f32[8,128]{1,0:T(8,128)S(1)}, u32[]{:S(2)}, u32[]{:S(2)}) collective-permute-start(f32[8,128]{1,0:T(8,128)S(1)} %add_add_fusion.1), channel_id=1, source_target_pairs={{0,32},{32,64},{64,96},{96,0},{1,33},{33,65},{65,97},{97,1},{2,34}... | collective-permute-start | bytes 12296 | tf_op jit(solution)/shard_map/ppermute | solution.py:568
  67.7 6.7 %collective-permute-start.14 = (f32[2,768,128]{2,1,0:T(8,128)S(1)}, f32[2,768,128]{2,1,0:T(8,128)S(1)}, u32[]{:S(2)}, u32[]{:S(2)}) collective-permute-start(f32[2,768,128]{2,1,0:T(8,128)S(1)} %get-tuple-element.82), channel_id=1, source_target_pairs={{0,4},{4,0},{1,5},{5,1},{2,6},{6,2},{3,7},{7,3},{8,12},{12,8},{9,1... | collective-permute-start | bytes 2359304 | tf_op jit(solution)/shard_map/ppermute | solution.py:704
  116.8 5.7 %collective-permute-start.15 = (f32[64,32,128]{2,1,0:T(8,128)S(1)}, f32[64,32,128]{2,1,0:T(8,128)S(1)}, u32[]{:S(2)}, u32[]{:S(2)}) collective-permute-start(f32[64,32,128]{2,1,0:T(8,128)S(1)} %all_to_all.11.half), channel_id=1, source_target_pairs={{0,4},{4,0},{1,5},{5,1},{2,6},{6,2},{3,7},{7,3},{8,12},{12,8},{9,1... | collective-permute-start | bytes 3145736 | tf_op jit(solution)/shard_map/ppermute | solution.py:710

commit v4 on v3

--- a/solution.py
+++ b/solution.py
@@ -206,11 +206,11 @@
         last = term if last is None else last + term
         volume = density[e] if volume is None else volume + density[e]
     totals += [last, volume]
-    row_number = lax.broadcasted_iota(jnp.int32, sums.shape, 0)
+    lane = lax.broadcasted_iota(jnp.int32, sums.shape, 1)
     result = jnp.zeros(sums.shape, F32)
     for k, total in enumerate(totals):
         scalar = jnp.sum(jnp.sum(total, axis=0, keepdims=True), axis=1, keepdims=True)
-        result = jnp.where(row_number == k, scalar, result)
+        result = jnp.where(lane == k, scalar, result)
     sums[...] = result
     for p in range(cells + 1):
         for d in range(3):
@@ -264,7 +264,14 @@
 def energy_kernel(
     elements, place, sums, loads, ahead, first, second, density, solution, slope, out
 ):
-    rows_of = [sums[k : k + 1, :] for k in range(2 * ITERS + 1)]
+    total = jnp.sum(sums[...], axis=0)
+    lane = lax.broadcasted_iota(jnp.int32, total.shape, 1)
+    rows_of = [
+        jnp.broadcast_to(
+            jnp.sum(jnp.where(lane == k, total, 0.0), axis=1, keepdims=True), total.shape
+        )
+        for k in range(2 * ITERS + 1)
+    ]
     factors, compliance = krylov_steps(rows_of[: 2 * ITERS])
     volume = rows_of[2 * ITERS]
     constant = 2.0 * penalty * (volume / elements - vol_target) / elements
@@ -568,12 +575,10 @@
     return lax.ppermute(block, axis, [(i, (i + distance) % size) for i in range(size)])
 
 
-def summed(values):
-    values = values + lax.ppermute(values, "c", [(0, 1), (1, 0)])
-    for axis in ("z", "y", "x"):
-        others = [shifted(values, axis, k) for k in range(1, lax.axis_size(axis))]
-        values = values + sum(others)
-    return values
+def gathered(values):
+    chip = values + lax.ppermute(values, "c", [(0, 1), (1, 0)])
+    sent = jnp.broadcast_to(chip[None], (lax.axis_size(CHIPS),) + chip.shape)
+    return lax.all_to_all(sent, CHIPS, 0, 0)
 
 
 def on_device(load_values, load_mask, fixed_mask, frequencies, weight_in, weight_mid, weight_out):
@@ -678,14 +683,14 @@
     first, second, sums = run(
         krylov_kernel,
         "krylov",
-        [vector, vector, held(8, 128)],
+        [vector, vector, held(1, 128)],
         place, loads, stiff, planes_ahead, planes_behind, density, ready,
     )
     solution, slope, density = run(
         functools.partial(energy_kernel, elements_total),
         "energy",
         [shaped(3, *field), held(*field), shaped(*field)],
-        place, summed(sums), loads, planes_ahead, first, second, density,
+        place, gathered(sums), loads, planes_ahead, first, second, density,
     )
 
     height = hidden + inputs

time: 125 us -> 118 us (0.944)
  blocking collectives: 41.6 us -> 55.3 us
  starting transfers between devices: 26.2 us -> 15.3 us
  waiting for transfers between devices: 15.6 us -> 5.73 us
    all_to_all x0 -> x1, blocking collectives: none -> 15.5 us  [gathered(): return lax.all_to_all(sent, CHIPS, 0, 0)]
    ppermute x13 -> x4, waiting for transfers between devices: 10.6 us -> 0.71 us  [shifted(): lax.ppermute(block, axis, [(i, (i + distance) % size) for i in range(size)])]
    ppermute x13 -> x4, starting transfers between devices: 14.7 us -> 6.94 us  [shifted(): lax.ppermute(block, axis, [(i, (i + distance) % size) for i in range(size)])]
    ppermute x1, starting transfers between devices: 4.78 us -> 1.7 us  [on_device(): half = (mine + lax.ppermute(other, 'c', swap)).reshape(chips, -1, 128)]
    all_to_all x1, blocking collectives: 20.8 us -> 19 us  [on_device(): parts = lax.all_to_all(half, CHIPS, 0, 0)]
  transfers between devices with their start and end apart: 16 -> 7, of which waited for: 10 -> 4; matrix products, arithmetic and copies ran while one was open for 0% -> 0% of each run, Pallas kernels for 10% -> 11%
where the time goes in v4:
time: 118 us; the launch traced here: 117 us
  blocking collectives  55.3 us (47%)
  Pallas kernels  40.1 us (34%)
  starting transfers between devices  15.3 us (13%)
  waiting for transfers between devices  5.73 us (5%)
    pallas_call x10, Pallas kernels, run(): pl.pallas_call(kernel, name=name, in_specs=[SCALARS] * scalars + [WHOLE]...  40.1 us
    all_to_all x1, blocking collectives, on_device(): half = lax.all_to_all(shares, CHIPS, 0, 0)  20.8 us
    all_to_all x1, blocking collectives, on_device(): parts = lax.all_to_all(half, CHIPS, 0, 0)  19 us
    all_to_all x1, blocking collectives, gathered(): return lax.all_to_all(sent, CHIPS, 0, 0)  15.5 us
    ppermute x4, starting transfers between devices, shifted(): lax.ppermute(block, axis, [(i, (i + distance) % size) for i in range(size)])  6.94 us
    ppermute x1, starting transfers between devices, on_device(): away = lax.ppermute(half, 'c', swap)  3.45 us
    ppermute x1, starting transfers between devices, gathered(): chip = values + lax.ppermute(values, 'c', [(0, 1), (1, 0)])  3.21 us
  transfers between devices with their start and end apart: 7, of which 4 were waited for; matrix products, arithmetic and copies ran while one was open for 0% of the time, Pallas kernels for 11%

profile of v4, /device:TPU:1, one launch (start us, length us, event | category | flops | bytes accessed | tf_op | source)
XLA Modules:
  0.0 117.4 jit_solution(11082513443706799462)
XLA Ops:
  0.7 2.6 %prepare.1 = (f32[4,4,8,256]{3,2,1,0:T(8,128)S(1)}, f32[8,128,4]{2,1,0:T(8,128)S(1)}, f32[8,128,4]{2,1,0:T(8,128)S(1)}, f32[128,256]{1,0:T(8,128)S(1)}, f32[128,...) custom-call(s32[8]{0:T(128)S(1)} %stack.47.place, ...), custom_call_target="tpu_custom_call" | custom-call | tf_op jit(solution)/shard_map/prepare/pallas_call | solution.py:561
  3.3 7.3 %outer.1 = (f32[4,4,256]{2,1,0:T(4,128)S(1)}, f32[20,3,256]{2,1,0:T(4,128)S(1)}, f32[20,2,256]{2,1,0:T(2,128)S(1)}, bf16[512,8192]{1,0:T(8,128)(2,1)S(1)}, bf16[...) custom-call(f32[8,128,4]{2,1,0:T(8,128)S(1)} %get-tuple-element.47.x_cos, ...), custom_call_target="tpu_custom_call" | custom-call | flops 3221225472 | bytes 16777216 | tf_op jit(solution)/shard_map/outer/pallas_call | solution.py:561
  10.7 2.5 %collective-permute-start.1 = (f32[20,2,256]{2,1,0:T(2,128)S(1)}, f32[20,2,256]{2,1,0:T(2,128)S(1)}, u32[]{:S(2)}, u32[]{:S(2)}) collective-permute-start(f32[20,2,256]{2,1,0:T(2,128)S(1)} %get-tuple-element.62), channel_id=1, source_target_pairs={{0,1},{1,2},{2,3},{3,0},{4,5},{5,6},{6,7},{7,4},{8,9},{9,10},{10,1... | collective-permute-start | bytes 122888 | tf_op jit(solution)/shard_map/ppermute | solution.py:575
  13.2 2.2 %collective-permute-start = (f32[20,3,256]{2,1,0:T(4,128)S(1)}, f32[20,3,256]{2,1,0:T(4,128)S(1)}, u32[]{:S(2)}, u32[]{:S(2)}) collective-permute-start(f32[20,3,256]{2,1,0:T(4,128)S(1)} %get-tuple-element.61), channel_id=1, source_target_pairs={{0,3},{1,0},{2,1},{3,2},{4,7},{5,4},{6,5},{7,6},{8,11},{9,8},{10,9... | collective-permute-start | bytes 184328 | tf_op jit(solution)/shard_map/ppermute | solution.py:575
  15.4 7.3 %inner.1 = (f32[4,8,256]{2,1,0:T(8,128)S(1)}, f32[4,8,256]{2,1,0:T(8,128)S(1)}, bf16[512,8192]{1,0:T(8,128)(2,1)S(1)}, bf16[512,8192]{1,0:T(8,128)(2,1)S(1)}, bf...) custom-call(f32[8,128,4]{2,1,0:T(8,128)S(1)} %get-tuple-element.47.x, ...), custom_call_target="tpu_custom_call", output_to_operand_aliasing={{2}: (9, {}), {3}: (10, {}), {4}: (11, {}), {5}: (12, {})} | custom-call | flops 3221225472 | bytes 16777216 | tf_op jit(solution)/shard_map/inner/pallas_call | solution.py:561
  22.8 0.6 join.1
  23.4 2.2 %collective-permute-start.3 = (f32[10,16,256]{2,1,0:T(8,128)S(1)}, f32[10,16,256]{2,1,0:T(8,128)S(1)}, u32[]{:S(2)}, u32[]{:S(2)}) collective-permute-start(f32[10,16,256]{2,1,0:T(8,128)S(1)} %get-tuple-element.66), channel_id=1, source_target_pairs={{0,4},{4,8},{8,12},{12,16},{16,20},{20,24},{24,28},{28,32},{32,36}... | collective-permute-start | bytes 491528 | tf_op jit(solution)/shard_map/ppermute | solution.py:575
  25.6 5.0 %back.1 = (bf16[512,8192]{1,0:T(8,128)(2,1)S(1)}, f32[8,128]{1,0:T(8,128)S(1)}) custom-call(bf16[512,512]{1,0:T(8,128)(2,1)S(1)} %get-tuple-element.68.w_mid, bf16[512,8192]{1,0:T(8,128)(2,1)S(1)} %get-tuple-element.69.slope_mid, bf16[512,8192]{1,0:T(8,128)(2,1)S(1)} %get-tuple-element.70.slope_in), custom_call_target="tpu_custom_call", output_to_operand_aliasing={{0}: (2, {})} | custom-call | flops 4294967296 | bytes 25165824 | tf_op jit(solution)/shard_map/back/pallas_call | solution.py:561
  30.6 0.7 collective-permute-done.2.ahead
  31.3 2.7 %krylov.1 = (f32[3,5,16,256]{3,2,1,0:T(8,128)S(1)}, f32[3,5,16,256]{3,2,1,0:T(8,128)S(1)}, f32[1,128]{1,0:T(1,128)S(1)}) custom-call(s32[8]{0:T(128)S(1)} %stack.47.place, f32[4,4,16,256]{3,2,1,0:T(8,128)S(1)} %get-tuple-element.63.loads, f32[4,16,256]{2,1,0:T(8,128)S(1)} %get-tuple-element.64.stiff, f32[14,16,256]{2,1,0:T(8,128)S(1)} %collective-permute-done.2.ahead, ...), custom_call_target="tpu_custom_call" | custom-call | tf_op jit(solution)/shard_map/krylov/pallas_call | solution.py:561
  34.0 3.2 %collective-permute-start.4 = (f32[1,128]{1,0:T(1,128)S(1)}, f32[1,128]{1,0:T(1,128)S(1)}, u32[]{:S(2)}, u32[]{:S(2)}) collective-permute-start(f32[1,128]{1,0:T(1,128)S(1)} %get-tuple-element.72), channel_id=1, source_target_pairs={{0,4},{4,0},{1,5},{5,1},{2,6},{6,2},{3,7},{7,3},{8,12},{12,8},{9,1... | collective-permute-start | bytes 1544 | tf_op jit(solution)/shard_map/ppermute | solution.py:579
  37.2 0.8 collective-permute-done.4
  38.1 15.5 %all_to_all.15.sums = f32[64,1,128]{2,1,0:T(1,128)S(1)} all-to-all(f32[64,1,128]{2,1,0:T(1,128)S(1)} %broadcast_in_dim.9), channel_id=1, replica_groups=mesh['x'=4,'y'=4,'c'=2,'z'=4] {'x','y','z'}, dimensions={0} | all-to-all | bytes 65536 | tf_op jit(solution)/shard_map/all_to_all | solution.py:581
  53.6 1.5 %energy.1 = (f32[3,4,8,256]{3,2,1,0:T(8,128)}, f32[4,8,256]{2,1,0:T(8,128)S(1)}, f32[4,8,256]{2,1,0:T(8,128)}) custom-call(s32[8]{0:T(128)S(1)} %stack.47.place, f32[64,1,128]{2,1,0:T(1,128)S(1)} %all_to_all.15.sums, f32[4,4,16,256]{3,2,1,0:T(8,128)S(1)} %get-tuple-element.63.loads, f32[14,16,256]{2,1,0:T(8,128)S(1)} %collective-permute-done.2.ahead, ...), custom_call_target="tpu_custom_call" | custom-call | tf_op jit(solution)/shard_map/energy/pallas_call | solution.py:561
  55.0 10.5 %gradients.1 = (f32[2,768,128]{2,1,0:T(8,128)S(1)}, f32[2,768,128]{2,1,0:T(8,128)S(1)}, f32[4,128]{1,0:T(4,128)S(1)}) custom-call(s32[8]{0:T(128)S(1)} %stack.47.place, f32[4,8,256]{2,1,0:T(8,128)S(1)} %get-tuple-element.77.slope, f32[8,128,4]{2,1,0:T(8,128)S(1)} %get-tuple-element.47.x_cos, f32[8,128,4]{2,1,0:T(8,128)S(1)} %get-tuple-element.48.x_sin, ...), custom_call_target="tpu_custom_call" | custom-call | tf_op jit(solution)/shard_map/gradients/pallas_call | solution.py:561
  65.6 1.7 %collective-permute-start.5 = (f32[2,768,128]{2,1,0:T(8,128)S(1)}, f32[2,768,128]{2,1,0:T(8,128)S(1)}, u32[]{:S(2)}, u32[]{:S(2)}) collective-permute-start(f32[2,768,128]{2,1,0:T(8,128)S(1)} %get-tuple-element.82), channel_id=1, source_target_pairs={{0,4},{4,0},{1,5},{5,1},{2,6},{6,2},{3,7},{7,3},{8,12},{12,8},{9,1... | collective-permute-start | bytes 2359304 | tf_op jit(solution)/shard_map/ppermute | solution.py:709
  67.3 1.9 %collective-permute-done.5 = f32[2,768,128]{2,1,0:T(8,128)S(1)} collective-permute-done((f32[2,768,128]{2,1,0:T(8,128)S(1)}, f32[2,768,128]{2,1,0:T(8,128)S(1)}, u32[]{:S(2)}, u32[]{:S(2)}) %collective-permute-start.5) | collective-permute-done | bytes 786464 | tf_op jit(solution)/shard_map/ppermute | solution.py:709
  69.2 0.1 add.15
  69.3 19.0 %all_to_all.16.parts = f32[64,24,128]{2,1,0:T(8,128)S(1)} all-to-all(f32[64,24,128]{2,1,0:T(8,128)S(1)} %bitcast.11), channel_id=1, replica_groups=mesh['x'=4,'y'=4,'c'=2,'z'=4] {'x','y','z'}, dimensions={0} | all-to-all | bytes 1572864 | tf_op jit(solution)/shard_map/all_to_all | solution.py:710
  88.3 0.7 share.1
  89.0 20.8 %all_to_all.17.half = f32[64,32,128]{2,1,0:T(8,128)S(1)} all-to-all(f32[64,32,128]{2,1,0:T(8,128)S(1)} %share.1), channel_id=1, replica_groups=mesh['x'=4,'y'=4,'c'=2,'z'=4] {'x','y','z'}, dimensions={0} | all-to-all | bytes 2097152 | tf_op jit(solution)/shard_map/all_to_all | solution.py:714
  109.8 3.5 %collective-permute-start.6 = (f32[64,32,128]{2,1,0:T(8,128)S(1)}, f32[64,32,128]{2,1,0:T(8,128)S(1)}, u32[]{:S(2)}, u32[]{:S(2)}) collective-permute-start(f32[64,32,128]{2,1,0:T(8,128)S(1)} %all_to_all.17.half), channel_id=1, source_target_pairs={{0,4},{4,0},{1,5},{5,1},{2,6},{6,2},{3,7},{7,3},{8,12},{12,8},{9,1... | collective-permute-start | bytes 3145736 | tf_op jit(solution)/shard_map/ppermute | solution.py:715
  113.2 2.3 %collective-permute-done.6.away = f32[64,32,128]{2,1,0:T(8,128)S(1)} collective-permute-done((f32[64,32,128]{2,1,0:T(8,128)S(1)}, f32[64,32,128]{2,1,0:T(8,128)S(1)}, u32[]{:S(2)}, u32[]{:S(2)}) %collective-permute-start.6) | collective-permute-done | bytes 1048608 | tf_op jit(solution)/shard_map/ppermute | solution.py:715
  115.5 1.8 %finish.1 = (f32[256,512]{1,0:T(8,128)}, f32[512,512]{1,0:T(8,128)}, f32[4,128]{1,0:T(4,128)}) custom-call(s32[8]{0:T(128)S(1)} %stack.47.place, f32[64,32,128]{2,1,0:T(8,128)S(1)} %all_to_all.17.half, f32[64,32,128]{2,1,0:T(8,128)S(1)} %collective-permute-done.6.away), custom_call_target="tpu_custom_call" | custom-call | tf_op jit(solution)/shard_map/finish/pallas_call | solution.py:561
  (7 shorter events, 0.1 us)
Async XLA Ops:
  10.7 12.1 %collective-permute-start.1 = (f32[20,2,256]{2,1,0:T(2,128)S(1)}, f32[20,2,256]{2,1,0:T(2,128)S(1)}, u32[]{:S(2)}, u32[]{:S(2)}) collective-permute-start(f32[20,2,256]{2,1,0:T(2,128)S(1)} %get-tuple-element.62), channel_id=1, source_target_pairs={{0,1},{1,2},{2,3},{3,0},{4,5},{5,6},{6,7},{7,4},{8,9},{9,10},{10,1... | collective-permute-start | bytes 122888 | tf_op jit(solution)/shard_map/ppermute | solution.py:575
  13.2 9.6 %collective-permute-start = (f32[20,3,256]{2,1,0:T(4,128)S(1)}, f32[20,3,256]{2,1,0:T(4,128)S(1)}, u32[]{:S(2)}, u32[]{:S(2)}) collective-permute-start(f32[20,3,256]{2,1,0:T(4,128)S(1)} %get-tuple-element.61), channel_id=1, source_target_pairs={{0,3},{1,0},{2,1},{3,2},{4,7},{5,4},{6,5},{7,6},{8,11},{9,8},{10,9... | collective-permute-start | bytes 184328 | tf_op jit(solution)/shard_map/ppermute | solution.py:575
  23.4 7.2 %collective-permute-start.3 = (f32[10,16,256]{2,1,0:T(8,128)S(1)}, f32[10,16,256]{2,1,0:T(8,128)S(1)}, u32[]{:S(2)}, u32[]{:S(2)}) collective-permute-start(f32[10,16,256]{2,1,0:T(8,128)S(1)} %get-tuple-element.66), channel_id=1, source_target_pairs={{0,4},{4,8},{8,12},{12,16},{16,20},{20,24},{24,28},{28,32},{32,36}... | collective-permute-start | bytes 491528 | tf_op jit(solution)/shard_map/ppermute | solution.py:575
  25.6 5.7 %collective-permute-start.2 = (f32[14,16,256]{2,1,0:T(8,128)S(1)}, f32[14,16,256]{2,1,0:T(8,128)S(1)}, u32[]{:S(2)}, u32[]{:S(2)}) collective-permute-start(f32[14,16,256]{2,1,0:T(8,128)S(1)} %get-tuple-element.65), channel_id=1, source_target_pairs={{0,124},{4,0},{8,4},{12,8},{16,12},{20,16},{24,20},{28,24},{32,28}... | collective-permute-start | bytes 688136 | tf_op jit(solution)/shard_map/ppermute | solution.py:575
  34.0 4.0 %collective-permute-start.4 = (f32[1,128]{1,0:T(1,128)S(1)}, f32[1,128]{1,0:T(1,128)S(1)}, u32[]{:S(2)}, u32[]{:S(2)}) collective-permute-start(f32[1,128]{1,0:T(1,128)S(1)} %get-tuple-element.72), channel_id=1, source_target_pairs={{0,4},{4,0},{1,5},{5,1},{2,6},{6,2},{3,7},{7,3},{8,12},{12,8},{9,1... | collective-permute-start | bytes 1544 | tf_op jit(solution)/shard_map/ppermute | solution.py:579
  65.6 3.6 %collective-permute-start.5 = (f32[2,768,128]{2,1,0:T(8,128)S(1)}, f32[2,768,128]{2,1,0:T(8,128)S(1)}, u32[]{:S(2)}, u32[]{:S(2)}) collective-permute-start(f32[2,768,128]{2,1,0:T(8,128)S(1)} %get-tuple-element.82), channel_id=1, source_target_pairs={{0,4},{4,0},{1,5},{5,1},{2,6},{6,2},{3,7},{7,3},{8,12},{12,8},{9,1... | collective-permute-start | bytes 2359304 | tf_op jit(solution)/shard_map/ppermute | solution.py:709
  109.8 5.7 %collective-permute-start.6 = (f32[64,32,128]{2,1,0:T(8,128)S(1)}, f32[64,32,128]{2,1,0:T(8,128)S(1)}, u32[]{:S(2)}, u32[]{:S(2)}) collective-permute-start(f32[64,32,128]{2,1,0:T(8,128)S(1)} %all_to_all.17.half), channel_id=1, source_target_pairs={{0,4},{4,0},{1,5},{5,1},{2,6},{6,2},{3,7},{7,3},{8,12},{12,8},{9,1... | collective-permute-start | bytes 3145736 | tf_op jit(solution)/shard_map/ppermute | solution.py:715

commit v5 on v4

--- a/solution.py
+++ b/solution.py
@@ -460,7 +460,7 @@
 
 def gradient_kernel(
     place, slope, x_cos, x_sin, z_cos, z_sin, hidden_in, slope_mid, back, hidden_mid,
-    mine, other, grad_out, mid, first, running,
+    mine, other, out_mine, mid, first, running,
 ):
     tables = (x_cos, x_sin, z_cos, z_sin)
     cells, rows, size = slope.shape
@@ -503,39 +503,64 @@
 
             @pl.when(core != owner)
             def _():
-                other[k, :height, :] = mid[:, lanes]
-                other[k, height:, :] = first_t[:, lanes]
+                start = k * mine.shape[1]
+                other[start : start + height, :] = mid[:, lanes]
+                other[start + height : start + mine.shape[1], :] = first_t[:, lanes]
 
     line = jnp.sum(running[...].T, axis=0, keepdims=True)
-    for k in range(grad_out.shape[0]):
-        grad_out[k : k + 1, :] = line[:, k * 128 : (k + 1) * 128]
-
-
-def share_kernel(place, parts, grad_out, shares):
-    chips, height, lanes = parts.shape
+    for k in range(2):
+        low = line[:, k * 128 : (k + 1) * 128]
+        high = line[:, (2 + k) * 128 : (3 + k) * 128]
+        out_mine[k : k + 1, :] = jnp.where(core == 0, low, high)
+        at = 2 * mine.shape[1] + k
+        other[at : at + 1, :] = jnp.where(core == 0, high, low)
+    other[2 * mine.shape[1] + 2 :, :] = jnp.zeros((6, 128), F32)
+
+
+def share_kernel(place, parts, out_mine, swapped, shares):
+    chips = parts.shape[0]
     total = parts[0]
     for chip in range(1, chips):
         total = total + parts[chip]
-    block = jnp.concatenate([total, grad_out[...], jnp.zeros(grad_out.shape, F32)], axis=0)
+    last = swapped.shape[0] - 8
+    out = out_mine[...] + swapped[last : last + 2, :]
+    block = jnp.concatenate([total, out], axis=0)
+    height = block.shape[0]
     for chip in range(chips):
-        shares[chip] = block
+        shares[chip * height : (chip + 1) * height, :] = block
 
 
 def finish_kernel(place, half, away, grad_in, grad_mid, grad_out):
-    chips = half.shape[0]
-    height = half.shape[1] - 2 * grad_out.shape[0]
+    height = 26
+    chips = half.shape[0] // height
     middle = grad_mid.shape[0]
-    at_first = place[CORE] == 0
-    for group in range(4):
-        part = pl.ds((group % 2) * (chips // 2), chips // 2)
-        own, far = half[part, :height, :], away[part, :height, :]
-        picked = jnp.where(at_first, own, far) if group < 2 else jnp.where(at_first, far, own)
-        picked = picked.reshape(-1, 128)
-        lanes = slice(group * 128, (group + 1) * 128)
-        grad_mid[:, lanes] = picked[:middle]
-        grad_in[:, lanes] = picked[middle:]
-    out = jnp.sum(half[:, height:, :], axis=0) + jnp.sum(away[:, height:, :], axis=0)
-    grad_out[...] = out[: grad_out.shape[0]]
+
+    def put(source, owner):
+        for group in range(2):
+            first = group * (chips // 2)
+            lanes = slice((2 * owner + group) * 128, (2 * owner + group + 1) * 128)
+            for chip in range(chips // 2):
+                start = (first + chip) * height
+                block = source[start : start + height - 2, :]
+                row = chip * (height - 2)
+                if row + height - 2 <= middle:
+                    grad_mid[row : row + height - 2, lanes] = block
+                elif row >= middle:
+                    grad_in[row - middle : row - middle + height - 2, lanes] = block
+                else:
+                    grad_mid[row:, lanes] = block[: middle - row]
+                    grad_in[: row + height - 2 - middle, lanes] = block[middle - row :]
+        total = source[height - 2 : height, :]
+        for chip in range(1, chips):
+            total = total + source[(chip + 1) * height - 2 : (chip + 1) * height, :]
+        grad_out[2 * owner : 2 * owner + 2, :] = total
+
+    for owner in range(2):
+
+        @pl.when(place[CORE] == owner)
+        def _():
+            put(half, owner)
+            put(away, 1 - owner)
 
 
 VM = pltpu.VMEM
@@ -695,10 +720,11 @@
 
     height = hidden + inputs
     groups = hidden // 128
-    mine, other, grad_out = run(
+    mine, other, out_mine = run(
         gradient_kernel,
         "gradients",
-        [held(groups // 2, height, 128)] * 2 + [held(groups, 128)],
+        [held(groups // 2, height, 128), held(groups // 2 * height + 8, 128)]
+        + [held(groups // 2, 128)],
         place, slope, x_cos, x_sin, z_cos, z_sin, hidden_in, slope_mid, back, hidden_mid,
         limit=16,
         scratch=[VM((hidden, hidden), F32), VM((hidden, inputs), F32), VM((hidden, 128), F32)],
@@ -706,12 +732,15 @@
 
     chips = lax.axis_size(CHIPS)
     swap = [(0, 1), (1, 0)]
-    half = (mine + lax.ppermute(other, "c", swap)).reshape(chips, -1, 128)
+    swapped = lax.ppermute(other, "c", swap)
+    half = (mine.reshape(-1, 128) + swapped[:-8]).reshape(chips, -1, 128)
     parts = lax.all_to_all(half, CHIPS, 0, 0)
+    tall = half.shape[1] + groups // 2
     (shares,) = run(
-        share_kernel, "share", [held(chips, half.shape[1] + 2 * groups, 128)], place, parts, grad_out
-    )
-    half = lax.all_to_all(shares, CHIPS, 0, 0)
+        share_kernel, "share", [held(chips * tall, 128)], place, parts, out_mine, swapped
+    )
+    half = lax.all_to_all(shares.reshape(chips, tall, 1, 128), CHIPS, 0, 0)
+    half = half.reshape(chips * tall, 128)
     away = lax.ppermute(half, "c", swap)
     grad_in, grad_mid, grad_out = run(
         finish_kernel,

time: 118 us -> 115 us (0.975)
  blocking collectives: 55.3 us -> 53.5 us
    all_to_all x1, blocking collectives: 20.8 us -> 18.9 us  [on_device(): half = lax.all_to_all(shares.reshape(chips, tall, 1, 128), CHIPS, 0, 0)]
where the time goes in v5:
time: 115 us
  blocking collectives  53.5 us (47%)
  Pallas kernels  40.1 us (35%)
  starting transfers between devices  15.1 us (13%)
  waiting for transfers between devices  5.53 us (5%)
    pallas_call x10, Pallas kernels, run(): pl.pallas_call(kernel, name=name, in_specs=[SCALARS] * scalars + [WHOLE]...  40.1 us
    all_to_all x1, blocking collectives, on_device(): parts = lax.all_to_all(half, CHIPS, 0, 0)  19 us
    all_to_all x1, blocking collectives, on_device(): half = lax.all_to_all(shares.reshape(chips, tall, 1, 128), CHIPS, 0, 0)  18.9 us
    all_to_all x1, blocking collectives, gathered(): return lax.all_to_all(sent, CHIPS, 0, 0)  15.6 us
    ppermute x4, starting transfers between devices, shifted(): lax.ppermute(block, axis, [(i, (i + distance) % size) for i in range(size)])  6.94 us
    ppermute x1, starting transfers between devices, on_device(): away = lax.ppermute(half, 'c', swap)  3.32 us
    ppermute x1, starting transfers between devices, gathered(): chip = values + lax.ppermute(values, 'c', [(0, 1), (1, 0)])  3.14 us
  transfers between devices with their start and end apart: 7, of which 4 were waited for; matrix products, arithmetic and copies ran while one was open for 0% of the time, Pallas kernels for 11%

profile of v5, /device:TPU:1, one launch (start us, length us, event | category | flops | bytes accessed | tf_op | source)
XLA Modules:
  0.0 115.2 jit_solution(16007752900122643065)
XLA Ops:
  0.7 2.6 %prepare.1 = (f32[4,4,8,256]{3,2,1,0:T(8,128)S(1)}, f32[8,128,4]{2,1,0:T(8,128)S(1)}, f32[8,128,4]{2,1,0:T(8,128)S(1)}, f32[128,256]{1,0:T(8,128)S(1)}, f32[128,...) custom-call(s32[8]{0:T(128)S(1)} %stack.47.place, ...), custom_call_target="tpu_custom_call" | custom-call | tf_op jit(solution)/shard_map/prepare/pallas_call | solution.py:586
  3.3 7.3 %outer.1 = (f32[4,4,256]{2,1,0:T(4,128)S(1)}, f32[20,3,256]{2,1,0:T(4,128)S(1)}, f32[20,2,256]{2,1,0:T(2,128)S(1)}, bf16[512,8192]{1,0:T(8,128)(2,1)S(1)}, bf16[...) custom-call(f32[8,128,4]{2,1,0:T(8,128)S(1)} %get-tuple-element.47.x_cos, ...), custom_call_target="tpu_custom_call" | custom-call | flops 3221225472 | bytes 16777216 | tf_op jit(solution)/shard_map/outer/pallas_call | solution.py:586
  10.7 2.5 %collective-permute-start.1 = (f32[20,2,256]{2,1,0:T(2,128)S(1)}, f32[20,2,256]{2,1,0:T(2,128)S(1)}, u32[]{:S(2)}, u32[]{:S(2)}) collective-permute-start(f32[20,2,256]{2,1,0:T(2,128)S(1)} %get-tuple-element.62), channel_id=1, source_target_pairs={{0,1},{1,2},{2,3},{3,0},{4,5},{5,6},{6,7},{7,4},{8,9},{9,10},{10,1... | collective-permute-start | bytes 122888 | tf_op jit(solution)/shard_map/ppermute | solution.py:600
  13.2 2.2 %collective-permute-start = (f32[20,3,256]{2,1,0:T(4,128)S(1)}, f32[20,3,256]{2,1,0:T(4,128)S(1)}, u32[]{:S(2)}, u32[]{:S(2)}) collective-permute-start(f32[20,3,256]{2,1,0:T(4,128)S(1)} %get-tuple-element.61), channel_id=1, source_target_pairs={{0,3},{1,0},{2,1},{3,2},{4,7},{5,4},{6,5},{7,6},{8,11},{9,8},{10,9... | collective-permute-start | bytes 184328 | tf_op jit(solution)/shard_map/ppermute | solution.py:600
  15.4 7.3 %inner.1 = (f32[4,8,256]{2,1,0:T(8,128)S(1)}, f32[4,8,256]{2,1,0:T(8,128)S(1)}, bf16[512,8192]{1,0:T(8,128)(2,1)S(1)}, bf16[512,8192]{1,0:T(8,128)(2,1)S(1)}, bf...) custom-call(f32[8,128,4]{2,1,0:T(8,128)S(1)} %get-tuple-element.47.x, ...), custom_call_target="tpu_custom_call", output_to_operand_aliasing={{2}: (9, {}), {3}: (10, {}), {4}: (11, {}), {5}: (12, {})} | custom-call | flops 3221225472 | bytes 16777216 | tf_op jit(solution)/shard_map/inner/pallas_call | solution.py:586
  22.8 0.6 join.1
  23.4 2.2 %collective-permute-start.3 = (f32[10,16,256]{2,1,0:T(8,128)S(1)}, f32[10,16,256]{2,1,0:T(8,128)S(1)}, u32[]{:S(2)}, u32[]{:S(2)}) collective-permute-start(f32[10,16,256]{2,1,0:T(8,128)S(1)} %get-tuple-element.66), channel_id=1, source_target_pairs={{0,4},{4,8},{8,12},{12,16},{16,20},{20,24},{24,28},{28,32},{32,36}... | collective-permute-start | bytes 491528 | tf_op jit(solution)/shard_map/ppermute | solution.py:600
  25.6 4.9 %back.1 = (bf16[512,8192]{1,0:T(8,128)(2,1)S(1)}, f32[8,128]{1,0:T(8,128)S(1)}) custom-call(bf16[512,512]{1,0:T(8,128)(2,1)S(1)} %get-tuple-element.68.w_mid, bf16[512,8192]{1,0:T(8,128)(2,1)S(1)} %get-tuple-element.69.slope_mid, bf16[512,8192]{1,0:T(8,128)(2,1)S(1)} %get-tuple-element.70.slope_in), custom_call_target="tpu_custom_call", output_to_operand_aliasing={{0}: (2, {})} | custom-call | flops 4294967296 | bytes 25165824 | tf_op jit(solution)/shard_map/back/pallas_call | solution.py:586
  30.6 0.8 collective-permute-done.2.ahead
  31.3 2.7 %krylov.1 = (f32[3,5,16,256]{3,2,1,0:T(8,128)S(1)}, f32[3,5,16,256]{3,2,1,0:T(8,128)S(1)}, f32[1,128]{1,0:T(1,128)S(1)}) custom-call(s32[8]{0:T(128)S(1)} %stack.47.place, f32[4,4,16,256]{3,2,1,0:T(8,128)S(1)} %get-tuple-element.63.loads, f32[4,16,256]{2,1,0:T(8,128)S(1)} %get-tuple-element.64.stiff, f32[14,16,256]{2,1,0:T(8,128)S(1)} %collective-permute-done.2.ahead, ...), custom_call_target="tpu_custom_call" | custom-call | tf_op jit(solution)/shard_map/krylov/pallas_call | solution.py:586
  34.0 3.1 %collective-permute-start.4 = (f32[1,128]{1,0:T(1,128)S(1)}, f32[1,128]{1,0:T(1,128)S(1)}, u32[]{:S(2)}, u32[]{:S(2)}) collective-permute-start(f32[1,128]{1,0:T(1,128)S(1)} %get-tuple-element.72), channel_id=1, source_target_pairs={{0,4},{4,0},{1,5},{5,1},{2,6},{6,2},{3,7},{7,3},{8,12},{12,8},{9,1... | collective-permute-start | bytes 1544 | tf_op jit(solution)/shard_map/ppermute | solution.py:604
  37.1 0.8 collective-permute-done.4
  38.0 15.6 %all_to_all.15.sums = f32[64,1,128]{2,1,0:T(1,128)S(1)} all-to-all(f32[64,1,128]{2,1,0:T(1,128)S(1)} %broadcast_in_dim.9), channel_id=1, replica_groups=mesh['x'=4,'y'=4,'c'=2,'z'=4] {'x','y','z'}, dimensions={0} | all-to-all | bytes 65536 | tf_op jit(solution)/shard_map/all_to_all | solution.py:606
  53.6 1.5 %energy.1 = (f32[3,4,8,256]{3,2,1,0:T(8,128)}, f32[4,8,256]{2,1,0:T(8,128)S(1)}, f32[4,8,256]{2,1,0:T(8,128)}) custom-call(s32[8]{0:T(128)S(1)} %stack.47.place, f32[64,1,128]{2,1,0:T(1,128)S(1)} %all_to_all.15.sums, f32[4,4,16,256]{3,2,1,0:T(8,128)S(1)} %get-tuple-element.63.loads, f32[14,16,256]{2,1,0:T(8,128)S(1)} %collective-permute-done.2.ahead, ...), custom_call_target="tpu_custom_call" | custom-call | tf_op jit(solution)/shard_map/energy/pallas_call | solution.py:586
  55.0 10.5 %gradients.1 = (f32[2,768,128]{2,1,0:T(8,128)S(1)}, f32[1544,128]{1,0:T(8,128)S(1)}, f32[2,128]{1,0:T(2,128)S(1)}) custom-call(s32[8]{0:T(128)S(1)} %stack.47.place, f32[4,8,256]{2,1,0:T(8,128)S(1)} %get-tuple-element.77.slope, f32[8,128,4]{2,1,0:T(8,128)S(1)} %get-tuple-element.47.x_cos, f32[8,128,4]{2,1,0:T(8,128)S(1)} %get-tuple-element.48.x_sin, ...), custom_call_target="tpu_custom_call" | custom-call | tf_op jit(solution)/shard_map/gradients/pallas_call | solution.py:586
  65.5 1.7 %collective-permute-start.5 = (f32[1544,128]{1,0:T(8,128)S(1)}, f32[1544,128]{1,0:T(8,128)S(1)}, u32[]{:S(2)}, u32[]{:S(2)}) collective-permute-start(f32[1544,128]{1,0:T(8,128)S(1)} %get-tuple-element.82), channel_id=1, source_target_pairs={{0,4},{4,0},{1,5},{5,1},{2,6},{6,2},{3,7},{7,3},{8,12},{12,8},{9,1... | collective-permute-start | bytes 2371592 | tf_op jit(solution)/shard_map/ppermute | solution.py:735
  67.2 1.9 %collective-permute-done.5.swapped = f32[1544,128]{1,0:T(8,128)S(1)} collective-permute-done((f32[1544,128]{1,0:T(8,128)S(1)}, f32[1544,128]{1,0:T(8,128)S(1)}, u32[]{:S(2)}, u32[]{:S(2)}) %collective-permute-start.5) | collective-permute-done | bytes 790560 | tf_op jit(solution)/shard_map/ppermute | solution.py:735
  69.2 0.1 slice_add_fusion
  69.3 19.0 %all_to_all.16.parts = f32[64,24,128]{2,1,0:T(8,128)S(1)} all-to-all(f32[64,24,128]{2,1,0:T(8,128)S(1)} %bitcast.18), channel_id=1, replica_groups=mesh['x'=4,'y'=4,'c'=2,'z'=4] {'x','y','z'}, dimensions={0} | all-to-all | bytes 1572864 | tf_op jit(solution)/shard_map/all_to_all | solution.py:737
  88.3 0.7 share.1
  89.0 18.9 %all_to_all.17 = f32[64,26,1,128]{3,2,1,0:T(1,128)S(1)} all-to-all(f32[64,26,1,128]{3,2,1,0:T(1,128)S(1)} %bitcast.17), channel_id=1, replica_groups=mesh['x'=4,'y'=4,'c'=2,'z'=4] {'x','y','z'}, dimensions={0} | all-to-all | bytes 1703936 | tf_op jit(solution)/shard_map/all_to_all | solution.py:742
  107.9 3.3 %collective-permute-start.6 = (f32[1664,128]{1,0:T(8,128)S(1)}, f32[1664,128]{1,0:T(8,128)S(1)}, u32[]{:S(2)}, u32[]{:S(2)}) collective-permute-start(f32[1664,128]{1,0:T(8,128)S(1)} %bitcast.15), channel_id=1, source_target_pairs={{0,4},{4,0},{1,5},{5,1},{2,6},{6,2},{3,7},{7,3},{8,12},{12,8},{9,1... | collective-permute-start | bytes 2555912 | tf_op jit(solution)/shard_map/ppermute | solution.py:744
  111.2 2.0 %collective-permute-done.6.away = f32[1664,128]{1,0:T(8,128)S(1)} collective-permute-done((f32[1664,128]{1,0:T(8,128)S(1)}, f32[1664,128]{1,0:T(8,128)S(1)}, u32[]{:S(2)}, u32[]{:S(2)}) %collective-permute-start.6) | collective-permute-done | bytes 852000 | tf_op jit(solution)/shard_map/ppermute | solution.py:744
  113.2 2.0 %finish.1 = (f32[256,512]{1,0:T(8,128)}, f32[512,512]{1,0:T(8,128)}, f32[4,128]{1,0:T(4,128)}) custom-call(s32[8]{0:T(128)S(1)} %stack.47.place, f32[1664,128]{1,0:T(8,128)S(1)} %bitcast.16, f32[1664,128]{1,0:T(8,128)S(1)} %collective-permute-done.6.away), custom_call_target="tpu_custom_call" | custom-call | tf_op jit(solution)/shard_map/finish/pallas_call | solution.py:586
  (7 shorter events, 0.1 us)
Async XLA Ops:
  10.7 12.1 %collective-permute-start.1 = (f32[20,2,256]{2,1,0:T(2,128)S(1)}, f32[20,2,256]{2,1,0:T(2,128)S(1)}, u32[]{:S(2)}, u32[]{:S(2)}) collective-permute-start(f32[20,2,256]{2,1,0:T(2,128)S(1)} %get-tuple-element.62), channel_id=1, source_target_pairs={{0,1},{1,2},{2,3},{3,0},{4,5},{5,6},{6,7},{7,4},{8,9},{9,10},{10,1... | collective-permute-start | bytes 122888 | tf_op jit(solution)/shard_map/ppermute | solution.py:600
  13.2 9.6 %collective-permute-start = (f32[20,3,256]{2,1,0:T(4,128)S(1)}, f32[20,3,256]{2,1,0:T(4,128)S(1)}, u32[]{:S(2)}, u32[]{:S(2)}) collective-permute-start(f32[20,3,256]{2,1,0:T(4,128)S(1)} %get-tuple-element.61), channel_id=1, source_target_pairs={{0,3},{1,0},{2,1},{3,2},{4,7},{5,4},{6,5},{7,6},{8,11},{9,8},{10,9... | collective-permute-start | bytes 184328 | tf_op jit(solution)/shard_map/ppermute | solution.py:600
  23.4 7.2 %collective-permute-start.3 = (f32[10,16,256]{2,1,0:T(8,128)S(1)}, f32[10,16,256]{2,1,0:T(8,128)S(1)}, u32[]{:S(2)}, u32[]{:S(2)}) collective-permute-start(f32[10,16,256]{2,1,0:T(8,128)S(1)} %get-tuple-element.66), channel_id=1, source_target_pairs={{0,4},{4,8},{8,12},{12,16},{16,20},{20,24},{24,28},{28,32},{32,36}... | collective-permute-start | bytes 491528 | tf_op jit(solution)/shard_map/ppermute | solution.py:600
  25.6 5.7 %collective-permute-start.2 = (f32[14,16,256]{2,1,0:T(8,128)S(1)}, f32[14,16,256]{2,1,0:T(8,128)S(1)}, u32[]{:S(2)}, u32[]{:S(2)}) collective-permute-start(f32[14,16,256]{2,1,0:T(8,128)S(1)} %get-tuple-element.65), channel_id=1, source_target_pairs={{0,124},{4,0},{8,4},{12,8},{16,12},{20,16},{24,20},{28,24},{32,28}... | collective-permute-start | bytes 688136 | tf_op jit(solution)/shard_map/ppermute | solution.py:600
  34.0 4.0 %collective-permute-start.4 = (f32[1,128]{1,0:T(1,128)S(1)}, f32[1,128]{1,0:T(1,128)S(1)}, u32[]{:S(2)}, u32[]{:S(2)}) collective-permute-start(f32[1,128]{1,0:T(1,128)S(1)} %get-tuple-element.72), channel_id=1, source_target_pairs={{0,4},{4,0},{1,5},{5,1},{2,6},{6,2},{3,7},{7,3},{8,12},{12,8},{9,1... | collective-permute-start | bytes 1544 | tf_op jit(solution)/shard_map/ppermute | solution.py:604
  65.5 3.6 %collective-permute-start.5 = (f32[1544,128]{1,0:T(8,128)S(1)}, f32[1544,128]{1,0:T(8,128)S(1)}, u32[]{:S(2)}, u32[]{:S(2)}) collective-permute-start(f32[1544,128]{1,0:T(8,128)S(1)} %get-tuple-element.82), channel_id=1, source_target_pairs={{0,4},{4,0},{1,5},{5,1},{2,6},{6,2},{3,7},{7,3},{8,12},{12,8},{9,1... | collective-permute-start | bytes 2371592 | tf_op jit(solution)/shard_map/ppermute | solution.py:735
  107.9 5.3 %collective-permute-start.6 = (f32[1664,128]{1,0:T(8,128)S(1)}, f32[1664,128]{1,0:T(8,128)S(1)}, u32[]{:S(2)}, u32[]{:S(2)}) collective-permute-start(f32[1664,128]{1,0:T(8,128)S(1)} %bitcast.15), channel_id=1, source_target_pairs={{0,4},{4,0},{1,5},{5,1},{2,6},{6,2},{3,7},{7,3},{8,12},{12,8},{9,1... | collective-permute-start | bytes 2555912 | tf_op jit(solution)/shard_map/ppermute | solution.py:744

commit v6 on v5

--- a/solution.py
+++ b/solution.py
@@ -81,6 +81,21 @@
     return blocks
 
 
+def connected(block, used):
+    parts = []
+    for d in used:
+        for part in parts:
+            if block[d, part[0]] != 0.0:
+                part.append(d)
+                break
+        else:
+            parts.append([d])
+    for part in parts:
+        pairs = [block[i, j] for i in part for j in part if i != j]
+        assert np.ptp(pairs) < 1e-9 if pairs else True
+    return parts
+
+
 BLOCKS = modal_stiffness()
 
 
@@ -112,15 +127,26 @@
 
 def modal_forces(modes):
     for waves, block in BLOCKS:
-        values = [modes[d][waves[d]] for d in range(3)]
-        for d in range(3):
-            total = None
-            for other in range(3):
-                if block[d, other] != 0.0:
-                    term = np.float32(block[d, other]) * values[other]
-                    total = term if total is None else total + term
-            if total is not None:
-                yield d, waves[d], values[d], total
+        used = [d for d in range(3) if np.any(block[d] != 0.0)]
+        for part in connected(block, used):
+            values = [modes[d][waves[d]] for d in part]
+            if len(part) == 1:
+                forces = [np.float32(block[part[0], part[0]]) * values[0]]
+            else:
+                common = block[part[0], part[1]]
+                total = values[0] + values[1]
+                for value in values[2:]:
+                    total = total + value
+                shared = np.float32(common) * total
+                forces = []
+                for d, value in zip(part, values):
+                    extra = block[d, d] - common
+                    if abs(extra) > 1e-9:
+                        forces.append(shared + np.float32(extra) * value)
+                    else:
+                        forces.append(shared)
+            for d, value, force in zip(part, values, forces):
+                yield d, waves[d], value, force
 
 
 def energy_of(modes):
@@ -306,7 +332,14 @@
 def prepare_kernel(
     grid_cells, place, load_values, load_mask, fixed_mask, frequencies, w_in, w_mid, w_out,
     loads, x_cos, x_sin, z_cos, z_sin, w_in_t, w_mid_t, w_mid_half, w_column, w_row,
+    w_in_here, w_mid_here, arrived,
 ):
+    copies = [
+        pltpu.make_async_copy(w_in, w_in_here, arrived.at[0]),
+        pltpu.make_async_copy(w_mid, w_mid_here, arrived.at[1]),
+    ]
+    for copy in copies:
+        copy.start()
     cells, rows, size = load_mask.shape
     free = (1 - fixed_mask[...]).astype(F32)
     held = free * load_mask[...].astype(F32)
@@ -331,13 +364,15 @@
     phase = two_pi * (((z_number.astype(F32) + 0.5) / grid_cells[2]) * columns[2])
     z_cos[...] = jnp.cos(phase)
     z_sin[...] = jnp.sin(phase)
-    w_in_t[...] = (0.5 * w_in[...].astype(F32)).T.astype(BF)
-    middle = 0.5 * w_mid[...].astype(F32)
-    w_mid_half[...] = middle.astype(BF)
-    w_mid_t[...] = middle.T.astype(BF)
     line = w_out[...].astype(F32)[None, :]
     w_column[...] = 0.5 * column_of(line)
     w_row[...] = jnp.broadcast_to(line, w_row.shape).astype(BF)
+    for copy in copies:
+        copy.wait()
+    w_in_t[...] = (0.5 * w_in_here[...].astype(F32)).T.astype(BF)
+    middle = 0.5 * w_mid_here[...].astype(F32)
+    w_mid_half[...] = middle.astype(BF)
+    w_mid_t[...] = middle.T.astype(BF)
 
 
 def join_kernel(place, loads, stiff, ahead, behind, loads_16, stiff_16, to_before, to_next):
@@ -475,15 +510,16 @@
         line = jnp.concatenate(lines, 1)
         span = slice(p * rows * size, (p + 1) * rows * size)
         hidden = (hidden_in[:, span].astype(F32) * line).astype(BF)
-        product = hidden_mid[:, span].astype(F32) * line
-        total = product[:, :128]
-        for k in range(1, rows * size // 128):
-            total = total + product[:, k * 128 : (k + 1) * 128]
         terms = (
             lax.dot_general(hidden, slope_mid[:, span], LAST, preferred_element_type=F32),
             lax.dot_general(back[:, span], features, LAST, preferred_element_type=F32),
-            total,
         )
+        total = None
+        for k in range(rows * size // 128):
+            lanes = slice(p * rows * size + k * 128, p * rows * size + (k + 1) * 128)
+            term = hidden_mid[:, lanes].astype(F32) * line[:, k * 128 : (k + 1) * 128]
+            total = term if total is None else total + term
+        terms = terms + (total,)
         for held, term in zip((mid, first, running), terms):
             if p == 0:
                 held[...] = term
@@ -530,42 +566,61 @@
         shares[chip * height : (chip + 1) * height, :] = block
 
 
-def finish_kernel(place, half, away, grad_in, grad_mid, grad_out):
+def finish_kernel(place, half, away, grad_in, grad_mid, grad_out, filled, sent):
     height = 26
+    count = height - 2
     chips = half.shape[0] // height
-    middle = grad_mid.shape[0]
-
-    def put(source, owner):
+    middle, total_rows = grad_mid.shape[0], filled.shape[0]
+    some = 8
+
+    def put(source, owner, start):
         for group in range(2):
-            first = group * (chips // 2)
             lanes = slice((2 * owner + group) * 128, (2 * owner + group + 1) * 128)
-            for chip in range(chips // 2):
-                start = (first + chip) * height
-                block = source[start : start + height - 2, :]
-                row = chip * (height - 2)
-                if row + height - 2 <= middle:
-                    grad_mid[row : row + height - 2, lanes] = block
-                elif row >= middle:
-                    grad_in[row - middle : row - middle + height - 2, lanes] = block
-                else:
-                    grad_mid[row:, lanes] = block[: middle - row]
-                    grad_in[: row + height - 2 - middle, lanes] = block[middle - row :]
-        total = source[height - 2 : height, :]
+            for chip in range(start, start + some):
+                at = (group * (chips // 2) + chip) * height
+                filled[chip * count : (chip + 1) * count, lanes] = source[at : at + count, :]
+
+    def put_out(source, owner):
+        total = source[count:height, :]
         for chip in range(1, chips):
-            total = total + source[(chip + 1) * height - 2 : (chip + 1) * height, :]
+            total = total + source[chip * height + count : (chip + 1) * height, :]
         grad_out[2 * owner : 2 * owner + 2, :] = total
 
+    copies = []
+    for start in range(0, chips // 2, some):
+        for owner in range(2):
+
+            @pl.when(place[CORE] == owner)
+            def _():
+                put(half, owner, start)
+                put(away, 1 - owner, start)
+
+        low, high = start * count, (start + some) * count
+        for target, first, last in ((grad_mid, 0, middle), (grad_in, middle, total_rows)):
+            begin, end = max(low, first), min(high, last)
+            if begin < end:
+                copy = pltpu.make_async_copy(
+                    filled.at[begin:end, :],
+                    target.at[begin - first : end - first, :],
+                    sent.at[len(copies)],
+                )
+                copy.start()
+                copies.append(copy)
     for owner in range(2):
 
         @pl.when(place[CORE] == owner)
         def _():
-            put(half, owner)
-            put(away, 1 - owner)
+            put_out(half, owner)
+            put_out(away, 1 - owner)
+
+    for copy in copies:
+        copy.wait()
 
 
 VM = pltpu.VMEM
 WHOLE = pl.BlockSpec(memory_space=pltpu.VMEM)
 SCALARS = pl.BlockSpec(memory_space=pltpu.SMEM)
+FAR = pl.BlockSpec(memory_space=pltpu.HBM)
 X_FIRST, Y_FIRST, CORE, SLAB_FIRST, SLAB_LAST, Z_FIRST, Z_LAST = range(7)
 
 
@@ -581,13 +636,17 @@
     return VM(shape, dtype)
 
 
-def run(kernel, name, out_shape, *operands, scalars=1, space=pltpu.VMEM, scratch=(), limit=16, **more):
+def run(
+    kernel, name, out_shape, *operands,
+    scalars=1, space=pltpu.VMEM, scratch=(), limit=16, far_in=(), far_out=(), **more,
+):
     arrays = [pltpu.with_memory_space_constraint(array, space) for array in operands[scalars:]]
     return pl.pallas_call(
         kernel,
         name=name,
-        in_specs=[SCALARS] * scalars + [WHOLE] * len(arrays),
-        out_specs=[WHOLE] * len(out_shape),
+        in_specs=[SCALARS] * scalars
+        + [FAR if k in far_in else WHOLE for k in range(len(arrays))],
+        out_specs=[FAR if k in far_out else WHOLE for k in range(len(out_shape))],
         out_shape=out_shape,
         scratch_shapes=list(scratch),
         compiler_params=params(limit),
@@ -641,7 +700,10 @@
             held(16, hidden, dtype=BF),
         ],
         place, load_values, load_mask, fixed_mask, frequencies, weight_in, weight_mid,
-        weight_out, space=pltpu.HBM,
+        weight_out, space=pltpu.HBM, far_in=(4, 5),
+        scratch=[
+            VM((inputs, hidden), BF), VM((hidden, hidden), BF), pltpu.SemaphoreType.DMA((2,)),
+        ],
     )
 
     network = (x_cos, x_sin, z_cos, z_sin, w_in_t, w_mid_t, w_column, w_row)
@@ -747,6 +809,8 @@
         "finish",
         [shaped(inputs, hidden), shaped(hidden, hidden), shaped(groups, 128)],
         place, half, away,
+        far_out=(0, 1),
+        scratch=[VM((height, hidden), F32), pltpu.SemaphoreType.DMA((5,))],
     )
     return solution, density, grad_in, grad_mid, grad_out.reshape(hidden)
 

time: 115 us -> 117 us (1.017)
  Pallas kernels: 40.1 us -> 41.8 us
    pallas_call x10, Pallas kernels: 40.1 us -> 41.8 us  [run(): pl.pallas_call(kernel, name=name, in_specs=[SCALARS] * scalars + [FAR if...]
  transfers between devices with their start and end apart: 7 -> 7, of which waited for: 4 -> 4; matrix products, arithmetic and copies ran while one was open for 0% -> 0% of each run, Pallas kernels for 11% -> 10%
where the time goes in v6:
time: 117 us
  blocking collectives  53.5 us (46%)
  Pallas kernels  41.8 us (36%)
  starting transfers between devices  15.1 us (13%)
  waiting for transfers between devices  5.53 us (5%)
    pallas_call x10, Pallas kernels, run(): pl.pallas_call(kernel, name=name, in_specs=[SCALARS] * scalars + [FAR if...  41.8 us
    all_to_all x1, blocking collectives, on_device(): parts = lax.all_to_all(half, CHIPS, 0, 0)  19 us
    all_to_all x1, blocking collectives, on_device(): half = lax.all_to_all(shares.reshape(chips, tall, 1, 128), CHIPS, 0, 0)  18.9 us
    all_to_all x1, blocking collectives, gathered(): return lax.all_to_all(sent, CHIPS, 0, 0)  15.6 us
    ppermute x4, starting transfers between devices, shifted(): lax.ppermute(block, axis, [(i, (i + distance) % size) for i in range(size)])  6.95 us
    ppermute x1, starting transfers between devices, on_device(): away = lax.ppermute(half, 'c', swap)  3.32 us
    ppermute x1, starting transfers between devices, gathered(): chip = values + lax.ppermute(values, 'c', [(0, 1), (1, 0)])  3.14 us
  transfers between devices with their start and end apart: 7, of which 4 were waited for; matrix products, arithmetic and copies ran while one was open for 0% of the time, Pallas kernels for 10%

profile of v6, /device:TPU:1, one launch (start us, length us, event | category | flops | bytes accessed | tf_op | source)
XLA Modules:
  0.0 117.1 jit_solution(1010429030514834424)
XLA Ops:
  0.7 3.4 %prepare.1 = (f32[4,4,8,256]{3,2,1,0:T(8,128)S(1)}, f32[8,128,4]{2,1,0:T(8,128)S(1)}, f32[8,128,4]{2,1,0:T(8,128)S(1)}, f32[128,256]{1,0:T(8,128)S(1)}, f32[128,...) custom-call(s32[8]{0:T(128)S(1)} %stack.47.place, ...), custom_call_target="tpu_custom_call" | custom-call | tf_op jit(solution)/shard_map/prepare/pallas_call | solution.py:644
  4.1 7.3 %outer.1 = (f32[4,4,256]{2,1,0:T(4,128)S(1)}, f32[20,3,256]{2,1,0:T(4,128)S(1)}, f32[20,2,256]{2,1,0:T(2,128)S(1)}, bf16[512,8192]{1,0:T(8,128)(2,1)S(1)}, bf16[...) custom-call(f32[8,128,4]{2,1,0:T(8,128)S(1)} %get-tuple-element.47.x_cos, ...), custom_call_target="tpu_custom_call" | custom-call | flops 3221225472 | bytes 16777216 | tf_op jit(solution)/shard_map/outer/pallas_call | solution.py:644
  11.4 2.5 %collective-permute-start.1 = (f32[20,2,256]{2,1,0:T(2,128)S(1)}, f32[20,2,256]{2,1,0:T(2,128)S(1)}, u32[]{:S(2)}, u32[]{:S(2)}) collective-permute-start(f32[20,2,256]{2,1,0:T(2,128)S(1)} %get-tuple-element.62), channel_id=1, source_target_pairs={{0,1},{1,2},{2,3},{3,0},{4,5},{5,6},{6,7},{7,4},{8,9},{9,10},{10,1... | collective-permute-start | bytes 122888 | tf_op jit(solution)/shard_map/ppermute | solution.py:659
  14.0 2.2 %collective-permute-start = (f32[20,3,256]{2,1,0:T(4,128)S(1)}, f32[20,3,256]{2,1,0:T(4,128)S(1)}, u32[]{:S(2)}, u32[]{:S(2)}) collective-permute-start(f32[20,3,256]{2,1,0:T(4,128)S(1)} %get-tuple-element.61), channel_id=1, source_target_pairs={{0,3},{1,0},{2,1},{3,2},{4,7},{5,4},{6,5},{7,6},{8,11},{9,8},{10,9... | collective-permute-start | bytes 184328 | tf_op jit(solution)/shard_map/ppermute | solution.py:659
  16.2 7.3 %inner.1 = (f32[4,8,256]{2,1,0:T(8,128)S(1)}, f32[4,8,256]{2,1,0:T(8,128)S(1)}, bf16[512,8192]{1,0:T(8,128)(2,1)S(1)}, bf16[512,8192]{1,0:T(8,128)(2,1)S(1)}, bf...) custom-call(f32[8,128,4]{2,1,0:T(8,128)S(1)} %get-tuple-element.47.x, ...), custom_call_target="tpu_custom_call", output_to_operand_aliasing={{2}: (9, {}), {3}: (10, {}), {4}: (11, {}), {5}: (12, {})} | custom-call | flops 3221225472 | bytes 16777216 | tf_op jit(solution)/shard_map/inner/pallas_call | solution.py:644
  23.5 0.6 join.1
  24.1 2.2 %collective-permute-start.3 = (f32[10,16,256]{2,1,0:T(8,128)S(1)}, f32[10,16,256]{2,1,0:T(8,128)S(1)}, u32[]{:S(2)}, u32[]{:S(2)}) collective-permute-start(f32[10,16,256]{2,1,0:T(8,128)S(1)} %get-tuple-element.66), channel_id=1, source_target_pairs={{0,4},{4,8},{8,12},{12,16},{16,20},{20,24},{24,28},{28,32},{32,36}... | collective-permute-start | bytes 491528 | tf_op jit(solution)/shard_map/ppermute | solution.py:659
  26.3 4.9 %back.1 = (bf16[512,8192]{1,0:T(8,128)(2,1)S(1)}, f32[8,128]{1,0:T(8,128)S(1)}) custom-call(bf16[512,512]{1,0:T(8,128)(2,1)S(1)} %get-tuple-element.68.w_mid, bf16[512,8192]{1,0:T(8,128)(2,1)S(1)} %get-tuple-element.69.slope_mid, bf16[512,8192]{1,0:T(8,128)(2,1)S(1)} %get-tuple-element.70.slope_in), custom_call_target="tpu_custom_call", output_to_operand_aliasing={{0}: (2, {})} | custom-call | flops 4294967296 | bytes 25165824 | tf_op jit(solution)/shard_map/back/pallas_call | solution.py:644
  31.3 0.8 collective-permute-done.2.ahead
  32.1 2.6 %krylov.1 = (f32[3,5,16,256]{3,2,1,0:T(8,128)S(1)}, f32[3,5,16,256]{3,2,1,0:T(8,128)S(1)}, f32[1,128]{1,0:T(1,128)S(1)}) custom-call(s32[8]{0:T(128)S(1)} %stack.47.place, f32[4,4,16,256]{3,2,1,0:T(8,128)S(1)} %get-tuple-element.63.loads, f32[4,16,256]{2,1,0:T(8,128)S(1)} %get-tuple-element.64.stiff, f32[14,16,256]{2,1,0:T(8,128)S(1)} %collective-permute-done.2.ahead, ...), custom_call_target="tpu_custom_call" | custom-call | tf_op jit(solution)/shard_map/krylov/pallas_call | solution.py:644
  34.7 3.1 %collective-permute-start.4 = (f32[1,128]{1,0:T(1,128)S(1)}, f32[1,128]{1,0:T(1,128)S(1)}, u32[]{:S(2)}, u32[]{:S(2)}) collective-permute-start(f32[1,128]{1,0:T(1,128)S(1)} %get-tuple-element.72), channel_id=1, source_target_pairs={{0,4},{4,0},{1,5},{5,1},{2,6},{6,2},{3,7},{7,3},{8,12},{12,8},{9,1... | collective-permute-start | bytes 1544 | tf_op jit(solution)/shard_map/ppermute | solution.py:663
  37.8 0.8 collective-permute-done.4
  38.7 15.6 %all_to_all.15.sums = f32[64,1,128]{2,1,0:T(1,128)S(1)} all-to-all(f32[64,1,128]{2,1,0:T(1,128)S(1)} %broadcast_in_dim.9), channel_id=1, replica_groups=mesh['x'=4,'y'=4,'c'=2,'z'=4] {'x','y','z'}, dimensions={0} | all-to-all | bytes 65536 | tf_op jit(solution)/shard_map/all_to_all | solution.py:665
  54.2 1.5 %energy.1 = (f32[3,4,8,256]{3,2,1,0:T(8,128)}, f32[4,8,256]{2,1,0:T(8,128)S(1)}, f32[4,8,256]{2,1,0:T(8,128)}) custom-call(s32[8]{0:T(128)S(1)} %stack.47.place, f32[64,1,128]{2,1,0:T(1,128)S(1)} %all_to_all.15.sums, f32[4,4,16,256]{3,2,1,0:T(8,128)S(1)} %get-tuple-element.63.loads, f32[14,16,256]{2,1,0:T(8,128)S(1)} %collective-permute-done.2.ahead, ...), custom_call_target="tpu_custom_call" | custom-call | tf_op jit(solution)/shard_map/energy/pallas_call | solution.py:644
  55.7 11.2 %gradients.1 = (f32[2,768,128]{2,1,0:T(8,128)S(1)}, f32[1544,128]{1,0:T(8,128)S(1)}, f32[2,128]{1,0:T(2,128)S(1)}) custom-call(s32[8]{0:T(128)S(1)} %stack.47.place, f32[4,8,256]{2,1,0:T(8,128)S(1)} %get-tuple-element.77.slope, f32[8,128,4]{2,1,0:T(8,128)S(1)} %get-tuple-element.47.x_cos, f32[8,128,4]{2,1,0:T(8,128)S(1)} %get-tuple-element.48.x_sin, ...), custom_call_target="tpu_custom_call" | custom-call | tf_op jit(solution)/shard_map/gradients/pallas_call | solution.py:644
  66.9 1.7 %collective-permute-start.5 = (f32[1544,128]{1,0:T(8,128)S(1)}, f32[1544,128]{1,0:T(8,128)S(1)}, u32[]{:S(2)}, u32[]{:S(2)}) collective-permute-start(f32[1544,128]{1,0:T(8,128)S(1)} %get-tuple-element.82), channel_id=1, source_target_pairs={{0,4},{4,0},{1,5},{5,1},{2,6},{6,2},{3,7},{7,3},{8,12},{12,8},{9,1... | collective-permute-start | bytes 2371592 | tf_op jit(solution)/shard_map/ppermute | solution.py:797
  68.7 1.9 %collective-permute-done.5.swapped = f32[1544,128]{1,0:T(8,128)S(1)} collective-permute-done((f32[1544,128]{1,0:T(8,128)S(1)}, f32[1544,128]{1,0:T(8,128)S(1)}, u32[]{:S(2)}, u32[]{:S(2)}) %collective-permute-start.5) | collective-permute-done | bytes 790560 | tf_op jit(solution)/shard_map/ppermute | solution.py:797
  70.6 0.1 slice_add_fusion
  70.7 19.0 %all_to_all.16.parts = f32[64,24,128]{2,1,0:T(8,128)S(1)} all-to-all(f32[64,24,128]{2,1,0:T(8,128)S(1)} %bitcast.18), channel_id=1, replica_groups=mesh['x'=4,'y'=4,'c'=2,'z'=4] {'x','y','z'}, dimensions={0} | all-to-all | bytes 1572864 | tf_op jit(solution)/shard_map/all_to_all | solution.py:799
  89.7 0.7 share.1
  90.4 18.9 %all_to_all.17 = f32[64,26,1,128]{3,2,1,0:T(1,128)S(1)} all-to-all(f32[64,26,1,128]{3,2,1,0:T(1,128)S(1)} %bitcast.17), channel_id=1, replica_groups=mesh['x'=4,'y'=4,'c'=2,'z'=4] {'x','y','z'}, dimensions={0} | all-to-all | bytes 1703936 | tf_op jit(solution)/shard_map/all_to_all | solution.py:804
  109.3 3.3 %collective-permute-start.6 = (f32[1664,128]{1,0:T(8,128)S(1)}, f32[1664,128]{1,0:T(8,128)S(1)}, u32[]{:S(2)}, u32[]{:S(2)}) collective-permute-start(f32[1664,128]{1,0:T(8,128)S(1)} %bitcast.15), channel_id=1, source_target_pairs={{0,4},{4,0},{1,5},{5,1},{2,6},{6,2},{3,7},{7,3},{8,12},{12,8},{9,1... | collective-permute-start | bytes 2555912 | tf_op jit(solution)/shard_map/ppermute | solution.py:806
  112.6 2.0 %collective-permute-done.6.away = f32[1664,128]{1,0:T(8,128)S(1)} collective-permute-done((f32[1664,128]{1,0:T(8,128)S(1)}, f32[1664,128]{1,0:T(8,128)S(1)}, u32[]{:S(2)}, u32[]{:S(2)}) %collective-permute-start.6) | collective-permute-done | bytes 852000 | tf_op jit(solution)/shard_map/ppermute | solution.py:806
  114.6 2.4 %finish.1 = (f32[256,512]{1,0:T(8,128)}, f32[512,512]{1,0:T(8,128)}, f32[4,128]{1,0:T(4,128)}) custom-call(s32[8]{0:T(128)S(1)} %stack.47.place, f32[1664,128]{1,0:T(8,128)S(1)} %bitcast.16, f32[1664,128]{1,0:T(8,128)S(1)} %collective-permute-done.6.away), custom_call_target="tpu_custom_call" | custom-call | tf_op jit(solution)/shard_map/finish/pallas_call | solution.py:644
  (7 shorter events, 0.1 us)
Async XLA Ops:
  11.4 12.1 %collective-permute-start.1 = (f32[20,2,256]{2,1,0:T(2,128)S(1)}, f32[20,2,256]{2,1,0:T(2,128)S(1)}, u32[]{:S(2)}, u32[]{:S(2)}) collective-permute-start(f32[20,2,256]{2,1,0:T(2,128)S(1)} %get-tuple-element.62), channel_id=1, source_target_pairs={{0,1},{1,2},{2,3},{3,0},{4,5},{5,6},{6,7},{7,4},{8,9},{9,10},{10,1... | collective-permute-start | bytes 122888 | tf_op jit(solution)/shard_map/ppermute | solution.py:659
  14.0 9.6 %collective-permute-start = (f32[20,3,256]{2,1,0:T(4,128)S(1)}, f32[20,3,256]{2,1,0:T(4,128)S(1)}, u32[]{:S(2)}, u32[]{:S(2)}) collective-permute-start(f32[20,3,256]{2,1,0:T(4,128)S(1)} %get-tuple-element.61), channel_id=1, source_target_pairs={{0,3},{1,0},{2,1},{3,2},{4,7},{5,4},{6,5},{7,6},{8,11},{9,8},{10,9... | collective-permute-start | bytes 184328 | tf_op jit(solution)/shard_map/ppermute | solution.py:659
  24.1 7.2 %collective-permute-start.3 = (f32[10,16,256]{2,1,0:T(8,128)S(1)}, f32[10,16,256]{2,1,0:T(8,128)S(1)}, u32[]{:S(2)}, u32[]{:S(2)}) collective-permute-start(f32[10,16,256]{2,1,0:T(8,128)S(1)} %get-tuple-element.66), channel_id=1, source_target_pairs={{0,4},{4,8},{8,12},{12,16},{16,20},{20,24},{24,28},{28,32},{32,36}... | collective-permute-start | bytes 491528 | tf_op jit(solution)/shard_map/ppermute | solution.py:659
  26.3 5.7 %collective-permute-start.2 = (f32[14,16,256]{2,1,0:T(8,128)S(1)}, f32[14,16,256]{2,1,0:T(8,128)S(1)}, u32[]{:S(2)}, u32[]{:S(2)}) collective-permute-start(f32[14,16,256]{2,1,0:T(8,128)S(1)} %get-tuple-element.65), channel_id=1, source_target_pairs={{0,124},{4,0},{8,4},{12,8},{16,12},{20,16},{24,20},{28,24},{32,28}... | collective-permute-start | bytes 688136 | tf_op jit(solution)/shard_map/ppermute | solution.py:659
  34.7 4.0 %collective-permute-start.4 = (f32[1,128]{1,0:T(1,128)S(1)}, f32[1,128]{1,0:T(1,128)S(1)}, u32[]{:S(2)}, u32[]{:S(2)}) collective-permute-start(f32[1,128]{1,0:T(1,128)S(1)} %get-tuple-element.72), channel_id=1, source_target_pairs={{0,4},{4,0},{1,5},{5,1},{2,6},{6,2},{3,7},{7,3},{8,12},{12,8},{9,1... | collective-permute-start | bytes 1544 | tf_op jit(solution)/shard_map/ppermute | solution.py:663
  66.9 3.6 %collective-permute-start.5 = (f32[1544,128]{1,0:T(8,128)S(1)}, f32[1544,128]{1,0:T(8,128)S(1)}, u32[]{:S(2)}, u32[]{:S(2)}) collective-permute-start(f32[1544,128]{1,0:T(8,128)S(1)} %get-tuple-element.82), channel_id=1, source_target_pairs={{0,4},{4,0},{1,5},{5,1},{2,6},{6,2},{3,7},{7,3},{8,12},{12,8},{9,1... | collective-permute-start | bytes 2371592 | tf_op jit(solution)/shard_map/ppermute | solution.py:797
  109.3 5.3 %collective-permute-start.6 = (f32[1664,128]{1,0:T(8,128)S(1)}, f32[1664,128]{1,0:T(8,128)S(1)}, u32[]{:S(2)}, u32[]{:S(2)}) collective-permute-start(f32[1664,128]{1,0:T(8,128)S(1)} %bitcast.15), channel_id=1, source_target_pairs={{0,4},{4,0},{1,5},{5,1},{2,6},{6,2},{3,7},{7,3},{8,12},{12,8},{9,1... | collective-permute-start | bytes 2555912 | tf_op jit(solution)/shard_map/ppermute | solution.py:806

commit v7 on v5

--- a/solution.py
+++ b/solution.py
@@ -81,6 +81,21 @@
     return blocks
 
 
+def connected(block, used):
+    parts = []
+    for d in used:
+        for part in parts:
+            if block[d, part[0]] != 0.0:
+                part.append(d)
+                break
+        else:
+            parts.append([d])
+    for part in parts:
+        pairs = [block[i, j] for i in part for j in part if i != j]
+        assert np.ptp(pairs) < 1e-9 if pairs else True
+    return parts
+
+
 BLOCKS = modal_stiffness()
 
 
@@ -112,15 +127,26 @@
 
 def modal_forces(modes):
     for waves, block in BLOCKS:
-        values = [modes[d][waves[d]] for d in range(3)]
-        for d in range(3):
-            total = None
-            for other in range(3):
-                if block[d, other] != 0.0:
-                    term = np.float32(block[d, other]) * values[other]
-                    total = term if total is None else total + term
-            if total is not None:
-                yield d, waves[d], values[d], total
+        used = [d for d in range(3) if np.any(block[d] != 0.0)]
+        for part in connected(block, used):
+            values = [modes[d][waves[d]] for d in part]
+            if len(part) == 1:
+                forces = [np.float32(block[part[0], part[0]]) * values[0]]
+            else:
+                common = block[part[0], part[1]]
+                total = values[0] + values[1]
+                for value in values[2:]:
+                    total = total + value
+                shared = np.float32(common) * total
+                forces = []
+                for d, value in zip(part, values):
+                    extra = block[d, d] - common
+                    if abs(extra) > 1e-9:
+                        forces.append(shared + np.float32(extra) * value)
+                    else:
+                        forces.append(shared)
+            for d, value, force in zip(part, values, forces):
+                yield d, waves[d], value, force
 
 
 def energy_of(modes):
@@ -459,8 +485,8 @@
 
 
 def gradient_kernel(
-    place, slope, x_cos, x_sin, z_cos, z_sin, hidden_in, slope_mid, back, hidden_mid,
-    mine, other, out_mine, mid, first, running,
+    place, slope, x_cos, x_sin, z_cos, z_sin, hidden_in, slope_mid, back,
+    mine, other, mid, first,
 ):
     tables = (x_cos, x_sin, z_cos, z_sin)
     cells, rows, size = slope.shape
@@ -475,16 +501,11 @@
         line = jnp.concatenate(lines, 1)
         span = slice(p * rows * size, (p + 1) * rows * size)
         hidden = (hidden_in[:, span].astype(F32) * line).astype(BF)
-        product = hidden_mid[:, span].astype(F32) * line
-        total = product[:, :128]
-        for k in range(1, rows * size // 128):
-            total = total + product[:, k * 128 : (k + 1) * 128]
         terms = (
             lax.dot_general(hidden, slope_mid[:, span], LAST, preferred_element_type=F32),
             lax.dot_general(back[:, span], features, LAST, preferred_element_type=F32),
-            total,
         )
-        for held, term in zip((mid, first, running), terms):
+        for held, term in zip((mid, first), terms):
             if p == 0:
                 held[...] = term
             else:
@@ -503,35 +524,45 @@
 
             @pl.when(core != owner)
             def _():
-                start = k * mine.shape[1]
-                other[start : start + height, :] = mid[:, lanes]
-                other[start + height : start + mine.shape[1], :] = first_t[:, lanes]
+                other[k, :height, :] = mid[:, lanes]
+                other[k, height:, :] = first_t[:, lanes]
+
+
+def out_kernel(slope, hidden_mid, grad_out, running):
+    cells, rows, size = slope.shape
+    running[...] = jnp.zeros_like(running)
+
+    @pl.loop(0, cells)
+    def _(p):
+        total = None
+        for r in range(rows):
+            line = slope[p, r : r + 1, :]
+            for k in range(size // 128):
+                start = pl.multiple_of(p * (rows * size) + r * size + k * 128, 128)
+                term = hidden_mid[:, pl.ds(start, 128)].astype(F32)
+                term = term * line[:, k * 128 : (k + 1) * 128]
+                total = term if total is None else total + term
+        running[...] += total
 
     line = jnp.sum(running[...].T, axis=0, keepdims=True)
-    for k in range(2):
-        low = line[:, k * 128 : (k + 1) * 128]
-        high = line[:, (2 + k) * 128 : (3 + k) * 128]
-        out_mine[k : k + 1, :] = jnp.where(core == 0, low, high)
-        at = 2 * mine.shape[1] + k
-        other[at : at + 1, :] = jnp.where(core == 0, high, low)
-    other[2 * mine.shape[1] + 2 :, :] = jnp.zeros((6, 128), F32)
-
-
-def share_kernel(place, parts, out_mine, swapped, shares):
+    for k in range(grad_out.shape[0]):
+        grad_out[k : k + 1, :] = line[:, k * 128 : (k + 1) * 128]
+
+
+def share_kernel(place, parts, grad_out, shares):
     chips = parts.shape[0]
     total = parts[0]
     for chip in range(1, chips):
         total = total + parts[chip]
-    last = swapped.shape[0] - 8
-    out = out_mine[...] + swapped[last : last + 2, :]
-    block = jnp.concatenate([total, out], axis=0)
+    block = jnp.concatenate([total, grad_out[...]], axis=0)
     height = block.shape[0]
     for chip in range(chips):
         shares[chip * height : (chip + 1) * height, :] = block
 
 
 def finish_kernel(place, half, away, grad_in, grad_mid, grad_out):
-    height = 26
+    extra = grad_out.shape[0]
+    height = 24 + extra
     chips = half.shape[0] // height
     middle = grad_mid.shape[0]
 
@@ -541,26 +572,26 @@
             lanes = slice((2 * owner + group) * 128, (2 * owner + group + 1) * 128)
             for chip in range(chips // 2):
                 start = (first + chip) * height
-                block = source[start : start + height - 2, :]
-                row = chip * (height - 2)
-                if row + height - 2 <= middle:
-                    grad_mid[row : row + height - 2, lanes] = block
+                block = source[start : start + height - extra, :]
+                row = chip * (height - extra)
+                if row + height - extra <= middle:
+                    grad_mid[row : row + height - extra, lanes] = block
                 elif row >= middle:
-                    grad_in[row - middle : row - middle + height - 2, lanes] = block
+                    grad_in[row - middle : row - middle + height - extra, lanes] = block
                 else:
                     grad_mid[row:, lanes] = block[: middle - row]
-                    grad_in[: row + height - 2 - middle, lanes] = block[middle - row :]
-        total = source[height - 2 : height, :]
+                    grad_in[: row + height - extra - middle, lanes] = block[middle - row :]
+        total = source[height - extra : height, :]
         for chip in range(1, chips):
-            total = total + source[(chip + 1) * height - 2 : (chip + 1) * height, :]
-        grad_out[2 * owner : 2 * owner + 2, :] = total
+            total = total + source[(chip + 1) * height - extra : (chip + 1) * height, :]
+        return total
 
     for owner in range(2):
 
         @pl.when(place[CORE] == owner)
         def _():
-            put(half, owner)
-            put(away, 1 - owner)
+            own, far = put(half, owner), put(away, 1 - owner)
+            grad_out[...] = own + far
 
 
 VM = pltpu.VMEM
@@ -581,7 +612,7 @@
     return VM(shape, dtype)
 
 
-def run(kernel, name, out_shape, *operands, scalars=1, space=pltpu.VMEM, scratch=(), limit=16, **more):
+def run(kernel, name, out_shape, *operands, scalars=1, space=pltpu.VMEM, scratch=(), limit=12, **more):
     arrays = [pltpu.with_memory_space_constraint(array, space) for array in operands[scalars:]]
     return pl.pallas_call(
         kernel,
@@ -659,7 +690,7 @@
         *network,
         loads,
         scalars=0,
-        limit=16,
+        limit=12,
         cost_estimate=cost,
     )
     rows_ahead = shifted(rows_first, "z", -1)
@@ -672,7 +703,7 @@
         outer,
         *stored,
         scalars=0,
-        limit=16,
+        limit=12,
         input_output_aliases={9 + k: 2 + k for k in range(4)},
         cost_estimate=cost,
     )
@@ -695,7 +726,7 @@
         slope_mid,
         slope_in,
         scalars=0,
-        limit=16,
+        limit=12,
         input_output_aliases={2: 0},
         cost_estimate=pl.CostEstimate(
             flops=2 * hidden * hidden * rows,
@@ -720,25 +751,35 @@
 
     height = hidden + inputs
     groups = hidden // 128
-    mine, other, out_mine = run(
+    mine, other = run(
         gradient_kernel,
         "gradients",
-        [held(groups // 2, height, 128), held(groups // 2 * height + 8, 128)]
-        + [held(groups // 2, 128)],
-        place, slope, x_cos, x_sin, z_cos, z_sin, hidden_in, slope_mid, back, hidden_mid,
-        limit=16,
-        scratch=[VM((hidden, hidden), F32), VM((hidden, inputs), F32), VM((hidden, 128), F32)],
+        [held(groups // 2, height, 128)] * 2,
+        place, slope, x_cos, x_sin, z_cos, z_sin, hidden_in, slope_mid, back,
+        limit=12,
+        scratch=[VM((hidden, hidden), F32), VM((hidden, inputs), F32)],
     )
 
     chips = lax.axis_size(CHIPS)
     swap = [(0, 1), (1, 0)]
     swapped = lax.ppermute(other, "c", swap)
-    half = (mine.reshape(-1, 128) + swapped[:-8]).reshape(chips, -1, 128)
+    (grad_out,) = run(
+        out_kernel,
+        "grad_out",
+        [held(groups, 128)],
+        lax.optimization_barrier((slope, other))[0],
+        hidden_mid,
+        scalars=0,
+        scratch=[VM((hidden, 128), F32)],
+        cost_estimate=pl.CostEstimate(
+            flops=2 * hidden * rows, bytes_accessed=2 * hidden * rows, transcendentals=0
+        ),
+    )
+    half = (mine + swapped).reshape(chips, -1, 128)
+    half, grad_out = lax.optimization_barrier((half, grad_out))
     parts = lax.all_to_all(half, CHIPS, 0, 0)
-    tall = half.shape[1] + groups // 2
-    (shares,) = run(
-        share_kernel, "share", [held(chips * tall, 128)], place, parts, out_mine, swapped
-    )
+    tall = half.shape[1] + groups
+    (shares,) = run(share_kernel, "share", [held(chips * tall, 128)], place, parts, grad_out)
     half = lax.all_to_all(shares.reshape(chips, tall, 1, 128), CHIPS, 0, 0)
     half = half.reshape(chips * tall, 128)
     away = lax.ppermute(half, "c", swap)

time: 115 us -> 114 us (level)
  waiting for transfers between devices: 5.53 us -> 3.65 us
    ppermute x1, waiting for transfers between devices: 1.92 us -> 0.01 us  [on_device(): swapped = lax.ppermute(other, 'c', swap)]
    pallas_call x10 -> x11, Pallas kernels: 40.1 us -> 40 us  [run(): pl.pallas_call(kernel, name=name, in_specs=[SCALARS] * scalars + [WHOLE]...]
  transfers between devices with their start and end apart: 7 -> 7, of which waited for: 4 -> 3; matrix products, arithmetic and copies ran while one was open for 0% -> 0% of each run, Pallas kernels for 11% -> 13%
where the time goes in v7:
time: 114 us
  blocking collectives  54.4 us (48%)
  Pallas kernels  40 us (35%)
  starting transfers between devices  15.2 us (13%)
  waiting for transfers between devices  3.65 us (3%)
    pallas_call x11, Pallas kernels, run(): pl.pallas_call(kernel, name=name, in_specs=[SCALARS] * scalars + [WHOLE]...  40 us
    all_to_all x1, blocking collectives, on_device(): half = lax.all_to_all(shares.reshape(chips, tall, 1, 128), CHIPS, 0, 0)  19.6 us
    all_to_all x1, blocking collectives, on_device(): parts = lax.all_to_all(half, CHIPS, 0, 0)  19.2 us
    all_to_all x1, blocking collectives, gathered(): return lax.all_to_all(sent, CHIPS, 0, 0)  15.5 us
    ppermute x4, starting transfers between devices, shifted(): lax.ppermute(block, axis, [(i, (i + distance) % size) for i in range(size)])  6.94 us
    ppermute x1, starting transfers between devices, on_device(): away = lax.ppermute(half, 'c', swap)  3.34 us
    ppermute x1, starting transfers between devices, gathered(): chip = values + lax.ppermute(values, 'c', [(0, 1), (1, 0)])  3.2 us
  transfers between devices with their start and end apart: 7, of which 3 were waited for; matrix products, arithmetic and copies ran while one was open for 0% of the time, Pallas kernels for 13%

profile of v7, /device:TPU:1, one launch (start us, length us, event | category | flops | bytes accessed | tf_op | source)
XLA Modules:
  0.0 114.2 jit_solution(893221973435666143)
XLA Ops:
  0.7 2.6 %prepare.1 = (f32[4,4,8,256]{3,2,1,0:T(8,128)S(1)}, f32[8,128,4]{2,1,0:T(8,128)S(1)}, f32[8,128,4]{2,1,0:T(8,128)S(1)}, f32[128,256]{1,0:T(8,128)S(1)}, f32[128,...) custom-call(s32[8]{0:T(128)S(1)} %stack.47.place, ...), custom_call_target="tpu_custom_call" | custom-call | tf_op jit(solution)/shard_map/prepare/pallas_call | solution.py:617
  3.3 7.4 %outer.1 = (f32[4,4,256]{2,1,0:T(4,128)S(1)}, f32[20,3,256]{2,1,0:T(4,128)S(1)}, f32[20,2,256]{2,1,0:T(2,128)S(1)}, bf16[512,8192]{1,0:T(8,128)(2,1)S(1)}, bf16[...) custom-call(f32[8,128,4]{2,1,0:T(8,128)S(1)} %get-tuple-element.49.x_cos, ...), custom_call_target="tpu_custom_call" | custom-call | flops 3221225472 | bytes 16777216 | tf_op jit(solution)/shard_map/outer/pallas_call | solution.py:617
  10.7 2.5 %collective-permute-start.1 = (f32[20,2,256]{2,1,0:T(2,128)S(1)}, f32[20,2,256]{2,1,0:T(2,128)S(1)}, u32[]{:S(2)}, u32[]{:S(2)}) collective-permute-start(f32[20,2,256]{2,1,0:T(2,128)S(1)} %get-tuple-element.64), channel_id=1, source_target_pairs={{0,1},{1,2},{2,3},{3,0},{4,5},{5,6},{6,7},{7,4},{8,9},{9,10},{10,1... | collective-permute-start | bytes 122888 | tf_op jit(solution)/shard_map/ppermute | solution.py:631
  13.2 2.2 %collective-permute-start = (f32[20,3,256]{2,1,0:T(4,128)S(1)}, f32[20,3,256]{2,1,0:T(4,128)S(1)}, u32[]{:S(2)}, u32[]{:S(2)}) collective-permute-start(f32[20,3,256]{2,1,0:T(4,128)S(1)} %get-tuple-element.63), channel_id=1, source_target_pairs={{0,3},{1,0},{2,1},{3,2},{4,7},{5,4},{6,5},{7,6},{8,11},{9,8},{10,9... | collective-permute-start | bytes 184328 | tf_op jit(solution)/shard_map/ppermute | solution.py:631
  15.4 7.3 %inner.1 = (f32[4,8,256]{2,1,0:T(8,128)S(1)}, f32[4,8,256]{2,1,0:T(8,128)S(1)}, bf16[512,8192]{1,0:T(8,128)(2,1)S(1)}, bf16[512,8192]{1,0:T(8,128)(2,1)S(1)}, bf...) custom-call(f32[8,128,4]{2,1,0:T(8,128)S(1)} %get-tuple-element.49.x, ...), custom_call_target="tpu_custom_call", output_to_operand_aliasing={{2}: (9, {}), {3}: (10, {}), {4}: (11, {}), {5}: (12, {})} | custom-call | flops 3221225472 | bytes 16777216 | tf_op jit(solution)/shard_map/inner/pallas_call | solution.py:617
  22.8 0.6 join.1
  23.4 2.2 %collective-permute-start.3 = (f32[10,16,256]{2,1,0:T(8,128)S(1)}, f32[10,16,256]{2,1,0:T(8,128)S(1)}, u32[]{:S(2)}, u32[]{:S(2)}) collective-permute-start(f32[10,16,256]{2,1,0:T(8,128)S(1)} %get-tuple-element.68), channel_id=1, source_target_pairs={{0,4},{4,8},{8,12},{12,16},{16,20},{20,24},{24,28},{28,32},{32,36}... | collective-permute-start | bytes 491528 | tf_op jit(solution)/shard_map/ppermute | solution.py:631
  25.6 5.0 %back.1 = (bf16[512,8192]{1,0:T(8,128)(2,1)S(1)}, f32[8,128]{1,0:T(8,128)S(1)}) custom-call(bf16[512,512]{1,0:T(8,128)(2,1)S(1)} %get-tuple-element.70.w_mid, bf16[512,8192]{1,0:T(8,128)(2,1)S(1)} %get-tuple-element.71.slope_mid, bf16[512,8192]{1,0:T(8,128)(2,1)S(1)} %get-tuple-element.72.slope_in), custom_call_target="tpu_custom_call", output_to_operand_aliasing={{0}: (2, {})} | custom-call | flops 4294967296 | bytes 25165824 | tf_op jit(solution)/shard_map/back/pallas_call | solution.py:617
  30.6 0.7 collective-permute-done.2.ahead
  31.4 2.6 %krylov.1 = (f32[3,5,16,256]{3,2,1,0:T(8,128)S(1)}, f32[3,5,16,256]{3,2,1,0:T(8,128)S(1)}, f32[1,128]{1,0:T(1,128)S(1)}) custom-call(s32[8]{0:T(128)S(1)} %stack.47.place, f32[4,4,16,256]{3,2,1,0:T(8,128)S(1)} %get-tuple-element.65.loads, f32[4,16,256]{2,1,0:T(8,128)S(1)} %get-tuple-element.66.stiff, f32[14,16,256]{2,1,0:T(8,128)S(1)} %collective-permute-done.2.ahead, ...), custom_call_target="tpu_custom_call" | custom-call | tf_op jit(solution)/shard_map/krylov/pallas_call | solution.py:617
  33.9 3.2 %collective-permute-start.4 = (f32[1,128]{1,0:T(1,128)S(1)}, f32[1,128]{1,0:T(1,128)S(1)}, u32[]{:S(2)}, u32[]{:S(2)}) collective-permute-start(f32[1,128]{1,0:T(1,128)S(1)} %get-tuple-element.74), channel_id=1, source_target_pairs={{0,4},{4,0},{1,5},{5,1},{2,6},{6,2},{3,7},{7,3},{8,12},{12,8},{9,1... | collective-permute-start | bytes 1544 | tf_op jit(solution)/shard_map/ppermute | solution.py:635
  37.1 0.8 collective-permute-done.4
  38.0 15.5 %all_to_all.15.sums = f32[64,1,128]{2,1,0:T(1,128)S(1)} all-to-all(f32[64,1,128]{2,1,0:T(1,128)S(1)} %broadcast_in_dim.9), channel_id=1, replica_groups=mesh['x'=4,'y'=4,'c'=2,'z'=4] {'x','y','z'}, dimensions={0} | all-to-all | bytes 65536 | tf_op jit(solution)/shard_map/all_to_all | solution.py:637
  53.5 1.5 %energy.1 = (f32[3,4,8,256]{3,2,1,0:T(8,128)}, f32[4,8,256]{2,1,0:T(8,128)S(1)}, f32[4,8,256]{2,1,0:T(8,128)}) custom-call(s32[8]{0:T(128)S(1)} %stack.47.place, f32[64,1,128]{2,1,0:T(1,128)S(1)} %all_to_all.15.sums, f32[4,4,16,256]{3,2,1,0:T(8,128)S(1)} %get-tuple-element.65.loads, f32[14,16,256]{2,1,0:T(8,128)S(1)} %collective-permute-done.2.ahead, ...), custom_call_target="tpu_custom_call" | custom-call | tf_op jit(solution)/shard_map/energy/pallas_call | solution.py:617
  55.0 8.0 %gradients.1 = (f32[2,768,128]{2,1,0:T(8,128)S(1)}, f32[2,768,128]{2,1,0:T(8,128)S(1)}) custom-call(s32[8]{0:T(128)S(1)} %stack.47.place, f32[4,8,256]{2,1,0:T(8,128)S(1)} %get-tuple-element.84.slope, f32[8,128,4]{2,1,0:T(8,128)S(1)} %get-tuple-element.49.x_cos, f32[8,128,4]{2,1,0:T(8,128)S(1)} %get-tuple-element.50.x_sin, ...), custom_call_target="tpu_custom_call" | custom-call | tf_op jit(solution)/shard_map/gradients/pallas_call | solution.py:617
  62.9 1.7 %collective-permute-start.5 = (f32[2,768,128]{2,1,0:T(8,128)S(1)}, f32[2,768,128]{2,1,0:T(8,128)S(1)}, u32[]{:S(2)}, u32[]{:S(2)}) collective-permute-start(f32[2,768,128]{2,1,0:T(8,128)S(1)} %get-tuple-element.83), channel_id=1, source_target_pairs={{0,4},{4,0},{1,5},{5,1},{2,6},{6,2},{3,7},{7,3},{8,12},{12,8},{9,1... | collective-permute-start | bytes 2359304 | tf_op jit(solution)/shard_map/ppermute | solution.py:765
  64.7 2.5 %grad_out.1 = f32[4,128]{1,0:T(4,128)S(1)} custom-call(f32[4,8,256]{2,1,0:T(8,128)S(1)} %get-tuple-element.84.slope, bf16[512,8192]{1,0:T(8,128)(2,1)S(1)} %get-tuple-element.85.hidden_mid), custom_call_target="tpu_custom_call" | custom-call | flops 8388608 | bytes 8388608 | tf_op jit(solution)/shard_map/grad_out/pallas_call | solution.py:617
  67.1 0.1 add.15
  67.2 19.2 %all_to_all.16.parts = f32[64,24,128]{2,1,0:T(8,128)S(1)} all-to-all(f32[64,24,128]{2,1,0:T(8,128)S(1)} %bitcast.16), channel_id=1, replica_groups=mesh['x'=4,'y'=4,'c'=2,'z'=4] {'x','y','z'}, dimensions={0} | all-to-all | bytes 1572864 | tf_op jit(solution)/shard_map/all_to_all | solution.py:780
  86.5 0.7 share.1
  87.1 19.6 %all_to_all.17 = f32[64,28,1,128]{3,2,1,0:T(1,128)S(1)} all-to-all(f32[64,28,1,128]{3,2,1,0:T(1,128)S(1)} %bitcast.13), channel_id=1, replica_groups=mesh['x'=4,'y'=4,'c'=2,'z'=4] {'x','y','z'}, dimensions={0} | all-to-all | bytes 1835008 | tf_op jit(solution)/shard_map/all_to_all | solution.py:783
  106.7 3.3 %collective-permute-start.6 = (f32[1792,128]{1,0:T(8,128)S(1)}, f32[1792,128]{1,0:T(8,128)S(1)}, u32[]{:S(2)}, u32[]{:S(2)}) collective-permute-start(f32[1792,128]{1,0:T(8,128)S(1)} %bitcast.14), channel_id=1, source_target_pairs={{0,4},{4,0},{1,5},{5,1},{2,6},{6,2},{3,7},{7,3},{8,12},{12,8},{9,1... | collective-permute-start | bytes 2752520 | tf_op jit(solution)/shard_map/ppermute | solution.py:785
  110.1 2.1 %collective-permute-done.6.away = f32[1792,128]{1,0:T(8,128)S(1)} collective-permute-done((f32[1792,128]{1,0:T(8,128)S(1)}, f32[1792,128]{1,0:T(8,128)S(1)}, u32[]{:S(2)}, u32[]{:S(2)}) %collective-permute-start.6) | collective-permute-done | bytes 917536 | tf_op jit(solution)/shard_map/ppermute | solution.py:785
  112.2 2.0 %finish.1 = (f32[256,512]{1,0:T(8,128)}, f32[512,512]{1,0:T(8,128)}, f32[4,128]{1,0:T(4,128)}) custom-call(s32[8]{0:T(128)S(1)} %stack.47.place, f32[1792,128]{1,0:T(8,128)S(1)} %bitcast.15, f32[1792,128]{1,0:T(8,128)S(1)} %collective-permute-done.6.away), custom_call_target="tpu_custom_call" | custom-call | tf_op jit(solution)/shard_map/finish/pallas_call | solution.py:617
  (8 shorter events, 0.1 us)
Async XLA Ops:
  10.7 12.1 %collective-permute-start.1 = (f32[20,2,256]{2,1,0:T(2,128)S(1)}, f32[20,2,256]{2,1,0:T(2,128)S(1)}, u32[]{:S(2)}, u32[]{:S(2)}) collective-permute-start(f32[20,2,256]{2,1,0:T(2,128)S(1)} %get-tuple-element.64), channel_id=1, source_target_pairs={{0,1},{1,2},{2,3},{3,0},{4,5},{5,6},{6,7},{7,4},{8,9},{9,10},{10,1... | collective-permute-start | bytes 122888 | tf_op jit(solution)/shard_map/ppermute | solution.py:631
  13.2 9.6 %collective-permute-start = (f32[20,3,256]{2,1,0:T(4,128)S(1)}, f32[20,3,256]{2,1,0:T(4,128)S(1)}, u32[]{:S(2)}, u32[]{:S(2)}) collective-permute-start(f32[20,3,256]{2,1,0:T(4,128)S(1)} %get-tuple-element.63), channel_id=1, source_target_pairs={{0,3},{1,0},{2,1},{3,2},{4,7},{5,4},{6,5},{7,6},{8,11},{9,8},{10,9... | collective-permute-start | bytes 184328 | tf_op jit(solution)/shard_map/ppermute | solution.py:631
  23.4 7.2 %collective-permute-start.3 = (f32[10,16,256]{2,1,0:T(8,128)S(1)}, f32[10,16,256]{2,1,0:T(8,128)S(1)}, u32[]{:S(2)}, u32[]{:S(2)}) collective-permute-start(f32[10,16,256]{2,1,0:T(8,128)S(1)} %get-tuple-element.68), channel_id=1, source_target_pairs={{0,4},{4,8},{8,12},{12,16},{16,20},{20,24},{24,28},{28,32},{32,36}... | collective-permute-start | bytes 491528 | tf_op jit(solution)/shard_map/ppermute | solution.py:631
  25.6 5.7 %collective-permute-start.2 = (f32[14,16,256]{2,1,0:T(8,128)S(1)}, f32[14,16,256]{2,1,0:T(8,128)S(1)}, u32[]{:S(2)}, u32[]{:S(2)}) collective-permute-start(f32[14,16,256]{2,1,0:T(8,128)S(1)} %get-tuple-element.67), channel_id=1, source_target_pairs={{0,124},{4,0},{8,4},{12,8},{16,12},{20,16},{24,20},{28,24},{32,28}... | collective-permute-start | bytes 688136 | tf_op jit(solution)/shard_map/ppermute | solution.py:631
  33.9 4.0 %collective-permute-start.4 = (f32[1,128]{1,0:T(1,128)S(1)}, f32[1,128]{1,0:T(1,128)S(1)}, u32[]{:S(2)}, u32[]{:S(2)}) collective-permute-start(f32[1,128]{1,0:T(1,128)S(1)} %get-tuple-element.74), channel_id=1, source_target_pairs={{0,4},{4,0},{1,5},{5,1},{2,6},{6,2},{3,7},{7,3},{8,12},{12,8},{9,1... | collective-permute-start | bytes 1544 | tf_op jit(solution)/shard_map/ppermute | solution.py:635
  62.9 4.2 %collective-permute-start.5 = (f32[2,768,128]{2,1,0:T(8,128)S(1)}, f32[2,768,128]{2,1,0:T(8,128)S(1)}, u32[]{:S(2)}, u32[]{:S(2)}) collective-permute-start(f32[2,768,128]{2,1,0:T(8,128)S(1)} %get-tuple-element.83), channel_id=1, source_target_pairs={{0,4},{4,0},{1,5},{5,1},{2,6},{6,2},{3,7},{7,3},{8,12},{12,8},{9,1... | collective-permute-start | bytes 2359304 | tf_op jit(solution)/shard_map/ppermute | solution.py:765
  106.7 5.4 %collective-permute-start.6 = (f32[1792,128]{1,0:T(8,128)S(1)}, f32[1792,128]{1,0:T(8,128)S(1)}, u32[]{:S(2)}, u32[]{:S(2)}) collective-permute-start(f32[1792,128]{1,0:T(8,128)S(1)} %bitcast.14), channel_id=1, source_target_pairs={{0,4},{4,0},{1,5},{5,1},{2,6},{6,2},{3,7},{7,3},{8,12},{12,8},{9,1... | collective-permute-start | bytes 2752520 | tf_op jit(solution)/shard_map/ppermute | solution.py:785

commit v8 on v7

--- a/solution.py
+++ b/solution.py
@@ -437,9 +437,8 @@
     tables, weights = (x_cos, x_sin, z_cos, z_sin), (w_in, w_mid, w_column, w_row)
     cells, _, size = density.shape
 
-    @pl.loop(0, cells)
-    def _(p):
-        start = pl.multiple_of(p * (8 * size), 8 * size)
+    for p in range(cells):
+        start = p * (8 * size)
         spans = [(start, 0, 2 * size), (start + 6 * size, 2 * size, 2 * size)]
         line = forward_columns(tables, p, weights, kept, spans)
         for q in range(4):

time: 114 us -> 114 us (level)
  no operation moved by 1% of the time
where the time goes in v8:
time: 114 us
  blocking collectives  54.4 us (48%)
  Pallas kernels  39.5 us (35%)
  starting transfers between devices  15.2 us (13%)
  waiting for transfers between devices  3.65 us (3%)
    pallas_call x11, Pallas kernels, run(): pl.pallas_call(kernel, name=name, in_specs=[SCALARS] * scalars + [WHOLE]...  39.5 us
    all_to_all x1, blocking collectives, on_device(): half = lax.all_to_all(shares.reshape(chips, tall, 1, 128), CHIPS, 0, 0)  19.6 us
    all_to_all x1, blocking collectives, on_device(): parts = lax.all_to_all(half, CHIPS, 0, 0)  19.2 us
    all_to_all x1, blocking collectives, gathered(): return lax.all_to_all(sent, CHIPS, 0, 0)  15.5 us
    ppermute x4, starting transfers between devices, shifted(): lax.ppermute(block, axis, [(i, (i + distance) % size) for i in range(size)])  6.95 us
    ppermute x1, starting transfers between devices, on_device(): away = lax.ppermute(half, 'c', swap)  3.34 us
    ppermute x1, starting transfers between devices, gathered(): chip = values + lax.ppermute(values, 'c', [(0, 1), (1, 0)])  3.2 us
  transfers between devices with their start and end apart: 7, of which 3 were waited for; matrix products, arithmetic and copies ran while one was open for 0% of the time, Pallas kernels for 13%

profile of v8, /device:TPU:1, one launch (start us, length us, event | category | flops | bytes accessed | tf_op | source)
XLA Modules:
  0.0 113.6 jit_solution(5491653804689146809)
XLA Ops:
  0.7 2.6 %prepare.1 = (f32[4,4,8,256]{3,2,1,0:T(8,128)S(1)}, f32[8,128,4]{2,1,0:T(8,128)S(1)}, f32[8,128,4]{2,1,0:T(8,128)S(1)}, f32[128,256]{1,0:T(8,128)S(1)}, f32[128,...) custom-call(s32[8]{0:T(128)S(1)} %stack.47.place, ...), custom_call_target="tpu_custom_call" | custom-call | tf_op jit(solution)/shard_map/prepare/pallas_call | solution.py:616
  3.3 6.8 %outer.1 = (f32[4,4,256]{2,1,0:T(4,128)S(1)}, f32[20,3,256]{2,1,0:T(4,128)S(1)}, f32[20,2,256]{2,1,0:T(2,128)S(1)}, bf16[512,8192]{1,0:T(8,128)(2,1)S(1)}, bf16[...) custom-call(f32[8,128,4]{2,1,0:T(8,128)S(1)} %get-tuple-element.49.x_cos, ...), custom_call_target="tpu_custom_call" | custom-call | flops 3221225472 | bytes 16777216 | tf_op jit(solution)/shard_map/outer/pallas_call | solution.py:616
  10.2 2.5 %collective-permute-start.1 = (f32[20,2,256]{2,1,0:T(2,128)S(1)}, f32[20,2,256]{2,1,0:T(2,128)S(1)}, u32[]{:S(2)}, u32[]{:S(2)}) collective-permute-start(f32[20,2,256]{2,1,0:T(2,128)S(1)} %get-tuple-element.64), channel_id=1, source_target_pairs={{0,1},{1,2},{2,3},{3,0},{4,5},{5,6},{6,7},{7,4},{8,9},{9,10},{10,1... | collective-permute-start | bytes 122888 | tf_op jit(solution)/shard_map/ppermute | solution.py:630
  12.7 2.2 %collective-permute-start = (f32[20,3,256]{2,1,0:T(4,128)S(1)}, f32[20,3,256]{2,1,0:T(4,128)S(1)}, u32[]{:S(2)}, u32[]{:S(2)}) collective-permute-start(f32[20,3,256]{2,1,0:T(4,128)S(1)} %get-tuple-element.63), channel_id=1, source_target_pairs={{0,3},{1,0},{2,1},{3,2},{4,7},{5,4},{6,5},{7,6},{8,11},{9,8},{10,9... | collective-permute-start | bytes 184328 | tf_op jit(solution)/shard_map/ppermute | solution.py:630
  14.9 7.3 %inner.1 = (f32[4,8,256]{2,1,0:T(8,128)S(1)}, f32[4,8,256]{2,1,0:T(8,128)S(1)}, bf16[512,8192]{1,0:T(8,128)(2,1)S(1)}, bf16[512,8192]{1,0:T(8,128)(2,1)S(1)}, bf...) custom-call(f32[8,128,4]{2,1,0:T(8,128)S(1)} %get-tuple-element.49.x, ...), custom_call_target="tpu_custom_call", output_to_operand_aliasing={{2}: (9, {}), {3}: (10, {}), {4}: (11, {}), {5}: (12, {})} | custom-call | flops 3221225472 | bytes 16777216 | tf_op jit(solution)/shard_map/inner/pallas_call | solution.py:616
  22.3 0.6 join.1
  22.9 2.2 %collective-permute-start.3 = (f32[10,16,256]{2,1,0:T(8,128)S(1)}, f32[10,16,256]{2,1,0:T(8,128)S(1)}, u32[]{:S(2)}, u32[]{:S(2)}) collective-permute-start(f32[10,16,256]{2,1,0:T(8,128)S(1)} %get-tuple-element.68), channel_id=1, source_target_pairs={{0,4},{4,8},{8,12},{12,16},{16,20},{20,24},{24,28},{28,32},{32,36}... | collective-permute-start | bytes 491528 | tf_op jit(solution)/shard_map/ppermute | solution.py:630
  25.1 5.0 %back.1 = (bf16[512,8192]{1,0:T(8,128)(2,1)S(1)}, f32[8,128]{1,0:T(8,128)S(1)}) custom-call(bf16[512,512]{1,0:T(8,128)(2,1)S(1)} %get-tuple-element.70.w_mid, bf16[512,8192]{1,0:T(8,128)(2,1)S(1)} %get-tuple-element.71.slope_mid, bf16[512,8192]{1,0:T(8,128)(2,1)S(1)} %get-tuple-element.72.slope_in), custom_call_target="tpu_custom_call", output_to_operand_aliasing={{0}: (2, {})} | custom-call | flops 4294967296 | bytes 25165824 | tf_op jit(solution)/shard_map/back/pallas_call | solution.py:616
  30.1 0.7 collective-permute-done.2.ahead
  30.8 2.6 %krylov.1 = (f32[3,5,16,256]{3,2,1,0:T(8,128)S(1)}, f32[3,5,16,256]{3,2,1,0:T(8,128)S(1)}, f32[1,128]{1,0:T(1,128)S(1)}) custom-call(s32[8]{0:T(128)S(1)} %stack.47.place, f32[4,4,16,256]{3,2,1,0:T(8,128)S(1)} %get-tuple-element.65.loads, f32[4,16,256]{2,1,0:T(8,128)S(1)} %get-tuple-element.66.stiff, f32[14,16,256]{2,1,0:T(8,128)S(1)} %collective-permute-done.2.ahead, ...), custom_call_target="tpu_custom_call" | custom-call | tf_op jit(solution)/shard_map/krylov/pallas_call | solution.py:616
  33.4 3.2 %collective-permute-start.4 = (f32[1,128]{1,0:T(1,128)S(1)}, f32[1,128]{1,0:T(1,128)S(1)}, u32[]{:S(2)}, u32[]{:S(2)}) collective-permute-start(f32[1,128]{1,0:T(1,128)S(1)} %get-tuple-element.74), channel_id=1, source_target_pairs={{0,4},{4,0},{1,5},{5,1},{2,6},{6,2},{3,7},{7,3},{8,12},{12,8},{9,1... | collective-permute-start | bytes 1544 | tf_op jit(solution)/shard_map/ppermute | solution.py:634
  36.6 0.8 collective-permute-done.4
  37.4 15.5 %all_to_all.15.sums = f32[64,1,128]{2,1,0:T(1,128)S(1)} all-to-all(f32[64,1,128]{2,1,0:T(1,128)S(1)} %broadcast_in_dim.9), channel_id=1, replica_groups=mesh['x'=4,'y'=4,'c'=2,'z'=4] {'x','y','z'}, dimensions={0} | all-to-all | bytes 65536 | tf_op jit(solution)/shard_map/all_to_all | solution.py:636
  53.0 1.5 %energy.1 = (f32[3,4,8,256]{3,2,1,0:T(8,128)}, f32[4,8,256]{2,1,0:T(8,128)S(1)}, f32[4,8,256]{2,1,0:T(8,128)}) custom-call(s32[8]{0:T(128)S(1)} %stack.47.place, f32[64,1,128]{2,1,0:T(1,128)S(1)} %all_to_all.15.sums, f32[4,4,16,256]{3,2,1,0:T(8,128)S(1)} %get-tuple-element.65.loads, f32[14,16,256]{2,1,0:T(8,128)S(1)} %collective-permute-done.2.ahead, ...), custom_call_target="tpu_custom_call" | custom-call | tf_op jit(solution)/shard_map/energy/pallas_call | solution.py:616
  54.5 8.0 %gradients.1 = (f32[2,768,128]{2,1,0:T(8,128)S(1)}, f32[2,768,128]{2,1,0:T(8,128)S(1)}) custom-call(s32[8]{0:T(128)S(1)} %stack.47.place, f32[4,8,256]{2,1,0:T(8,128)S(1)} %get-tuple-element.84.slope, f32[8,128,4]{2,1,0:T(8,128)S(1)} %get-tuple-element.49.x_cos, f32[8,128,4]{2,1,0:T(8,128)S(1)} %get-tuple-element.50.x_sin, ...), custom_call_target="tpu_custom_call" | custom-call | tf_op jit(solution)/shard_map/gradients/pallas_call | solution.py:616
  62.4 1.7 %collective-permute-start.5 = (f32[2,768,128]{2,1,0:T(8,128)S(1)}, f32[2,768,128]{2,1,0:T(8,128)S(1)}, u32[]{:S(2)}, u32[]{:S(2)}) collective-permute-start(f32[2,768,128]{2,1,0:T(8,128)S(1)} %get-tuple-element.83), channel_id=1, source_target_pairs={{0,4},{4,0},{1,5},{5,1},{2,6},{6,2},{3,7},{7,3},{8,12},{12,8},{9,1... | collective-permute-start | bytes 2359304 | tf_op jit(solution)/shard_map/ppermute | solution.py:764
  64.1 2.5 %grad_out.1 = f32[4,128]{1,0:T(4,128)S(1)} custom-call(f32[4,8,256]{2,1,0:T(8,128)S(1)} %get-tuple-element.84.slope, bf16[512,8192]{1,0:T(8,128)(2,1)S(1)} %get-tuple-element.85.hidden_mid), custom_call_target="tpu_custom_call" | custom-call | flops 8388608 | bytes 8388608 | tf_op jit(solution)/shard_map/grad_out/pallas_call | solution.py:616
  66.6 0.1 add.15
  66.7 19.2 %all_to_all.16.parts = f32[64,24,128]{2,1,0:T(8,128)S(1)} all-to-all(f32[64,24,128]{2,1,0:T(8,128)S(1)} %bitcast.16), channel_id=1, replica_groups=mesh['x'=4,'y'=4,'c'=2,'z'=4] {'x','y','z'}, dimensions={0} | all-to-all | bytes 1572864 | tf_op jit(solution)/shard_map/all_to_all | solution.py:779
  85.9 0.7 share.1
  86.6 19.6 %all_to_all.17 = f32[64,28,1,128]{3,2,1,0:T(1,128)S(1)} all-to-all(f32[64,28,1,128]{3,2,1,0:T(1,128)S(1)} %bitcast.13), channel_id=1, replica_groups=mesh['x'=4,'y'=4,'c'=2,'z'=4] {'x','y','z'}, dimensions={0} | all-to-all | bytes 1835008 | tf_op jit(solution)/shard_map/all_to_all | solution.py:782
  106.2 3.3 %collective-permute-start.6 = (f32[1792,128]{1,0:T(8,128)S(1)}, f32[1792,128]{1,0:T(8,128)S(1)}, u32[]{:S(2)}, u32[]{:S(2)}) collective-permute-start(f32[1792,128]{1,0:T(8,128)S(1)} %bitcast.14), channel_id=1, source_target_pairs={{0,4},{4,0},{1,5},{5,1},{2,6},{6,2},{3,7},{7,3},{8,12},{12,8},{9,1... | collective-permute-start | bytes 2752520 | tf_op jit(solution)/shard_map/ppermute | solution.py:784
  109.6 2.1 %collective-permute-done.6.away = f32[1792,128]{1,0:T(8,128)S(1)} collective-permute-done((f32[1792,128]{1,0:T(8,128)S(1)}, f32[1792,128]{1,0:T(8,128)S(1)}, u32[]{:S(2)}, u32[]{:S(2)}) %collective-permute-start.6) | collective-permute-done | bytes 917536 | tf_op jit(solution)/shard_map/ppermute | solution.py:784
  111.7 2.0 %finish.1 = (f32[256,512]{1,0:T(8,128)}, f32[512,512]{1,0:T(8,128)}, f32[4,128]{1,0:T(4,128)}) custom-call(s32[8]{0:T(128)S(1)} %stack.47.place, f32[1792,128]{1,0:T(8,128)S(1)} %bitcast.15, f32[1792,128]{1,0:T(8,128)S(1)} %collective-permute-done.6.away), custom_call_target="tpu_custom_call" | custom-call | tf_op jit(solution)/shard_map/finish/pallas_call | solution.py:616
  (8 shorter events, 0.1 us)
Async XLA Ops:
  10.2 12.1 %collective-permute-start.1 = (f32[20,2,256]{2,1,0:T(2,128)S(1)}, f32[20,2,256]{2,1,0:T(2,128)S(1)}, u32[]{:S(2)}, u32[]{:S(2)}) collective-permute-start(f32[20,2,256]{2,1,0:T(2,128)S(1)} %get-tuple-element.64), channel_id=1, source_target_pairs={{0,1},{1,2},{2,3},{3,0},{4,5},{5,6},{6,7},{7,4},{8,9},{9,10},{10,1... | collective-permute-start | bytes 122888 | tf_op jit(solution)/shard_map/ppermute | solution.py:630
  12.7 9.6 %collective-permute-start = (f32[20,3,256]{2,1,0:T(4,128)S(1)}, f32[20,3,256]{2,1,0:T(4,128)S(1)}, u32[]{:S(2)}, u32[]{:S(2)}) collective-permute-start(f32[20,3,256]{2,1,0:T(4,128)S(1)} %get-tuple-element.63), channel_id=1, source_target_pairs={{0,3},{1,0},{2,1},{3,2},{4,7},{5,4},{6,5},{7,6},{8,11},{9,8},{10,9... | collective-permute-start | bytes 184328 | tf_op jit(solution)/shard_map/ppermute | solution.py:630
  22.9 7.2 %collective-permute-start.3 = (f32[10,16,256]{2,1,0:T(8,128)S(1)}, f32[10,16,256]{2,1,0:T(8,128)S(1)}, u32[]{:S(2)}, u32[]{:S(2)}) collective-permute-start(f32[10,16,256]{2,1,0:T(8,128)S(1)} %get-tuple-element.68), channel_id=1, source_target_pairs={{0,4},{4,8},{8,12},{12,16},{16,20},{20,24},{24,28},{28,32},{32,36}... | collective-permute-start | bytes 491528 | tf_op jit(solution)/shard_map/ppermute | solution.py:630
  25.1 5.7 %collective-permute-start.2 = (f32[14,16,256]{2,1,0:T(8,128)S(1)}, f32[14,16,256]{2,1,0:T(8,128)S(1)}, u32[]{:S(2)}, u32[]{:S(2)}) collective-permute-start(f32[14,16,256]{2,1,0:T(8,128)S(1)} %get-tuple-element.67), channel_id=1, source_target_pairs={{0,124},{4,0},{8,4},{12,8},{16,12},{20,16},{24,20},{28,24},{32,28}... | collective-permute-start | bytes 688136 | tf_op jit(solution)/shard_map/ppermute | solution.py:630
  33.4 4.0 %collective-permute-start.4 = (f32[1,128]{1,0:T(1,128)S(1)}, f32[1,128]{1,0:T(1,128)S(1)}, u32[]{:S(2)}, u32[]{:S(2)}) collective-permute-start(f32[1,128]{1,0:T(1,128)S(1)} %get-tuple-element.74), channel_id=1, source_target_pairs={{0,4},{4,0},{1,5},{5,1},{2,6},{6,2},{3,7},{7,3},{8,12},{12,8},{9,1... | collective-permute-start | bytes 1544 | tf_op jit(solution)/shard_map/ppermute | solution.py:634
  62.4 4.2 %collective-permute-start.5 = (f32[2,768,128]{2,1,0:T(8,128)S(1)}, f32[2,768,128]{2,1,0:T(8,128)S(1)}, u32[]{:S(2)}, u32[]{:S(2)}) collective-permute-start(f32[2,768,128]{2,1,0:T(8,128)S(1)} %get-tuple-element.83), channel_id=1, source_target_pairs={{0,4},{4,0},{1,5},{5,1},{2,6},{6,2},{3,7},{7,3},{8,12},{12,8},{9,1... | collective-permute-start | bytes 2359304 | tf_op jit(solution)/shard_map/ppermute | solution.py:764
  106.2 5.4 %collective-permute-start.6 = (f32[1792,128]{1,0:T(8,128)S(1)}, f32[1792,128]{1,0:T(8,128)S(1)}, u32[]{:S(2)}, u32[]{:S(2)}) collective-permute-start(f32[1792,128]{1,0:T(8,128)S(1)} %bitcast.14), channel_id=1, source_target_pairs={{0,4},{4,0},{1,5},{5,1},{2,6},{6,2},{3,7},{7,3},{8,12},{12,8},{9,1... | collective-permute-start | bytes 2752520 | tf_op jit(solution)/shard_map/ppermute | solution.py:784
